TPU v7x, 32 devices: a whole 2x2x4 slice. The times are simulated.
32 devices in a mesh: gx: 4 (over z), gy: 8 (over y, x, core).
Axes of the slice: x: 2, y: 2, z: 4, core: 2. Of those that a mesh axis runs over, the one named last changes fastest.
Arguments:
- connectivity: int32 [8, 32768], P(None, ('gx', 'gy')), may hold values from 0 to 1407, as said below
- face_nodes: int32 [4, 4896], P(None, ('gx', 'gy')), may hold values from 0 to 1407, as said below
- coords: float32 [3, 45056], P(None, ('gx', 'gy')), may hold values from -0.1 to 80.1, as said below
- displacement: float32 [3, 45056], P(None, ('gx', 'gy')), may hold values from -0.2 to 0.2, as said below
- velocity: float32 [3, 45056], P(None, ('gx', 'gy')), may hold values from -0.4 to 0.4, as said below
- node_mass: float32 [45056], P(('gx', 'gy')), may hold values from 0.5 to 2, as said below
- modulus: float32 [32768], P(('gx', 'gy')), may hold values from 1 to 10
- surf_nodes: int32 [8192, 128], P(('gx', 'gy')), may hold values from 0 to 1376
- surf_ref: float32 [8192, 3, 128], P(('gx', 'gy')), may hold values from -4 to 4
- surf_angles: float32 [8192, 2, 128], P(('gx', 'gy')), may hold values from -3.140625 to 3.140625
- owner_map: int32 [8192], replicated, may hold values from 0 to 31, as said below
- pair_blocks: int32 [2, 2048], P(None, ('gx', 'gy')), may hold values from 0 to 511, as said below
- pair_masks: int32 [2, 2048, 128], P(None, ('gx', 'gy')), may hold values 0 or 1
- pair_count: int32 [32], P(('gx', 'gy')), may hold values from 8 to 64, as said below
Outputs:
- velocity_next: float32 [3, 45056], P(None, ('gx', 'gy'))
Inputs may be any that keep to these rules, and one draw needn't show every extreme that they name: `connectivity`: each device's elements are hexahedra over that device's node numbers, corners in the order of the steps; elements of one device share nodes among themselves. `face_nodes`: rows 0 and 1 list a device's nodes on its faces toward ix - 1 and ix + 1, rows 2 and 3 toward iy - 1 and iy + 1. Entry e of row 1 of a device and entry e of row 0 of the next device along gx are copies of one mesh node, likewise rows 3 and 2 along gy. Nodes on edges stand in a gx row and a gy row. Within a row the numbers are distinct, and rows 0 and 1 (2 and 3) share none. `coords`: copies of one mesh node on different devices carry equal values. The corners of every element are near the corners of a unit cube. `displacement`: copies of one mesh node on different devices carry equal values. `velocity`: copies of one mesh node on different devices carry equal values. `node_mass`: copies of one mesh node on different devices carry equal values. `owner_map`: block k belongs to the mesh partition of device k // 256. No partition has more than 16 blocks with one owner, and every owner has two blocks or more. `pair_blocks`: the two ranks of a pair differ and are smaller than the number of blocks that owner_map gives to the device that holds the pair. Only the first pair_count pairs of an owner are live.
All inputs are finite; a program needn't handle non-finite values. No bound on the sum of `pair_masks` on one device may be relied on, other than what follows from the above.
Results may differ from a plain program's by a relative error of at most 0.0003.
Values sent between devices are 32-bit elements; how exact they have to be, the bound alone decides.
No kernel may reach another device: no remote copies, remote signals or barrier semaphores. Data moves between devices by JAX's collectives and lax.ppermute only.
A program may use at most 128 MiB of HBM per device.

v0:
```python
import functools

import jax
import jax.numpy as jnp
from jax import lax
from jax.experimental import pallas as pl
from jax.experimental.pallas import tpu as pltpu
from jax.sharding import PartitionSpec as P

XI_SIGNS = [
    [-1, -1, -1],
    [1, -1, -1],
    [1, 1, -1],
    [-1, 1, -1],
    [-1, -1, 1],
    [1, -1, 1],
    [1, 1, 1],
    [-1, 1, 1],
]
HOUR_VEC = [
    [1, 1, -1, -1, -1, -1, 1, 1],
    [1, -1, -1, 1, -1, 1, 1, -1],
    [1, -1, 1, -1, 1, -1, 1, -1],
    [-1, 1, -1, 1, 1, -1, 1, -1],
]
HG_COEF = 0.05
PEN_STIFF = 0.05
PEN_DEPTH = 0.5
TIME_STEP = 0.2
LANES = 128
GROUP = 16
F32 = jnp.float32
BF16 = jnp.bfloat16
VMEM_LIMIT = 48 * 1024 * 1024


def iota(shape, dim):
    return lax.broadcasted_iota(jnp.int32, shape, dim)


def dot_nn(a, b):
    return lax.dot_general(a, b, (((1,), (0,)), ((), ())), preferred_element_type=F32)


def dot_nt(a, b):
    return lax.dot_general(a, b, (((1,), (1,)), ((), ())), preferred_element_type=F32)


def dot_tn(a, b):
    return lax.dot_general(a, b, (((0,), (0,)), ((), ())), preferred_element_type=F32)


def as_bf16(mask):
    return jnp.where(mask, 1.0, 0.0).astype(BF16)


def split2(x):
    high = x.astype(BF16)
    return high, (x - high.astype(F32)).astype(BF16)


def split3(x):
    high = x.astype(BF16)
    rest = x - high.astype(F32)
    mid = rest.astype(BF16)
    return high, mid, (rest - mid.astype(F32)).astype(BF16)


def strict_upper(size):
    return as_bf16(iota((size, size), 0) < iota((size, size), 1))


def take_lanes(row, index):
    table = jnp.broadcast_to(row, index.shape)
    return jnp.take_along_axis(table, index, axis=1, mode="promise_in_bounds")


def gather_chunks(rows_of, fields, chunks, ids):
    high = ids >> 7
    low = ids & (LANES - 1)
    found = [jnp.zeros(ids.shape, F32) for _ in range(fields)]
    for chunk in range(chunks):
        here = high == chunk
        for field in range(fields):
            found[field] = jnp.where(here, take_lanes(rows_of(field, chunk), low), found[field])
    return found


def scatter_terms(id_rows, force_rows):
    wide = []
    table = []
    for ids, forces in zip(id_rows, force_rows):
        here = jnp.broadcast_to(ids >> 7, (GROUP, LANES)) == iota((GROUP, LANES), 0)
        wide.append(
            jnp.concatenate(
                [jnp.where(here, jnp.broadcast_to(f, (GROUP, LANES)), 0.0) for f in forces], axis=0
            )
        )
        low = jnp.broadcast_to(ids & (LANES - 1), (LANES, LANES))
        table.append(as_bf16(low == iota((LANES, LANES), 0)))
    high, rest = split2(jnp.concatenate(wide, axis=1))
    both = jnp.concatenate([high, rest], axis=0)
    return dot_nt(both, jnp.concatenate(table, axis=1))


def fold_terms(acc):
    half = acc.shape[0] // 2
    return acc[:half] + acc[half:]


def routing_kernel(rows_per, own_ref, count_ref, map_ref, pairs_ref, index_ref):
    own = own_ref[0]
    rows = map_ref.shape[0]
    devices = rows // rows_per
    pairs = pairs_ref.shape[1]
    hit = as_bf16(map_ref[...] == own)
    source_of = iota((devices, rows), 1) // rows_per
    upto = as_bf16(source_of <= iota((devices, rows), 0))
    within = as_bf16(source_of == iota((devices, rows), 0))
    ends = jnp.sum(dot_nn(upto, hit), axis=1, keepdims=True)
    counts = jnp.sum(dot_nn(within, hit), axis=1, keepdims=True)
    ranks = pairs_ref[...].astype(F32)
    for side in range(2):
        rank = ranks[side : side + 1]
        below = jnp.broadcast_to(ends, (devices, pairs)) <= rank
        source = jnp.sum(jnp.where(below, 1.0, 0.0), axis=0, keepdims=True)
        source = jnp.minimum(source, devices - 1.0)
        start = jnp.sum(jnp.where(below, counts, 0.0), axis=0, keepdims=True)
        index_ref[2 * side : 2 * side + 1, :] = source.astype(jnp.int32)
        index_ref[2 * side + 1 : 2 * side + 2, :] = (rank - start).astype(jnp.int32)


def segment_kernel(disp_ref, nodes_ref, ref_ref, pos_ref):
    chunks = disp_ref.shape[1] // LANES

    def step(turn, carry):
        base = pl.multiple_of(turn * 8, 8)
        ids = nodes_ref[pl.ds(base, 8), :]
        found = gather_chunks(
            lambda field, chunk: disp_ref[field : field + 1, chunk * LANES : (chunk + 1) * LANES],
            3,
            chunks,
            ids,
        )
        for field in range(3):
            pos_ref[field, pl.ds(base, 8), :] = found[field] + ref_ref[pl.ds(base, 8), field, :]
        return carry

    lax.fori_loop(0, nodes_ref.shape[0] // 8, step, 0, unroll=2)


def pack_kernel(slots, rows_per, own_ref, map_ref, pos_ref, angles_ref, nodes_ref, out_ref, ids_ref):
    own = own_ref[0]
    devices = map_ref.shape[0] // rows_per
    owner = jnp.concatenate(
        [map_ref[pl.ds(own * rows_per + i, 1), :] for i in range(rows_per)], axis=1
    )
    blocks = owner.shape[1]
    mine = iota((devices, blocks), 0) == owner
    before = dot_nn(as_bf16(mine), strict_upper(blocks))
    rank = jnp.sum(jnp.where(mine, before, 0.0), axis=0, keepdims=True).astype(jnp.int32)
    place = owner * slots + rank
    move = as_bf16(iota((devices * slots, blocks), 0) == place)
    for field in range(5):
        values = pos_ref[field] if field < 3 else angles_ref[:, field - 3, :]
        moved = dot_nn(move, jnp.concatenate(split3(values), axis=1))
        moved = moved[:, :LANES] + moved[:, LANES : 2 * LANES] + moved[:, 2 * LANES :]
        out_ref[:, field * slots : (field + 1) * slots, :] = moved.reshape(devices, slots, LANES)
    nodes = nodes_ref[...]
    halves = jnp.concatenate(
        [(nodes >> 7).astype(F32).astype(BF16), (nodes & (LANES - 1)).astype(F32).astype(BF16)],
        axis=1,
    )
    moved = dot_nn(move, halves)
    ids_ref[...] = (moved[:, :LANES] * LANES + moved[:, LANES:]).astype(jnp.int32)


def sine_cosine(angle):
    half = 0.5 * angle
    sq = half * half
    sine = sq * (-1.0 / 39916800.0) + 1.0 / 362880.0
    for coef in (-1.0 / 5040.0, 1.0 / 120.0, -1.0 / 6.0, 1.0):
        sine = sine * sq + coef
    sine = sine * half
    cosine = sq * (1.0 / 479001600.0) - 1.0 / 3628800.0
    for coef in (1.0 / 40320.0, -1.0 / 720.0, 1.0 / 24.0, -0.5, 1.0):
        cosine = cosine * sq + coef
    return 2.0 * sine * cosine, 1.0 - 2.0 * sine * sine


def pair_kernel(
    slots, index_ref, count_ref, in_ref, masks_ref, out_ref, slave_ref, master_ref, sin_ref, cos_ref
):
    pairs = masks_ref.shape[1]
    count = jnp.minimum(count_ref[0], pairs)
    out_ref[...] = jnp.zeros_like(out_ref)

    def stage(pair, carry):
        source = index_ref[0, pair]
        slot = index_ref[1, pair]
        for field in range(3):
            slave_ref[pl.ds(pair * 8 + field, 1), :] = in_ref[source, pl.ds(field * slots + slot, 1), :]
        slave_ref[pl.ds(pair * 8 + 3, 1), :] = masks_ref[0, pl.ds(pair, 1), :].astype(F32)
        source = index_ref[2, pair]
        slot = index_ref[3, pair]
        for field in range(5):
            master_ref[pl.ds(pair * 8 + field, 1), :] = in_ref[source, pl.ds(field * slots + slot, 1), :]
        master_ref[pl.ds(pair * 8 + 5, 1), :] = masks_ref[1, pl.ds(pair, 1), :].astype(F32)
        return carry

    lax.fori_loop(0, count, stage, 0)
    sines, cosines = sine_cosine(master_ref[...])
    sin_ref[...] = sines
    cos_ref[...] = cosines

    def tile(pair, carry):
        base = pl.multiple_of(pair * 8, 8)
        slave = slave_ref[pl.ds(base, 8), :]
        columns = jnp.transpose(slave)
        master = master_ref[pl.ds(base, 8), :]
        sin_az = sin_ref[pl.ds(base + 3, 1), :]
        sin_pol = sin_ref[pl.ds(base + 4, 1), :]
        cos_az = cos_ref[pl.ds(base + 3, 1), :]
        cos_pol = cos_ref[pl.ds(base + 4, 1), :]
        normal = [cos_az * cos_pol, sin_az * cos_pol, sin_pol]
        shape = (LANES, LANES)
        dist = [
            jnp.broadcast_to(columns[:, k : k + 1], shape) - jnp.broadcast_to(master[k : k + 1], shape)
            for k in range(3)
        ]
        gap = dist[0] * normal[0] + dist[1] * normal[1] + dist[2] * normal[2]
        tang = dist[0] * dist[0] + dist[1] * dist[1] + dist[2] * dist[2] - gap * gap
        bend = gap * (-1.0 / PEN_DEPTH)
        soft = jnp.maximum(bend, 0.0) + jnp.log(1.0 + jnp.exp(-jnp.abs(bend)))
        press = soft * jnp.exp(-0.5 * tang)
        press = press * jnp.broadcast_to(columns[:, 3:4], shape)
        total = jnp.sum(press, axis=0, keepdims=True)
        scale = PEN_STIFF * PEN_DEPTH * master[5:6]
        push = [n * scale for n in normal]
        rows = jnp.concatenate(push + [jnp.zeros((5, LANES), F32)], axis=0)
        push_high, push_rest = split2(rows)
        both = jnp.concatenate([push_high, push_rest], axis=0)
        high, rest = split2(press)
        got = dot_nt(both, high) + dot_nt(both, rest)
        on_slave = got[0:8] + got[8:16]
        source = index_ref[0, pair]
        slot = index_ref[1, pair]
        for k in range(3):
            at = pl.ds(k * slots + slot, 1)
            out_ref[source, at, :] = out_ref[source, at, :] + on_slave[k : k + 1]
        source = index_ref[2, pair]
        slot = index_ref[3, pair]
        for k in range(3):
            at = pl.ds(k * slots + slot, 1)
            out_ref[source, at, :] = out_ref[source, at, :] - push[k] * total
        return carry

    lax.fori_loop(0, count, tile, 0)


def element_kernel(conn_ref, coords_ref, disp_ref, modulus_ref, out_ref, order_ref):
    chunks = coords_ref.shape[1] // LANES
    groups = conn_ref.shape[1] // LANES
    for group in range(groups):
        order_ref[pl.ds(group * 8, 8), :] = conn_ref[:, group * LANES : (group + 1) * LANES]
    pos = []
    disp = []
    for corner in range(8):
        ids = order_ref[pl.ds(corner, groups, stride=8), :]
        found = gather_chunks(
            lambda field, chunk: (coords_ref if field < 3 else disp_ref)[
                field % 3 : field % 3 + 1, chunk * LANES : (chunk + 1) * LANES
            ],
            6,
            chunks,
            ids,
        )
        pos.append(found[:3])
        disp.append(found[3:])
    first = list(pos[0])
    pos = [[pos[corner][j] - first[j] for j in range(3)] for corner in range(8)]

    def signed(values, signs):
        total = None
        for value, sign in zip(values, signs):
            if total is None:
                total = value if sign > 0 else -value
            else:
                total = total + value if sign > 0 else total - value
        return total

    corner_signs = [[XI_SIGNS[corner][k] for corner in range(8)] for k in range(3)]
    jac = [
        [signed([pos[c][j] for c in range(8)], corner_signs[k]) * 0.125 for k in range(3)]
        for j in range(3)
    ]
    cof = [
        [
            jac[(j + 1) % 3][(k + 1) % 3] * jac[(j + 2) % 3][(k + 2) % 3]
            - jac[(j + 1) % 3][(k + 2) % 3] * jac[(j + 2) % 3][(k + 1) % 3]
            for k in range(3)
        ]
        for j in range(3)
    ]
    det = jac[0][0] * cof[0][0] + jac[0][1] * cof[0][1] + jac[0][2] * cof[0][2]
    volume = 8.0 * det
    inverse = 1.0 / volume
    scaled = [[cof[j][k] * inverse for k in range(3)] for j in range(3)]
    grad = [[signed(scaled[j], XI_SIGNS[c]) for j in range(3)] for c in range(8)]

    def summed(terms):
        total = terms[0]
        for term in terms[1:]:
            total = total + term
        return total

    ugrad = [
        [summed([disp[c][i] * grad[c][j] for c in range(8)]) for j in range(3)] for i in range(3)
    ]
    modulus = modulus_ref[...]
    dilation = ugrad[0][0] + ugrad[1][1] + ugrad[2][2]
    stress = [[modulus * (ugrad[i][j] + ugrad[j][i]) for j in range(3)] for i in range(3)]
    for i in range(3):
        stress[i][i] = stress[i][i] + modulus * dilation
    squares = summed([grad[c][j] * grad[c][j] for c in range(8) for j in range(3)])
    hour_coef = HG_COEF * modulus * volume * squares
    shapes = []
    modes = []
    for a in range(4):
        hour_pos = [signed([pos[c][j] for c in range(8)], HOUR_VEC[a]) for j in range(3)]
        gam = [
            float(HOUR_VEC[a][c]) - summed([hour_pos[j] * grad[c][j] for j in range(3)])
            for c in range(8)
        ]
        shapes.append(gam)
        modes.append(
            [hour_coef * summed([disp[c][i] * gam[c] for c in range(8)]) for i in range(3)]
        )
    flux = [[volume * stress[i][j] for j in range(3)] for i in range(3)]
    acc = jnp.zeros((6 * GROUP, LANES), F32)
    for corner in range(8):
        ids = order_ref[pl.ds(corner, groups, stride=8), :]
        force = []
        for i in range(3):
            value = summed([flux[i][j] * grad[corner][j] for j in range(3)])
            value = value + summed([modes[a][i] * shapes[a][corner] for a in range(4)])
            force.append(-value)
        for group in range(0, groups, 2):
            picks = range(group, min(group + 2, groups))
            acc = acc + scatter_terms(
                [ids[g : g + 1] for g in picks], [[f[g : g + 1] for f in force] for g in picks]
            )
    out_ref[...] = fold_terms(acc)


def send_faces(total_ref, chunks, faces_ref, low_row, low_ref, high_ref):
    low_ref[...] = jnp.zeros_like(low_ref)
    high_ref[...] = jnp.zeros_like(high_ref)
    parts = faces_ref.shape[1] // LANES
    for part in range(parts):
        ids = faces_ref[:, part * LANES : (part + 1) * LANES]
        found = gather_chunks(
            lambda field, chunk: total_ref[field * GROUP + chunk : field * GROUP + chunk + 1, :],
            3,
            chunks,
            ids,
        )
        for field in range(3):
            at = field * parts + part
            low_ref[at : at + 1, :] = found[field][low_row : low_row + 1]
            high_ref[at : at + 1, :] = found[field][low_row + 1 : low_row + 2]


def add_faces(faces_ref, low_row, low_ref, high_ref):
    parts = faces_ref.shape[1] // LANES
    acc = None
    for row, got_ref in ((low_row, low_ref), (low_row + 1, high_ref)):
        ids = [faces_ref[row : row + 1, p * LANES : (p + 1) * LANES] for p in range(parts)]
        forces = [
            [got_ref[f * parts + p : f * parts + p + 1, :] for f in range(3)] for p in range(parts)
        ]
        terms = scatter_terms(ids, forces)
        acc = terms if acc is None else acc + terms
    return fold_terms(acc)


def assemble_kernel(slots, chunks, back_ref, ids_ref, inner_ref, faces_ref, out_ref, low_ref, high_ref):
    devices = back_ref.shape[0]

    def step(turn, acc):
        ids = ids_ref[pl.ds(turn * slots, slots), :]
        values = back_ref[turn]
        for slot in range(0, slots, 2):
            picks = range(slot, min(slot + 2, slots))
            acc = acc + scatter_terms(
                [ids[s : s + 1] for s in picks],
                [[values[f * slots + s : f * slots + s + 1] for f in range(3)] for s in picks],
            )
        return acc

    acc = lax.fori_loop(0, devices, step, jnp.zeros((6 * GROUP, LANES), F32))
    out_ref[...] = inner_ref[...] + fold_terms(acc)
    send_faces(out_ref, chunks, faces_ref, 0, low_ref, high_ref)


def middle_kernel(chunks, total_ref, from_low, from_high, faces_ref, out_ref, low_ref, high_ref):
    out_ref[...] = total_ref[...] + add_faces(faces_ref, 0, from_low, from_high)
    send_faces(out_ref, chunks, faces_ref, 2, low_ref, high_ref)


def final_kernel(total_ref, from_low, from_high, faces_ref, velocity_ref, mass_ref, out_ref, sum_ref):
    sum_ref[...] = total_ref[...] + add_faces(faces_ref, 2, from_low, from_high)
    for chunk in range(out_ref.shape[1] // LANES):
        span = slice(chunk * LANES, (chunk + 1) * LANES)
        scale = TIME_STEP / mass_ref[chunk : chunk + 1, :]
        for field in range(3):
            row = field * GROUP + chunk
            out_ref[field : field + 1, span] = (
                velocity_ref[field : field + 1, span] + scale * sum_ref[row : row + 1, :]
            )


def call(kernel, outs, in_smem, args, scratch=()):
    specs = [
        pl.BlockSpec(memory_space=pltpu.SMEM if i in in_smem else pltpu.VMEM)
        for i in range(len(args))
    ]
    out_shape = [jax.ShapeDtypeStruct(shape, dtype) for shape, dtype in outs]
    return pl.pallas_call(
        kernel,
        out_shape=out_shape,
        in_specs=specs,
        out_specs=[pl.BlockSpec(memory_space=pltpu.VMEM) for _ in outs],
        scratch_shapes=list(scratch),
        compiler_params=pltpu.CompilerParams(vmem_limit_bytes=VMEM_LIMIT),
    )(*args)


def exchange(low, high, axis):
    count = lax.axis_size(axis)
    forward = [(i, i + 1) for i in range(count - 1)]
    backward = [(target, source) for source, target in forward]
    return lax.ppermute(high, axis, forward), lax.ppermute(low, axis, backward)


def local(
    connectivity,
    face_nodes,
    coords,
    displacement,
    velocity,
    node_mass,
    modulus,
    surf_nodes,
    surf_ref,
    surf_angles,
    owner_map,
    pair_blocks,
    pair_masks,
    pair_count,
):
    axes = ("gx", "gy")
    devices = lax.axis_size("gx") * lax.axis_size("gy")
    per_dev = surf_nodes.shape[0]
    rows_per = per_dev // LANES
    node_count = coords.shape[1]
    chunks = node_count // LANES
    slots = 2 * per_dev // devices
    pairs = pair_blocks.shape[1]
    own = lax.axis_index(axes).reshape(1).astype(jnp.int32)
    owners = owner_map.reshape(devices * rows_per, LANES)
    face_pad = -face_nodes.shape[1] % LANES
    faces = jnp.pad(face_nodes, ((0, 4), (0, face_pad)), constant_values=-1)
    parts = faces.shape[1] // LANES
    face_rows = -(-3 * parts // 8) * 8
    total_shape = ((3 * GROUP, LANES), F32)
    face_shape = ((face_rows, LANES), F32)

    [index] = call(
        functools.partial(routing_kernel, rows_per),
        [((4, pairs), jnp.int32)],
        (0, 1),
        (own, pair_count, owners, pair_blocks),
    )
    [pos] = call(
        segment_kernel, [((3, per_dev, LANES), F32)], (), (displacement, surf_nodes, surf_ref)
    )
    outbound, ids = call(
        functools.partial(pack_kernel, slots, rows_per),
        [((devices, 5 * slots, LANES), F32), ((devices * slots, LANES), jnp.int32)],
        (0,),
        (own, owners, pos, surf_angles, surf_nodes),
    )
    inbound = lax.all_to_all(outbound, axes, split_axis=0, concat_axis=0, tiled=True)
    [internal] = call(
        element_kernel,
        [total_shape],
        (),
        (connectivity, coords, displacement, modulus.reshape(-1, LANES)),
        [pltpu.VMEM((connectivity.shape[1] // LANES * 8, LANES), jnp.int32)],
    )
    [forces] = call(
        functools.partial(pair_kernel, slots),
        [((devices, 3 * slots, LANES), F32)],
        (0, 1),
        (index, pair_count, inbound, pair_masks),
        [pltpu.VMEM((pairs * 8, LANES), F32)] * 4,
    )
    returned = lax.all_to_all(forces, axes, split_axis=0, concat_axis=0, tiled=True)
    total, low, high = call(
        functools.partial(assemble_kernel, slots, chunks),
        [total_shape, face_shape, face_shape],
        (),
        (returned, ids, internal, faces),
    )
    from_low, from_high = exchange(low, high, "gx")
    total, low, high = call(
        functools.partial(middle_kernel, chunks),
        [total_shape, face_shape, face_shape],
        (),
        (total, from_low, from_high, faces),
    )
    from_low, from_high = exchange(low, high, "gy")
    [result] = call(
        final_kernel,
        [((3, node_count), F32)],
        (),
        (total, from_low, from_high, faces, velocity, node_mass.reshape(chunks, LANES)),
        [pltpu.VMEM((3 * GROUP, LANES), F32)],
    )
    return result


def solution(mesh):
    in_specs = (
        P(None, ("gx", "gy")),
        P(None, ("gx", "gy")),
        P(None, ("gx", "gy")),
        P(None, ("gx", "gy")),
        P(None, ("gx", "gy")),
        P(("gx", "gy")),
        P(("gx", "gy")),
        P(("gx", "gy"), None),
        P(("gx", "gy"), None, None),
        P(("gx", "gy"), None, None),
        P(),
        P(None, ("gx", "gy")),
        P(None, ("gx", "gy"), None),
        P(("gx", "gy")),
    )
    out_specs = P(None, ("gx", "gy"))
    return jax.shard_map(local, mesh=mesh, in_specs=in_specs, out_specs=out_specs, check_vma=False)
```

profile of v0, /device:TPU:3, one launch (start us, length us, event | category | flops | bytes accessed | tf_op | source)
XLA Modules:
  0.0 125.6 jit_solution(8271635895660391946)
XLA Ops:
  0.0 1.3 %copy.15.ref_ref = f32[256,3,128]{2,1,0:T(4,128)S(1)} copy(f32[256,3,128]{2,0,1:T(8,128)} %param.22) | data formatting | bytes 786432 | tf_op args[8]
  1.3 0.0 copy-start
  1.4 0.9 copy-done
  2.3 0.7 copy-done.4
  3.0 2.3 %shard_map.137.pos_ref = f32[3,256,128]{2,1,0:T(8,128)S(1)} custom-call(f32[3,1408]{1,0:T(4,128)S(1)} %copy-done.4, s32[256,128]{1,0:T(8,128)S(1)} %copy-done, f32[256,3,128]{2,1,0:T(4,128)S(1)} %copy.15.ref_ref), custom_call_target="tpu_custom_call" | custom-call | tf_op jit(solution)/shard_map/pallas_call | solution.py:429
  5.3 3.0 %shard_map.138 = (f32[32,80,128]{2,1,0:T(8,128)}, s32[512,128]{1,0:T(8,128)S(1)}) custom-call(s32[1]{0:T(128)} %bitcast.own_ref, s32[64,128]{1,0:T(8,128)S(1)} %bitcast.4, f32[3,256,128]{2,1,0:T(8,128)S(1)} %shard_map.137.pos_ref, f32[256,2,128]{2,1,0:T(2,128)S(1)} %copy-done.2, s32[256,128]{1,0:T(8,128)S(1)} %copy-done.1), custom_call_target="tpu_custom_call" | custom-call | tf_op jit(solution)/shard_map/pallas_call | solution.py:429
  8.3 6.4 %all-to-all-start = ((f32[32,80,128]{2,1,0:T(8,128)}), f32[32,80,128]{2,1,0:T(8,128)S(1)}, u32[]{:S(2)}, u32[]{:S(2)}) async-start(f32[32,80,128]{2,1,0:T(8,128)} %get-tuple-element.13), calls=%async_computation | async-start | bytes 2621440 | tf_op jit(solution)/shard_map/all_to_all | solution.py:494
  15.4 0.2 shard_map.136.index_ref
  15.6 30.0 %all-to-all-done.in_ref = f32[32,80,128]{2,1,0:T(8,128)S(1)} async-done(((f32[32,80,128]{2,1,0:T(8,128)}), f32[32,80,128]{2,1,0:T(8,128)S(1)}, u32[]{:S(2)}, u32[]{:S(2)}) %all-to-all-start) | async-done | bytes 1310752 | tf_op jit(solution)/shard_map/all_to_all | solution.py:494
  45.6 11.2 %shard_map.139 = f32[32,48,128]{2,1,0:T(8,128)} custom-call(s32[4,64]{1,0:T(4,128)S(1)} %shard_map.136.index_ref, s32[1]{0:T(128)S(6)} %copy.16.count_ref, f32[32,80,128]{2,1,0:T(8,128)S(1)} %all-to-all-done.in_ref, s32[2,64,128]{2,1,0:T(8,128)S(1)} %copy-done.6), custom_call_target="tpu_custom_call" | custom-call | tf_op jit(solution)/shard_map/pallas_call | solution.py:429
  56.8 0.0 copy-start.11
  56.8 0.0 copy-start.9
  56.9 18.9 %all-to-all-start.1 = ((f32[32,48,128]{2,1,0:T(8,128)}), f32[32,48,128]{2,1,0:T(8,128)S(1)}, u32[]{:S(2)}, u32[]{:S(2)}) async-start(f32[32,48,128]{2,1,0:T(8,128)} %shard_map.139), calls=%async_computation.1 | async-start | bytes 1572864 | tf_op jit(solution)/shard_map/all_to_all | solution.py:509
  75.8 1.9 %shard_map.140.inner_ref = f32[48,128]{1,0:T(8,128)S(1)} custom-call(s32[8,1024]{1,0:T(8,128)S(1)} %copy-done.7, f32[3,1408]{1,0:T(4,128)S(1)} %copy-done.8, f32[3,1408]{1,0:T(4,128)S(1)} %copy-done.5, f32[8,128]{1,0:T(8,128)S(1)} %bitcast.7), custom_call_target="tpu_custom_call" | custom-call | tf_op jit(solution)/shard_map/pallas_call | solution.py:429
  77.7 18.4 %all-to-all-done.1.back_ref = f32[32,48,128]{2,1,0:T(8,128)S(1)} async-done(((f32[32,48,128]{2,1,0:T(8,128)}), f32[32,48,128]{2,1,0:T(8,128)S(1)}, u32[]{:S(2)}, u32[]{:S(2)}) %all-to-all-start.1) | async-done | bytes 786464 | tf_op jit(solution)/shard_map/all_to_all | solution.py:509
  96.1 10.9 %shard_map.141 = (f32[48,128]{1,0:T(8,128)S(1)}, f32[8,128]{1,0:T(8,128)S(1)}, f32[8,128]{1,0:T(8,128)S(1)}) custom-call(f32[32,48,128]{2,1,0:T(8,128)S(1)} %all-to-all-done.1.back_ref, s32[512,128]{1,0:T(8,128)S(1)} %get-tuple-element.14.ids_ref, f32[48,128]{1,0:T(8,128)S(1)} %shard_map.140.inner_ref, s32[8,256]{1,0:T(8,128)S(1)} %pad.4.faces_ref), custom_call_target="tpu_custom_call" | custom-call | tf_op jit(solution)/shard_map/pallas_call | solution.py:429
  107.0 2.5 %collective-permute-start = (f32[8,128]{1,0:T(8,128)S(1)}, f32[8,128]{1,0:T(8,128)S(1)}, u32[]{:S(2)}, u32[]{:S(2)}) collective-permute-start(f32[8,128]{1,0:T(8,128)S(1)} %get-tuple-element.16), channel_id=1, source_target_pairs={{0,8},{8,16},{16,24},{1,9},{9,17},{17,25},{2,10},{10,18},{18,26},{... | collective-permute-start | bytes 12296 | tf_op jit(solution)/shard_map/ppermute | solution.py:443
  109.5 1.3 %collective-permute-start.1 = (f32[8,128]{1,0:T(8,128)S(1)}, f32[8,128]{1,0:T(8,128)S(1)}, u32[]{:S(2)}, u32[]{:S(2)}) collective-permute-start(f32[8,128]{1,0:T(8,128)S(1)} %get-tuple-element.17), channel_id=1, source_target_pairs={{8,0},{16,8},{24,16},{9,1},{17,9},{25,17},{10,2},{18,10},{26,18},{... | collective-permute-start | bytes 12296 | tf_op jit(solution)/shard_map/ppermute | solution.py:443
  110.8 3.0 %collective-permute-done.1.from_high = f32[8,128]{1,0:T(8,128)S(1)} collective-permute-done((f32[8,128]{1,0:T(8,128)S(1)}, f32[8,128]{1,0:T(8,128)S(1)}, u32[]{:S(2)}, u32[]{:S(2)}) %collective-permute-start.1) | collective-permute-done | bytes 4128 | tf_op jit(solution)/shard_map/ppermute | solution.py:443
  113.9 0.3 shard_map.142
  114.2 4.7 %collective-permute-start.2 = (f32[8,128]{1,0:T(8,128)S(1)}, f32[8,128]{1,0:T(8,128)S(1)}, u32[]{:S(2)}, u32[]{:S(2)}) collective-permute-start(f32[8,128]{1,0:T(8,128)S(1)} %get-tuple-element.19), channel_id=1, source_target_pairs={{0,1},{1,2},{2,3},{3,4},{4,5},{5,6},{6,7},{8,9},{9,10},{10,11},{11... | collective-permute-start | bytes 12296 | tf_op jit(solution)/shard_map/ppermute | solution.py:443
  119.0 1.9 %collective-permute-start.3 = (f32[8,128]{1,0:T(8,128)S(1)}, f32[8,128]{1,0:T(8,128)S(1)}, u32[]{:S(2)}, u32[]{:S(2)}) collective-permute-start(f32[8,128]{1,0:T(8,128)S(1)} %get-tuple-element.20), channel_id=1, source_target_pairs={{1,0},{2,1},{3,2},{4,3},{5,4},{6,5},{7,6},{9,8},{10,9},{11,10},{12... | collective-permute-start | bytes 12296 | tf_op jit(solution)/shard_map/ppermute | solution.py:443
  120.9 3.9 %collective-permute-done.3.from_high = f32[8,128]{1,0:T(8,128)S(1)} collective-permute-done((f32[8,128]{1,0:T(8,128)S(1)}, f32[8,128]{1,0:T(8,128)S(1)}, u32[]{:S(2)}, u32[]{:S(2)}) %collective-permute-start.3) | collective-permute-done | bytes 4128 | tf_op jit(solution)/shard_map/ppermute | solution.py:443
  124.8 0.8 shard_map.143
  (26 shorter events, 0.1 us)
Async XLA Ops:
  0.0 5.3 %copy-start.1 = (s32[256,128]{1,0:T(8,128)S(1)}, s32[256,128]{1,0:T(8,128)}, u32[]{:S(2)}) copy-start(s32[256,128]{1,0:T(8,128)} %nodes_ref.3) | copy-start | bytes 393220
  0.0 5.3 %copy-start.3 = (s32[8192]{0:T(1024)S(1)}, s32[8192]{0:T(1024)}, u32[]{:S(2)}) copy-start(s32[8192]{0:T(1024)} %param.24) | copy-start | bytes 98308
  0.0 5.3 %copy-start.2 = (f32[256,2,128]{2,1,0:T(2,128)S(1)}, f32[256,2,128]{2,1,0:T(2,128)}, u32[]{:S(2)}) copy-start(f32[256,2,128]{2,1,0:T(2,128)} %angles_ref.1) | copy-start | bytes 786436
  1.3 0.9 copy-start
  2.3 0.7 copy-start.4
  8.3 7.1 %copy-start.12 = (s32[2,64]{1,0:T(2,128)S(1)}, s32[2,64]{1,0:T(2,128)}, u32[]{:S(2)}) copy-start(s32[2,64]{1,0:T(2,128)} %pairs_ref.1) | copy-start | bytes 1540
  8.3 37.3 %copy-start.6 = (s32[2,64,128]{2,1,0:T(8,128)S(1)}, s32[2,64,128]{2,1,0:T(8,128)}, u32[]{:S(2)}) copy-start(s32[2,64,128]{2,1,0:T(8,128)} %masks_ref.1) | copy-start | bytes 196612
  8.3 37.3 %all-to-all-start = ((f32[32,80,128]{2,1,0:T(8,128)}), f32[32,80,128]{2,1,0:T(8,128)S(1)}, u32[]{:S(2)}, u32[]{:S(2)}) async-start(f32[32,80,128]{2,1,0:T(8,128)} %get-tuple-element.13), calls=%async_computation | async-start | bytes 2621440 | tf_op jit(solution)/shard_map/all_to_all | solution.py:494
  56.8 18.9 %copy-start.13 = (s32[4,153]{1,0:T(4,128)S(1)}, s32[4,153]{1,0:T(4,128)}, u32[]{:S(2)}) copy-start(s32[4,153]{1,0:T(4,128)} %param.15) | copy-start | bytes 7348
  56.8 19.0 %copy-start.5 = (f32[3,1408]{1,0:T(4,128)S(1)}, f32[3,1408]{1,0:T(4,128)}, u32[]{:S(2)}) copy-start(f32[3,1408]{1,0:T(4,128)} %disp_ref.3) | copy-start | bytes 50692
  56.8 19.0 %copy-start.7 = (s32[8,1024]{1,0:T(8,128)S(1)}, s32[8,1024]{1,0:T(8,128)}, u32[]{:S(2)}) copy-start(s32[8,1024]{1,0:T(8,128)} %conn_ref.1) | copy-start | bytes 98308
  56.8 19.0 %copy-start.8 = (f32[3,1408]{1,0:T(4,128)S(1)}, f32[3,1408]{1,0:T(4,128)}, u32[]{:S(2)}) copy-start(f32[3,1408]{1,0:T(4,128)} %coords_ref.1) | copy-start | bytes 50692
  56.8 19.0 %copy-start.11 = (f32[1024]{0:T(1024)S(1)}, f32[1024]{0:T(1024)}, u32[]{:S(2)}) copy-start(f32[1024]{0:T(1024)} %param.20) | copy-start | bytes 12292
  56.8 68.0 %copy-start.9 = (f32[3,1408]{1,0:T(4,128)S(1)}, f32[3,1408]{1,0:T(4,128)}, u32[]{:S(2)}) copy-start(f32[3,1408]{1,0:T(4,128)} %velocity_ref.1) | copy-start | bytes 50692
  56.9 68.0 %copy-start.10 = (f32[1408]{0:T(1024)S(1)}, f32[1408]{0:T(1024)}, u32[]{:S(2)}) copy-start(f32[1408]{0:T(1024)} %param.19) | copy-start | bytes 16900
  56.9 39.2 %all-to-all-start.1 = ((f32[32,48,128]{2,1,0:T(8,128)}), f32[32,48,128]{2,1,0:T(8,128)S(1)}, u32[]{:S(2)}, u32[]{:S(2)}) async-start(f32[32,48,128]{2,1,0:T(8,128)} %shard_map.139), calls=%async_computation.1 | async-start | bytes 1572864 | tf_op jit(solution)/shard_map/all_to_all | solution.py:509
  107.0 3.8 %collective-permute-start = (f32[8,128]{1,0:T(8,128)S(1)}, f32[8,128]{1,0:T(8,128)S(1)}, u32[]{:S(2)}, u32[]{:S(2)}) collective-permute-start(f32[8,128]{1,0:T(8,128)S(1)} %get-tuple-element.16), channel_id=1, source_target_pairs={{0,8},{8,16},{16,24},{1,9},{9,17},{17,25},{2,10},{10,18},{18,26},{... | collective-permute-start | bytes 12296 | tf_op jit(solution)/shard_map/ppermute | solution.py:443
  109.5 4.4 %collective-permute-start.1 = (f32[8,128]{1,0:T(8,128)S(1)}, f32[8,128]{1,0:T(8,128)S(1)}, u32[]{:S(2)}, u32[]{:S(2)}) collective-permute-start(f32[8,128]{1,0:T(8,128)S(1)} %get-tuple-element.17), channel_id=1, source_target_pairs={{8,0},{16,8},{24,16},{9,1},{17,9},{25,17},{10,2},{18,10},{26,18},{... | collective-permute-start | bytes 12296 | tf_op jit(solution)/shard_map/ppermute | solution.py:443
  114.2 6.7 %collective-permute-start.2 = (f32[8,128]{1,0:T(8,128)S(1)}, f32[8,128]{1,0:T(8,128)S(1)}, u32[]{:S(2)}, u32[]{:S(2)}) collective-permute-start(f32[8,128]{1,0:T(8,128)S(1)} %get-tuple-element.19), channel_id=1, source_target_pairs={{0,1},{1,2},{2,3},{3,4},{4,5},{5,6},{6,7},{8,9},{9,10},{10,11},{11... | collective-permute-start | bytes 12296 | tf_op jit(solution)/shard_map/ppermute | solution.py:443
  119.0 5.8 %collective-permute-start.3 = (f32[8,128]{1,0:T(8,128)S(1)}, f32[8,128]{1,0:T(8,128)S(1)}, u32[]{:S(2)}, u32[]{:S(2)}) collective-permute-start(f32[8,128]{1,0:T(8,128)S(1)} %get-tuple-element.20), channel_id=1, source_target_pairs={{1,0},{2,1},{3,2},{4,3},{5,4},{6,5},{7,6},{9,8},{10,9},{11,10},{12... | collective-permute-start | bytes 12296 | tf_op jit(solution)/shard_map/ppermute | solution.py:443
where the time goes:
time: 126 us
  waiting for transfers between devices  55.3 us (44%)
  starting transfers between devices  35.8 us (28%)
  Pallas kernels  30.7 us (24%)
  local copies, waits for them, and re-layouts  3.01 us (2%)
    pallas_call x8, Pallas kernels, call(): pl.pallas_call(kernel, out_shape=out_shape, in_specs=specs, out_specs=[pl...  30.7 us
    all_to_all x1, waiting for transfers between devices, local(): lax.all_to_all(outbound, axes, split_axis=0, concat_axis=0, tiled=True)  30 us
    all_to_all x1, starting transfers between devices, local(): lax.all_to_all(forces, axes, split_axis=0, concat_axis=0, tiled=True)  18.9 us
    all_to_all x1, waiting for transfers between devices, local(): lax.all_to_all(forces, axes, split_axis=0, concat_axis=0, tiled=True)  18.4 us
    ppermute x2, starting transfers between devices, exchange(): lax.ppermute(high, axis, forward)  7.26 us
    ppermute x2, waiting for transfers between devices, exchange(): lax.ppermute(low, axis, backward)  6.93 us
    all_to_all x1, starting transfers between devices, local(): lax.all_to_all(outbound, axes, split_axis=0, concat_axis=0, tiled=True)  6.44 us
    ppermute x2, starting transfers between devices, exchange(): lax.ppermute(low, axis, backward)  3.21 us
  transfers between devices with their start and end apart: 6, of which 4 were waited for; matrix products, arithmetic and copies ran while one was open for 0% of the time, Pallas kernels for 2%

commit v1 on v0

--- a/solution.py
+++ b/solution.py
@@ -32,6 +32,15 @@
 F32 = jnp.float32
 BF16 = jnp.bfloat16
 VMEM_LIMIT = 48 * 1024 * 1024
+REQUEST_ROWS = 16
+TASK_CAP = 7
+TASK_LANE = 64
+ENTRY_LANE = 4
+ENTRY_CAP = 20
+SEND_ROWS = 32
+BACK_ROWS = 8
+ENTRIES = 160
+TASKS = 64
 
 
 def iota(shape, dim):
@@ -130,11 +139,110 @@
         index_ref[2 * side + 1 : 2 * side + 2, :] = (rank - start).astype(jnp.int32)
 
 
-def segment_kernel(disp_ref, nodes_ref, ref_ref, pos_ref):
+def request_kernel(rows_per, own_ref, count_ref, map_ref, pairs_ref, masks_ref, out_ref):
+    own = own_ref[0]
+    rows = map_ref.shape[0]
+    devices = rows // rows_per
+    pairs = pairs_ref.shape[1]
+    hit = as_bf16(map_ref[...] == own)
+    source_of = iota((devices, rows), 1) // rows_per
+    upto = as_bf16(source_of <= iota((devices, rows), 0))
+    within = as_bf16(source_of == iota((devices, rows), 0))
+    ends = jnp.sum(dot_nn(upto, hit), axis=1, keepdims=True)
+    counts = jnp.sum(dot_nn(within, hit), axis=1, keepdims=True)
+    ranks = pairs_ref[...].astype(F32)
+    where_is = []
+    for side in range(2):
+        rank = ranks[side : side + 1]
+        below = jnp.broadcast_to(ends, (devices, pairs)) <= rank
+        source = jnp.sum(jnp.where(below, 1.0, 0.0), axis=0, keepdims=True)
+        source = jnp.minimum(source, devices - 1.0)
+        start = jnp.sum(jnp.where(below, counts, 0.0), axis=0, keepdims=True)
+        where_is.append((source, rank - start))
+    (slave, slave_rank), (master, master_rank) = where_is
+    lane = iota((1, pairs), 1)
+    live = lane < count_ref[0]
+    me = own.astype(F32)
+    device = iota((devices, pairs), 0).astype(F32)
+    earlier = strict_upper(pairs)
+
+    def pick(target, keep):
+        return jnp.where((device == target) & keep, 1.0, 0.0)
+
+    worker = jnp.where(lane == 0, me, slave)
+    tasks = pick(worker, live)
+    turn = jnp.sum(tasks * dot_nn(tasks.astype(BF16), earlier), axis=0, keepdims=True)
+    worker = jnp.where(turn >= TASK_CAP, me, worker)
+    tasks = pick(worker, live)
+    turn = jnp.sum(tasks * dot_nn(tasks.astype(BF16), earlier), axis=0, keepdims=True)
+    send_slave = live & (slave != worker)
+    send_master = live & (master != worker)
+    from_slave = pick(slave, send_slave)
+    from_master = pick(master, send_master)
+    both = from_slave + from_master
+    ahead = dot_nn(both.astype(BF16), earlier)
+    slave_at = jnp.sum(from_slave * ahead, axis=0, keepdims=True)
+    master_at = jnp.sum(from_master * ahead, axis=0, keepdims=True)
+    master_at = master_at + jnp.where(send_slave & (slave == master), 1.0, 0.0)
+
+    column = iota((LANES, pairs), 0).astype(F32)
+
+    def placed(first, fields, fits):
+        total = jnp.zeros((LANES, pairs), F32)
+        for at, field in enumerate(fields):
+            total = jnp.where((column == first + at) & fits, field, total)
+        return total.astype(BF16)
+
+    zero = jnp.zeros_like(slave)
+    entry = placed(ENTRY_LANE + 3 * slave_at, (zero, slave_rank, worker), slave_at < ENTRY_CAP)
+    line = dot_nt(from_slave.astype(BF16), entry)
+    entry = placed(
+        ENTRY_LANE + 3 * master_at, (zero + 1.0, master_rank, worker), master_at < ENTRY_CAP
+    )
+    line = line + dot_nt(from_master.astype(BF16), entry)
+    entry = placed(
+        TASK_LANE + 4 * turn, (slave, slave_rank, master, master_rank), turn < TASK_CAP
+    )
+    line = line + dot_nt(tasks.astype(BF16), entry)
+    entry_count = jnp.sum(both, axis=1, keepdims=True)
+    task_count = jnp.sum(tasks, axis=1, keepdims=True)
+    over = jnp.where((entry_count > ENTRY_CAP) | (task_count > TASK_CAP), 1.0, 0.0)
+    over = jnp.max(over, axis=0, keepdims=True)
+    spot = iota((devices, LANES), 1)
+    line = jnp.where(spot == 0, entry_count, line)
+    line = jnp.where(spot == 1, task_count, line)
+    line = jnp.where(spot == 2, over, line)
+    out_ref[:, 0, :] = line.astype(jnp.int32)
+    chosen = [jnp.where(turn == t, tasks, 0.0) for t in range(TASK_CAP)]
+    chosen = jnp.concatenate(chosen, axis=0).astype(BF16)
+    masks = jnp.concatenate([masks_ref[0], masks_ref[1]], axis=1).astype(F32).astype(BF16)
+    got = dot_nn(chosen, masks).astype(jnp.int32)
+    for t in range(TASK_CAP):
+        part = got[t * devices : (t + 1) * devices]
+        out_ref[:, 1 + 2 * t, :] = part[:, :LANES]
+        out_ref[:, 2 + 2 * t, :] = part[:, LANES:]
+    for row in range(1 + 2 * TASK_CAP, REQUEST_ROWS):
+        out_ref[:, row, :] = jnp.zeros((devices, LANES), jnp.int32)
+
+
+def segment_kernel(
+    cap, owners_ref, disp_ref, nodes_ref, ref_ref, angles_ref, pos_ref, normal_ref, block_ref, seen_ref
+):
     chunks = disp_ref.shape[1] // LANES
+
+    def clear(device, carry):
+        seen_ref[device] = 0
+        return carry
+
+    lax.fori_loop(0, seen_ref.shape[0], clear, 0)
 
     def step(turn, carry):
         base = pl.multiple_of(turn * 8, 8)
+        for k in range(8):
+            owner = owners_ref[base + k]
+            rank = seen_ref[owner]
+            block_ref[owner * cap + rank] = base + k
+            seen_ref[owner] = rank + 1
         ids = nodes_ref[pl.ds(base, 8), :]
         found = gather_chunks(
             lambda field, chunk: disp_ref[field : field + 1, chunk * LANES : (chunk + 1) * LANES],
@@ -144,9 +252,98 @@
         )
         for field in range(3):
             pos_ref[field, pl.ds(base, 8), :] = found[field] + ref_ref[pl.ds(base, 8), field, :]
+        sin_az, cos_az = sine_cosine(angles_ref[pl.ds(base, 8), 0, :])
+        sin_pol, cos_pol = sine_cosine(angles_ref[pl.ds(base, 8), 1, :])
+        normal_ref[0, pl.ds(base, 8), :] = cos_az * cos_pol
+        normal_ref[1, pl.ds(base, 8), :] = sin_az * cos_pol
+        normal_ref[2, pl.ds(base, 8), :] = sin_pol
         return carry
 
     lax.fori_loop(0, nodes_ref.shape[0] // 8, step, 0, unroll=2)
+
+
+def plan_kernel(
+    cap, own_ref, list_ref, block_ref, pos_ref, angles_ref, out_ref, entry_ref, task_ref, used_ref
+):
+    own = own_ref[0]
+    devices = list_ref.shape[0]
+
+    def clear(device, carry):
+        for row in range(4):
+            used_ref[row, device] = 0
+        return carry
+
+    lax.fori_loop(0, devices, clear, 0)
+
+    def from_owner(owner, carry):
+        def entry(turn, state):
+            number, over = state
+            at = ENTRY_LANE + 3 * turn
+            role = list_ref[owner, at]
+            block = block_ref[owner * cap + list_ref[owner, at + 1]]
+            worker = list_ref[owner, at + 2]
+            first = used_ref[0, worker]
+            back = used_ref[1, worker]
+            after = first + 3 + 2 * role
+            back_after = back + 3 - 2 * role
+            fits = (after < SEND_ROWS) & (back_after <= BACK_ROWS) & (number < ENTRIES)
+
+            @pl.when(fits)
+            def _():
+                for field in range(3):
+                    out_ref[worker, pl.ds(first + field, 1), :] = pos_ref[field, pl.ds(block, 1), :]
+                entry_ref[0, number] = block
+                entry_ref[1, number] = role
+                entry_ref[2, number] = worker
+                entry_ref[3, number] = back
+
+            @pl.when(fits & (role == 1))
+            def _():
+                out_ref[worker, pl.ds(first + 3, 2), :] = angles_ref[block]
+
+            used_ref[0, worker] = after
+            used_ref[1, worker] = back_after
+            return (number + 1, jnp.where(fits, over, 1))
+
+        def task(turn, state):
+            number, over = state
+            at = TASK_LANE + 4 * turn
+            fits = number < TASKS
+
+            @pl.when(fits)
+            def _():
+                for side in range(2):
+                    source = list_ref[owner, at + 2 * side]
+                    here = source == own
+                    block = block_ref[owner * cap + list_ref[owner, at + 2 * side + 1]]
+                    used = used_ref[2, source]
+                    back = used_ref[3, source]
+                    task_ref[3 * side, number] = source
+                    task_ref[3 * side + 1, number] = jnp.where(here, block, used)
+                    task_ref[3 * side + 2, number] = back
+                    used_ref[2, source] = jnp.where(here, used, used + 3 + 2 * side)
+                    used_ref[3, source] = jnp.where(here, back, back + 3 - 2 * side)
+                task_ref[6, number] = owner
+                task_ref[7, number] = turn
+
+            return (number + 1, jnp.where(fits, over, 1))
+
+        entries, tasks, over = carry
+        over = jnp.maximum(over, list_ref[owner, 2])
+        entries, over = lax.fori_loop(
+            0, jnp.minimum(list_ref[owner, 0], ENTRY_CAP), entry, (entries, over)
+        )
+        tasks, over = lax.fori_loop(
+            0, jnp.minimum(list_ref[owner, 1], TASK_CAP), task, (tasks, over)
+        )
+        return (entries, tasks, over)
+
+    zero = jnp.int32(0)
+    entries, tasks, over = lax.fori_loop(0, devices, from_owner, (zero, zero, zero))
+    entry_ref[4, 0] = jnp.minimum(entries, ENTRIES)
+    task_ref[8, 0] = jnp.minimum(tasks, TASKS)
+    mark = jnp.full((devices, LANES), over.astype(F32), F32)
+    out_ref[:, SEND_ROWS - 1, :] = mark
 
 
 def pack_kernel(slots, rows_per, own_ref, map_ref, pos_ref, angles_ref, nodes_ref, out_ref, ids_ref):
@@ -258,6 +455,152 @@
     lax.fori_loop(0, count, tile, 0)
 
 
+def work_kernel(
+    own_ref,
+    task_ref,
+    in_ref,
+    request_ref,
+    pos_ref,
+    angles_ref,
+    back_ref,
+    slave_out,
+    master_out,
+    slave_ref,
+    master_ref,
+    sin_ref,
+    cos_ref,
+):
+    own = own_ref[0]
+    count = task_ref[8, 0]
+
+    def stage(task, carry):
+        owner = task_ref[6, task]
+        turn = task_ref[7, task]
+        for side, stage_ref in ((0, slave_ref), (1, master_ref)):
+            source = task_ref[3 * side, task]
+            first = task_ref[3 * side + 1, task]
+
+            @pl.when(source == own)
+            def _():
+                for field in range(3):
+                    stage_ref[pl.ds(task * 8 + field, 1), :] = pos_ref[field, pl.ds(first, 1), :]
+                if side == 1:
+                    stage_ref[pl.ds(task * 8 + 3, 2), :] = angles_ref[first]
+
+            @pl.when(source != own)
+            def _():
+                for field in range(3 + 2 * side):
+                    stage_ref[pl.ds(task * 8 + field, 1), :] = in_ref[source, pl.ds(first + field, 1), :]
+
+            stage_ref[pl.ds(task * 8 + 5, 1), :] = request_ref[
+                owner, pl.ds(1 + 2 * turn + side, 1), :
+            ].astype(F32)
+        return carry
+
+    lax.fori_loop(0, count, stage, 0)
+    sines, cosines = sine_cosine(master_ref[...])
+    sin_ref[...] = sines
+    cos_ref[...] = cosines
+
+    def tile(task, carry):
+        base = pl.multiple_of(task * 8, 8)
+        slave = slave_ref[pl.ds(base, 8), :]
+        columns = jnp.transpose(slave)
+        master = master_ref[pl.ds(base, 8), :]
+        sin_az = sin_ref[pl.ds(base + 3, 1), :]
+        sin_pol = sin_ref[pl.ds(base + 4, 1), :]
+        cos_az = cos_ref[pl.ds(base + 3, 1), :]
+        cos_pol = cos_ref[pl.ds(base + 4, 1), :]
+        normal = [cos_az * cos_pol, sin_az * cos_pol, sin_pol]
+        shape = (LANES, LANES)
+        dist = [
+            jnp.broadcast_to(columns[:, k : k + 1], shape) - jnp.broadcast_to(master[k : k + 1], shape)
+            for k in range(3)
+        ]
+        gap = dist[0] * normal[0] + dist[1] * normal[1] + dist[2] * normal[2]
+        tang = dist[0] * dist[0] + dist[1] * dist[1] + dist[2] * dist[2] - gap * gap
+        bend = gap * (-1.0 / PEN_DEPTH)
+        soft = jnp.maximum(bend, 0.0) + jnp.log(1.0 + jnp.exp(-jnp.abs(bend)))
+        press = soft * jnp.exp(-0.5 * tang)
+        press = press * jnp.broadcast_to(columns[:, 5:6], shape)
+        scale = PEN_STIFF * PEN_DEPTH * master[5:6]
+        total = jnp.sum(press, axis=0, keepdims=True) * scale
+        rows = jnp.concatenate([n * scale for n in normal] + [jnp.zeros((5, LANES), F32)], axis=0)
+        push_high, push_rest = split2(rows)
+        both = jnp.concatenate([push_high, push_rest], axis=0)
+        high, rest = split2(press)
+        got = dot_nt(both, high) + dot_nt(both, rest)
+        on_slave = got[0:8] + got[8:16]
+        slave_out[pl.ds(base, 8), :] = on_slave
+        for k in range(3):
+            master_out[pl.ds(base + k, 1), :] = -normal[k] * total
+        source = task_ref[0, task]
+
+        @pl.when(source != own)
+        def _():
+            for k in range(3):
+                back_ref[source, pl.ds(task_ref[2, task] + k, 1), :] = on_slave[k : k + 1]
+
+        source = task_ref[3, task]
+
+        @pl.when(source != own)
+        def _():
+            back_ref[source, pl.ds(task_ref[5, task], 1), :] = total
+
+        return carry
+
+    lax.fori_loop(0, count, tile, 0)
+
+
+def near_kernel(own_ref, task_ref, nodes_ref, slave_ref, master_ref, inner_ref, out_ref):
+    own = own_ref[0]
+
+    def step(task, acc):
+        ids = []
+        forces = []
+        for side, force_ref in ((0, slave_ref), (1, master_ref)):
+            here = task_ref[3 * side, task] == own
+            block = jnp.where(here, task_ref[3 * side + 1, task], 0)
+            ids.append(nodes_ref[pl.ds(block, 1), :])
+            rows = force_ref[pl.ds(pl.multiple_of(task * 8, 8), 8), :]
+            rows = jnp.where(here, rows, 0.0)
+            forces.append([rows[k : k + 1] for k in range(3)])
+        return acc + scatter_terms(ids, forces)
+
+    acc = lax.fori_loop(0, task_ref[8, 0], step, jnp.zeros((6 * GROUP, LANES), F32))
+    out_ref[...] = inner_ref[...] + fold_terms(acc)
+
+
+def far_kernel(
+    chunks, entry_ref, back_ref, nodes_ref, normal_ref, near_ref, faces_ref, out_ref, low_ref, high_ref
+):
+    count = entry_ref[4, 0]
+
+    def step(turn, acc):
+        ids = []
+        forces = []
+        for k in range(2):
+            valid = 2 * turn + k < count
+            number = jnp.where(valid, 2 * turn + k, 0)
+            block = entry_ref[0, number]
+            role = entry_ref[1, number]
+            worker = entry_ref[2, number]
+            first = entry_ref[3, number]
+            ids.append(nodes_ref[pl.ds(block, 1), :])
+            total = back_ref[worker, pl.ds(first, 1), :]
+            rows = []
+            for field in range(3):
+                row = back_ref[worker, pl.ds(jnp.minimum(first + field, BACK_ROWS - 1), 1), :]
+                row = jnp.where(role == 1, -normal_ref[field, pl.ds(block, 1), :] * total, row)
+                rows.append(jnp.where(valid, row, 0.0))
+            forces.append(rows)
+        return acc + scatter_terms(ids, forces)
+
+    acc = lax.fori_loop(0, (count + 1) // 2, step, jnp.zeros((6 * GROUP, LANES), F32))
+    out_ref[...] = near_ref[...] + fold_terms(acc)
+    send_faces(out_ref, chunks, faces_ref, 0, low_ref, high_ref)
+
+
 def element_kernel(conn_ref, coords_ref, disp_ref, modulus_ref, out_ref, order_ref):
     chunks = coords_ref.shape[1] // LANES
     groups = conn_ref.shape[1] // LANES
@@ -420,17 +763,15 @@
             )
 
 
-def call(kernel, outs, in_smem, args, scratch=()):
-    specs = [
-        pl.BlockSpec(memory_space=pltpu.SMEM if i in in_smem else pltpu.VMEM)
-        for i in range(len(args))
-    ]
-    out_shape = [jax.ShapeDtypeStruct(shape, dtype) for shape, dtype in outs]
+def call(kernel, outs, in_smem, args, scratch=(), out_smem=()):
+    def spec(smem):
+        return pl.BlockSpec(memory_space=pltpu.SMEM if smem else pltpu.VMEM)
+
     return pl.pallas_call(
         kernel,
-        out_shape=out_shape,
-        in_specs=specs,
-        out_specs=[pl.BlockSpec(memory_space=pltpu.VMEM) for _ in outs],
+        out_shape=[jax.ShapeDtypeStruct(shape, dtype) for shape, dtype in outs],
+        in_specs=[spec(i in in_smem) for i in range(len(args))],
+        out_specs=[spec(i in out_smem) for i in range(len(outs))],
         scratch_shapes=list(scratch),
         compiler_params=pltpu.CompilerParams(vmem_limit_bytes=VMEM_LIMIT),
     )(*args)
@@ -476,22 +817,29 @@
     total_shape = ((3 * GROUP, LANES), F32)
     face_shape = ((face_rows, LANES), F32)
 
-    [index] = call(
-        functools.partial(routing_kernel, rows_per),
-        [((4, pairs), jnp.int32)],
+    def to_all(values):
+        return lax.all_to_all(values, axes, split_axis=0, concat_axis=0, tiled=True)
+
+    [request] = call(
+        functools.partial(request_kernel, rows_per),
+        [((devices, REQUEST_ROWS, LANES), jnp.int32)],
         (0, 1),
-        (own, pair_count, owners, pair_blocks),
-    )
-    [pos] = call(
-        segment_kernel, [((3, per_dev, LANES), F32)], (), (displacement, surf_nodes, surf_ref)
-    )
-    outbound, ids = call(
-        functools.partial(pack_kernel, slots, rows_per),
-        [((devices, 5 * slots, LANES), F32), ((devices * slots, LANES), jnp.int32)],
+        (own, pair_count, owners, pair_blocks, pair_masks),
+    )
+    asked = to_all(request)
+    own_owners = lax.dynamic_slice_in_dim(owner_map, own[0] * per_dev, per_dev)
+    pos, normals, block_of = call(
+        functools.partial(segment_kernel, slots),
+        [
+            ((3, per_dev, LANES), F32),
+            ((3, per_dev, LANES), F32),
+            ((devices * slots,), jnp.int32),
+        ],
         (0,),
-        (own, owners, pos, surf_angles, surf_nodes),
-    )
-    inbound = lax.all_to_all(outbound, axes, split_axis=0, concat_axis=0, tiled=True)
+        (own_owners, displacement, surf_nodes, surf_ref, surf_angles),
+        [pltpu.SMEM((devices,), jnp.int32)],
+        (2,),
+    )
     [internal] = call(
         element_kernel,
         [total_shape],
@@ -499,20 +847,75 @@
         (connectivity, coords, displacement, modulus.reshape(-1, LANES)),
         [pltpu.VMEM((connectivity.shape[1] // LANES * 8, LANES), jnp.int32)],
     )
-    [forces] = call(
-        functools.partial(pair_kernel, slots),
-        [((devices, 3 * slots, LANES), F32)],
-        (0, 1),
-        (index, pair_count, inbound, pair_masks),
-        [pltpu.VMEM((pairs * 8, LANES), F32)] * 4,
-    )
-    returned = lax.all_to_all(forces, axes, split_axis=0, concat_axis=0, tiled=True)
-    total, low, high = call(
-        functools.partial(assemble_kernel, slots, chunks),
-        [total_shape, face_shape, face_shape],
-        (),
-        (returned, ids, internal, faces),
-    )
+    outbound, entries, tasks = call(
+        functools.partial(plan_kernel, slots),
+        [
+            ((devices, SEND_ROWS, LANES), F32),
+            ((8, ENTRIES), jnp.int32),
+            ((16, TASKS), jnp.int32),
+        ],
+        (0, 1, 2),
+        (own, asked[:, 0, :], block_of, pos, surf_angles),
+        [pltpu.SMEM((4, devices), jnp.int32)],
+        (1, 2),
+    )
+    inbound = to_all(outbound)
+    over = jnp.max(inbound[:, SEND_ROWS - 1, 0]) > 0.0
+
+    def by_tasks():
+        back, on_slave, on_master = call(
+            work_kernel,
+            [
+                ((devices, BACK_ROWS, LANES), F32),
+                ((TASKS * 8, LANES), F32),
+                ((TASKS * 8, LANES), F32),
+            ],
+            (0, 1),
+            (own, tasks, inbound, asked, pos, surf_angles),
+            [pltpu.VMEM((TASKS * 8, LANES), F32)] * 4,
+        )
+        returned = to_all(back)
+        [near] = call(
+            near_kernel,
+            [total_shape],
+            (0, 1),
+            (own, tasks, surf_nodes, on_slave, on_master, internal),
+        )
+        return call(
+            functools.partial(far_kernel, chunks),
+            [total_shape, face_shape, face_shape],
+            (0,),
+            (entries, returned, surf_nodes, normals, near, faces),
+        )
+
+    def by_owners():
+        [index] = call(
+            functools.partial(routing_kernel, rows_per),
+            [((4, pairs), jnp.int32)],
+            (0, 1),
+            (own, pair_count, owners, pair_blocks),
+        )
+        outbound, ids = call(
+            functools.partial(pack_kernel, slots, rows_per),
+            [((devices, 5 * slots, LANES), F32), ((devices * slots, LANES), jnp.int32)],
+            (0,),
+            (own, owners, pos, surf_angles, surf_nodes),
+        )
+        [forces] = call(
+            functools.partial(pair_kernel, slots),
+            [((devices, 3 * slots, LANES), F32)],
+            (0, 1),
+            (index, pair_count, to_all(outbound), pair_masks),
+            [pltpu.VMEM((pairs * 8, LANES), F32)] * 4,
+        )
+        return call(
+            functools.partial(assemble_kernel, slots, chunks),
+            [total_shape, face_shape, face_shape],
+            (),
+            (to_all(forces), ids, internal, faces),
+        )
+
+    total, low, high = lax.cond(over, by_owners, by_tasks)
     from_low, from_high = exchange(low, high, "gx")
     total, low, high = call(
         functools.partial(middle_kernel, chunks),

time: 126 us -> 90.7 us (0.72)
  waiting for transfers between devices: 55.3 us -> 26.3 us
  starting transfers between devices: 35.8 us -> 29.8 us
  Pallas kernels: 30.7 us -> 28.9 us
    all_to_all x2 -> x3, waiting for transfers between devices: 48.4 us -> 19.4 us  [to_all(): return lax.all_to_all(values, axes, split_axis=0, concat_axis=0, tiled=True)]
    all_to_all x2 -> x3, starting transfers between devices: 25.3 us -> 19.8 us  [to_all(): return lax.all_to_all(values, axes, split_axis=0, concat_axis=0, tiled=True)]
    pallas_call x8 -> x9, Pallas kernels: 30.7 us -> 28.9 us  [call(): pl.pallas_call(kernel, out_shape=[jax.ShapeDtypeStruct(shape, dtype) for...]
    unnamed x29 -> x25, local copies, waits for them, and re-layouts: 3 us -> 1.33 us
  transfers between devices with their start and end apart: 6 -> 7, of which waited for: 4 -> 5; matrix products, arithmetic and copies ran while one was open for 0% -> 2% of each run, Pallas kernels for 2% -> 11%
where the time goes in v1:
time: 90.7 us; the launch traced here: 89.4 us
  starting transfers between devices  29.8 us (33%)
  Pallas kernels  28.9 us (32%)
  waiting for transfers between devices  26.3 us (29%)
  local copies, waits for them, and re-layouts  2.11 us (2%)
  between operations  1.6 us (2%)
    pallas_call x9, Pallas kernels, call(): pl.pallas_call(kernel, out_shape=[jax.ShapeDtypeStruct(shape, dtype) for...  28.9 us
    all_to_all x3, starting transfers between devices, to_all(): return lax.all_to_all(values, axes, split_axis=0, concat_axis=0, tiled=True)  19.8 us
    all_to_all x3, waiting for transfers between devices, to_all(): return lax.all_to_all(values, axes, split_axis=0, concat_axis=0, tiled=True)  19.4 us
    ppermute x2, waiting for transfers between devices, exchange(): lax.ppermute(low, axis, backward)  6.93 us
    ppermute x2, starting transfers between devices, exchange(): lax.ppermute(high, axis, forward)  6.79 us
    ppermute x2, starting transfers between devices, exchange(): lax.ppermute(low, axis, backward)  3.21 us
  transfers between devices with their start and end apart: 7, of which 5 were waited for; matrix products, arithmetic and copies ran while one was open for 2% of the time, Pallas kernels for 11%

profile of v1, /device:TPU:3, one launch (start us, length us, event | category | flops | bytes accessed | tf_op | source)
XLA Modules:
  0.0 89.4 jit_solution(10132760450767246305)
XLA Ops:
  0.7 2.3 %shard_map.136 = s32[32,16,128]{2,1,0:T(8,128)} custom-call(s32[1]{0:T(128)} %bitcast.own_ref, s32[1]{0:T(128)S(6)} %copy.27.count_ref, s32[64,128]{1,0:T(8,128)} %bitcast.10, s32[2,64]{1,0:T(2,128)} %pairs_ref.1, s32[2,64,128]{2,1,0:T(8,128)} %masks_ref.1), custom_call_target="tpu_custom_call" | custom-call | tf_op jit(solution)/shard_map/pallas_call | solution.py:770
  3.0 6.4 %all-to-all-start.3 = ((s32[32,16,128]{2,1,0:T(8,128)}), s32[32,16,128]{2,1,0:T(8,128)S(1)}, u32[]{:S(2)}, u32[]{:S(2)}) async-start(s32[32,16,128]{2,1,0:T(8,128)} %shard_map.136), calls=%async_computation.3 | async-start | bytes 524288 | tf_op jit(solution)/shard_map/all_to_all | solution.py:821
  9.5 0.8 dynamic_slice.3.owners_ref
  10.3 1.3 %copy.19.ref_ref = f32[256,3,128]{2,1,0:T(4,128)S(1)} copy(f32[256,3,128]{2,0,1:T(8,128)} %param.24) | data formatting | bytes 786432 | tf_op args[8]
  11.6 4.6 %shard_map.137 = (f32[3,256,128]{2,1,0:T(8,128)S(1)}, f32[3,256,128]{2,1,0:T(8,128)S(1)}, s32[512]{0:T(512)S(1)}) custom-call(s32[256]{0:T(256)S(1)} %dynamic_slice.3.owners_ref, f32[3,1408]{1,0:T(4,128)S(1)} %copy-done, s32[256,128]{1,0:T(8,128)S(1)} %copy-done.7, f32[256,3,128]{2,1,0:T(4,128)S(1)} %copy.19.ref_ref, f32[256,2,128]{2,1,0:T(2,128)S(1)} %copy-done.6), custom_call_target="tpu_custom_call" | custom-call | tf_op jit(solution)/shard_map/pallas_call | solution.py:770
  16.2 2.7 %all-to-all-done.3 = s32[32,16,128]{2,1,0:T(8,128)S(1)} async-done(((s32[32,16,128]{2,1,0:T(8,128)}), s32[32,16,128]{2,1,0:T(8,128)S(1)}, u32[]{:S(2)}, u32[]{:S(2)}) %all-to-all-start.3) | async-done | bytes 262176 | tf_op jit(solution)/shard_map/all_to_all | solution.py:821
  19.0 4.0 %shard_map.138 = (f32[32,32,128]{2,1,0:T(8,128)}, s32[8,160]{1,0:T(8,128)S(1)}, s32[16,64]{1,0:T(8,128)S(1)}) custom-call(s32[1]{0:T(128)} %bitcast.own_ref, s32[32,128]{1,0:T(8,128)S(1)} %bitcast.7, s32[512]{0:T(512)S(1)} %get-tuple-element.85.block_ref, f32[3,256,128]{2,1,0:T(8,128)S(1)} %get-tuple-element.86.pos_ref, f32[256,2,128]{2,1,0:T(2,128)S(1)} %copy-done.6), custom_call_target="tpu_custom_call" | custom-call | tf_op jit(solution)/shard_map/pallas_call | solution.py:770
  23.0 5.2 %all-to-all-start.4 = ((f32[32,32,128]{2,1,0:T(8,128)}), f32[32,32,128]{2,1,0:T(8,128)S(1)}, u32[]{:S(2)}, u32[]{:S(2)}) async-start(f32[32,32,128]{2,1,0:T(8,128)} %get-tuple-element.87), calls=%async_computation.4 | async-start | bytes 1048576 | tf_op jit(solution)/shard_map/all_to_all | solution.py:821
  28.3 1.9 %shard_map.139 = f32[48,128]{1,0:T(8,128)S(1)} custom-call(s32[8,1024]{1,0:T(8,128)S(1)} %copy-done.1, f32[3,1408]{1,0:T(4,128)S(1)} %copy-done.2, f32[3,1408]{1,0:T(4,128)S(1)} %copy-done, f32[8,128]{1,0:T(8,128)S(1)} %bitcast.9), custom_call_target="tpu_custom_call" | custom-call | tf_op jit(solution)/shard_map/pallas_call | solution.py:770
  30.2 13.1 %all-to-all-done.4 = f32[32,32,128]{2,1,0:T(8,128)S(1)} async-done(((f32[32,32,128]{2,1,0:T(8,128)}), f32[32,32,128]{2,1,0:T(8,128)S(1)}, u32[]{:S(2)}, u32[]{:S(2)}) %all-to-all-start.4) | async-done | bytes 524320 | tf_op jit(solution)/shard_map/all_to_all | solution.py:821
  43.3 0.7 slice_reduce_fusion
  44.7 26.6 %conditional.1 = ((f32[48,128]{1,0:T(8,128)S(1)}, f32[8,128]{1,0:T(8,128)S(1)}, f32[8,128]{1,0:T(8,128)S(1)})) conditional(s32[]{:T(128)} %convert_element_type.3, (s32[1]{0:T(128)}, s32[16,64]{1,0:T(8,128)S(1)}, f32[32,32,128]{2,1,0:T(8,128)S(1)}, s32[32,16,128]{2,1,0:T(8,128)S(1)}, f32[3,256,128]{2,1,0:T(8,128)S(1)}, ...), branch_computations={%region_1.2_spmd, %region_2.3_spmd} | conditional | bytes 5505064 | solution.py:918
  44.7 8.9 %branch_0_fun.3 = (f32[32,8,128]{2,1,0:T(8,128)}, f32[512,128]{1,0:T(8,128)S(1)}, f32[512,128]{1,0:T(8,128)S(1)}) custom-call(s32[1]{0:T(128)} %get-tuple-element.48.own_ref, s32[16,64]{1,0:T(8,128)S(1)} %get-tuple-element.49.task_ref, f32[32,32,128]{2,1,0:T(8,128)S(1)} %get-tuple-element.50.in_ref, s32[32,16,128]{2,1,0:T(8,128)S(1)} %get-tuple-element.51.request_ref, ...), custom_call_target="tpu_custom_call" | custom-call | tf_op jit(solution)/shard_map/cond/branch_0_fun/pallas_call | solution.py:770
  53.5 8.2 %all-to-all-start = ((f32[32,8,128]{2,1,0:T(8,128)}), f32[32,8,128]{2,1,0:T(8,128)S(1)}, u32[]{:S(2)}, u32[]{:S(2)}) async-start(f32[32,8,128]{2,1,0:T(8,128)} %get-tuple-element.54), calls=%async_computation | async-start | bytes 262144 | tf_op jit(solution)/shard_map/cond/branch_0_fun/all_to_all | solution.py:821
  61.7 3.5 %branch_0_fun.4.near_ref = f32[48,128]{1,0:T(8,128)S(1)} custom-call(s32[1]{0:T(128)} %get-tuple-element.48.own_ref, s32[16,64]{1,0:T(8,128)S(1)} %get-tuple-element.49.task_ref, s32[256,128]{1,0:T(8,128)S(1)} %get-tuple-element.55.nodes_ref, f32[512,128]{1,0:T(8,128)S(1)} %get-tuple-element.57.slave_ref, f32[512,128]{1,0:T(8,128)S(1)} %get-tuple-element.58.master_ref, ...), custom_call_target="tpu_custom_call" | custom-call | tf_op jit(solution)/shard_map/cond/branch_0_fun/pallas_call | solution.py:770
  65.2 3.5 %all-to-all-done.back_ref = f32[32,8,128]{2,1,0:T(8,128)S(1)} async-done(((f32[32,8,128]{2,1,0:T(8,128)}), f32[32,8,128]{2,1,0:T(8,128)S(1)}, u32[]{:S(2)}, u32[]{:S(2)}) %all-to-all-start) | async-done | bytes 131104 | tf_op jit(solution)/shard_map/cond/branch_0_fun/all_to_all | solution.py:821
  68.7 2.5 %branch_0_fun.5 = (f32[48,128]{1,0:T(8,128)S(1)}, f32[8,128]{1,0:T(8,128)S(1)}, f32[8,128]{1,0:T(8,128)S(1)}) custom-call(s32[8,160]{1,0:T(8,128)S(1)} %get-tuple-element.47.entry_ref, f32[32,8,128]{2,1,0:T(8,128)S(1)} %all-to-all-done.back_ref, s32[256,128]{1,0:T(8,128)S(1)} %get-tuple-element.55.nodes_ref, ...), custom_call_target="tpu_custom_call" | custom-call | tf_op jit(solution)/shard_map/cond/branch_0_fun/pallas_call | solution.py:770
  71.2 1.8 %collective-permute-start = (f32[8,128]{1,0:T(8,128)S(1)}, f32[8,128]{1,0:T(8,128)S(1)}, u32[]{:S(2)}, u32[]{:S(2)}) collective-permute-start(f32[8,128]{1,0:T(8,128)S(1)} %get-tuple-element.92), channel_id=1, source_target_pairs={{0,8},{8,16},{16,24},{1,9},{9,17},{17,25},{2,10},{10,18},{18,26},{... | collective-permute-start | bytes 12296 | tf_op jit(solution)/shard_map/ppermute | solution.py:784
  73.0 1.3 %collective-permute-start.1 = (f32[8,128]{1,0:T(8,128)S(1)}, f32[8,128]{1,0:T(8,128)S(1)}, u32[]{:S(2)}, u32[]{:S(2)}) collective-permute-start(f32[8,128]{1,0:T(8,128)S(1)} %get-tuple-element.93), channel_id=1, source_target_pairs={{8,0},{16,8},{24,16},{9,1},{17,9},{25,17},{10,2},{18,10},{26,18},{... | collective-permute-start | bytes 12296 | tf_op jit(solution)/shard_map/ppermute | solution.py:784
  74.3 3.0 %collective-permute-done.1.from_high = f32[8,128]{1,0:T(8,128)S(1)} collective-permute-done((f32[8,128]{1,0:T(8,128)S(1)}, f32[8,128]{1,0:T(8,128)S(1)}, u32[]{:S(2)}, u32[]{:S(2)}) %collective-permute-start.1) | collective-permute-done | bytes 4128 | tf_op jit(solution)/shard_map/ppermute | solution.py:784
  77.7 5.0 %collective-permute-start.2 = (f32[8,128]{1,0:T(8,128)S(1)}, f32[8,128]{1,0:T(8,128)S(1)}, u32[]{:S(2)}, u32[]{:S(2)}) collective-permute-start(f32[8,128]{1,0:T(8,128)S(1)} %get-tuple-element.95), channel_id=1, source_target_pairs={{0,1},{1,2},{2,3},{3,4},{4,5},{5,6},{6,7},{8,9},{9,10},{10,11},{11... | collective-permute-start | bytes 12296 | tf_op jit(solution)/shard_map/ppermute | solution.py:784
  82.7 1.9 %collective-permute-start.3 = (f32[8,128]{1,0:T(8,128)S(1)}, f32[8,128]{1,0:T(8,128)S(1)}, u32[]{:S(2)}, u32[]{:S(2)}) collective-permute-start(f32[8,128]{1,0:T(8,128)S(1)} %get-tuple-element.96), channel_id=1, source_target_pairs={{1,0},{2,1},{3,2},{4,3},{5,4},{6,5},{7,6},{9,8},{10,9},{11,10},{12... | collective-permute-start | bytes 12296 | tf_op jit(solution)/shard_map/ppermute | solution.py:784
  84.7 3.9 %collective-permute-done.3.from_high = f32[8,128]{1,0:T(8,128)S(1)} collective-permute-done((f32[8,128]{1,0:T(8,128)S(1)}, f32[8,128]{1,0:T(8,128)S(1)}, u32[]{:S(2)}, u32[]{:S(2)}) %collective-permute-start.3) | collective-permute-done | bytes 4128 | tf_op jit(solution)/shard_map/ppermute | solution.py:784
  88.6 0.8 shard_map.141
  (29 shorter events, 0.4 us)
Async XLA Ops:
  0.0 11.5 %copy-start = (f32[3,1408]{1,0:T(4,128)S(1)}, f32[3,1408]{1,0:T(4,128)}, u32[]{:S(2)}) copy-start(f32[3,1408]{1,0:T(4,128)} %disp_ref.3) | copy-start | bytes 50692
  0.0 11.5 %copy-start.7 = (s32[256,128]{1,0:T(8,128)S(1)}, s32[256,128]{1,0:T(8,128)}, u32[]{:S(2)}) copy-start(s32[256,128]{1,0:T(8,128)} %nodes_ref.1) | copy-start | bytes 393220
  0.0 11.5 %copy-start.6 = (f32[256,2,128]{2,1,0:T(2,128)S(1)}, f32[256,2,128]{2,1,0:T(2,128)}, u32[]{:S(2)}) copy-start(f32[256,2,128]{2,1,0:T(2,128)} %angles_ref.3) | copy-start | bytes 786436
  3.0 16.0 %all-to-all-start.3 = ((s32[32,16,128]{2,1,0:T(8,128)}), s32[32,16,128]{2,1,0:T(8,128)S(1)}, u32[]{:S(2)}, u32[]{:S(2)}) async-start(s32[32,16,128]{2,1,0:T(8,128)} %shard_map.136), calls=%async_computation.3 | async-start | bytes 524288 | tf_op jit(solution)/shard_map/all_to_all | solution.py:821
  11.6 16.7 %copy-start.11 = (s32[4,153]{1,0:T(4,128)S(1)}, s32[4,153]{1,0:T(4,128)}, u32[]{:S(2)}) copy-start(s32[4,153]{1,0:T(4,128)} %param.17) | copy-start | bytes 7348
  11.6 16.7 %copy-start.1 = (s32[8,1024]{1,0:T(8,128)S(1)}, s32[8,1024]{1,0:T(8,128)}, u32[]{:S(2)}) copy-start(s32[8,1024]{1,0:T(8,128)} %conn_ref.1) | copy-start | bytes 98308
  11.6 16.7 %copy-start.2 = (f32[3,1408]{1,0:T(4,128)S(1)}, f32[3,1408]{1,0:T(4,128)}, u32[]{:S(2)}) copy-start(f32[3,1408]{1,0:T(4,128)} %coords_ref.1) | copy-start | bytes 50692
  11.6 16.7 %copy-start.5 = (f32[1024]{0:T(1024)S(1)}, f32[1024]{0:T(1024)}, u32[]{:S(2)}) copy-start(f32[1024]{0:T(1024)} %param.22) | copy-start | bytes 12292
  11.6 33.0 %copy-start.8 = (s32[8192]{0:T(1024)S(1)}, s32[8192]{0:T(1024)}, u32[]{:S(2)}) copy-start(s32[8192]{0:T(1024)} %param.26) | copy-start | bytes 98308
  11.6 33.0 %copy-start.9 = (s32[2,64,128]{2,1,0:T(8,128)S(1)}, s32[2,64,128]{2,1,0:T(8,128)}, u32[]{:S(2)}) copy-start(s32[2,64,128]{2,1,0:T(8,128)} %masks_ref.1) | copy-start | bytes 196612
  11.6 33.0 %copy-start.10 = (s32[2,64]{1,0:T(2,128)S(1)}, s32[2,64]{1,0:T(2,128)}, u32[]{:S(2)}) copy-start(s32[2,64]{1,0:T(2,128)} %pairs_ref.1) | copy-start | bytes 1540
  23.0 20.3 %all-to-all-start.4 = ((f32[32,32,128]{2,1,0:T(8,128)}), f32[32,32,128]{2,1,0:T(8,128)S(1)}, u32[]{:S(2)}, u32[]{:S(2)}) async-start(f32[32,32,128]{2,1,0:T(8,128)} %get-tuple-element.87), calls=%async_computation.4 | async-start | bytes 1048576 | tf_op jit(solution)/shard_map/all_to_all | solution.py:821
  44.6 43.9 %copy-start.3 = (f32[3,1408]{1,0:T(4,128)S(1)}, f32[3,1408]{1,0:T(4,128)}, u32[]{:S(2)}) copy-start(f32[3,1408]{1,0:T(4,128)} %velocity_ref.1) | copy-start | bytes 50692
  44.6 43.9 %copy-start.4 = (f32[1408]{0:T(1024)S(1)}, f32[1408]{0:T(1024)}, u32[]{:S(2)}) copy-start(f32[1408]{0:T(1024)} %param.21) | copy-start | bytes 16900
  53.5 15.2 %all-to-all-start = ((f32[32,8,128]{2,1,0:T(8,128)}), f32[32,8,128]{2,1,0:T(8,128)S(1)}, u32[]{:S(2)}, u32[]{:S(2)}) async-start(f32[32,8,128]{2,1,0:T(8,128)} %get-tuple-element.54), calls=%async_computation | async-start | bytes 262144 | tf_op jit(solution)/shard_map/cond/branch_0_fun/all_to_all | solution.py:821
  71.2 3.1 %collective-permute-start = (f32[8,128]{1,0:T(8,128)S(1)}, f32[8,128]{1,0:T(8,128)S(1)}, u32[]{:S(2)}, u32[]{:S(2)}) collective-permute-start(f32[8,128]{1,0:T(8,128)S(1)} %get-tuple-element.92), channel_id=1, source_target_pairs={{0,8},{8,16},{16,24},{1,9},{9,17},{17,25},{2,10},{10,18},{18,26},{... | collective-permute-start | bytes 12296 | tf_op jit(solution)/shard_map/ppermute | solution.py:784
  73.0 4.4 %collective-permute-start.1 = (f32[8,128]{1,0:T(8,128)S(1)}, f32[8,128]{1,0:T(8,128)S(1)}, u32[]{:S(2)}, u32[]{:S(2)}) collective-permute-start(f32[8,128]{1,0:T(8,128)S(1)} %get-tuple-element.93), channel_id=1, source_target_pairs={{8,0},{16,8},{24,16},{9,1},{17,9},{25,17},{10,2},{18,10},{26,18},{... | collective-permute-start | bytes 12296 | tf_op jit(solution)/shard_map/ppermute | solution.py:784
  77.7 7.0 %collective-permute-start.2 = (f32[8,128]{1,0:T(8,128)S(1)}, f32[8,128]{1,0:T(8,128)S(1)}, u32[]{:S(2)}, u32[]{:S(2)}) collective-permute-start(f32[8,128]{1,0:T(8,128)S(1)} %get-tuple-element.95), channel_id=1, source_target_pairs={{0,1},{1,2},{2,3},{3,4},{4,5},{5,6},{6,7},{8,9},{9,10},{10,11},{11... | collective-permute-start | bytes 12296 | tf_op jit(solution)/shard_map/ppermute | solution.py:784
  82.7 5.8 %collective-permute-start.3 = (f32[8,128]{1,0:T(8,128)S(1)}, f32[8,128]{1,0:T(8,128)S(1)}, u32[]{:S(2)}, u32[]{:S(2)}) collective-permute-start(f32[8,128]{1,0:T(8,128)S(1)} %get-tuple-element.96), channel_id=1, source_target_pairs={{1,0},{2,1},{3,2},{4,3},{5,4},{6,5},{7,6},{9,8},{10,9},{11,10},{12... | collective-permute-start | bytes 12296 | tf_op jit(solution)/shard_map/ppermute | solution.py:784

commit v2 on v1

--- a/solution.py
+++ b/solution.py
@@ -41,6 +41,7 @@
 BACK_ROWS = 8
 ENTRIES = 160
 TASKS = 64
+TASK_STEP = 8
 
 
 def iota(shape, dim):
@@ -465,10 +466,11 @@
     back_ref,
     slave_out,
     master_out,
-    slave_ref,
-    master_ref,
-    sin_ref,
-    cos_ref,
+    field_ref,
+    left_ref,
+    gap_ref,
+    far_ref,
+    push_ref,
 ):
     own = own_ref[0]
     count = task_ref[8, 0]
@@ -476,80 +478,114 @@
     def stage(task, carry):
         owner = task_ref[6, task]
         turn = task_ref[7, task]
-        for side, stage_ref in ((0, slave_ref), (1, master_ref)):
+        for side in range(2):
             source = task_ref[3 * side, task]
             first = task_ref[3 * side + 1, task]
+            base = 4 * side
 
             @pl.when(source == own)
             def _():
                 for field in range(3):
-                    stage_ref[pl.ds(task * 8 + field, 1), :] = pos_ref[field, pl.ds(first, 1), :]
+                    field_ref[base + field, pl.ds(task, 1), :] = pos_ref[field, pl.ds(first, 1), :]
                 if side == 1:
-                    stage_ref[pl.ds(task * 8 + 3, 2), :] = angles_ref[first]
+                    both = angles_ref[first]
+                    field_ref[8, pl.ds(task, 1), :] = both[0:1]
+                    field_ref[9, pl.ds(task, 1), :] = both[1:2]
 
             @pl.when(source != own)
             def _():
-                for field in range(3 + 2 * side):
-                    stage_ref[pl.ds(task * 8 + field, 1), :] = in_ref[source, pl.ds(first + field, 1), :]
-
-            stage_ref[pl.ds(task * 8 + 5, 1), :] = request_ref[
+                for field in range(3):
+                    field_ref[base + field, pl.ds(task, 1), :] = in_ref[
+                        source, pl.ds(first + field, 1), :
+                    ]
+                if side == 1:
+                    for field in range(2):
+                        field_ref[8 + field, pl.ds(task, 1), :] = in_ref[
+                            source, pl.ds(first + 3 + field, 1), :
+                        ]
+
+            field_ref[base + 3, pl.ds(task, 1), :] = request_ref[
                 owner, pl.ds(1 + 2 * turn + side, 1), :
             ].astype(F32)
         return carry
 
     lax.fori_loop(0, count, stage, 0)
-    sines, cosines = sine_cosine(master_ref[...])
-    sin_ref[...] = sines
-    cos_ref[...] = cosines
-
-    def tile(task, carry):
-        base = pl.multiple_of(task * 8, 8)
-        slave = slave_ref[pl.ds(base, 8), :]
-        columns = jnp.transpose(slave)
-        master = master_ref[pl.ds(base, 8), :]
-        sin_az = sin_ref[pl.ds(base + 3, 1), :]
-        sin_pol = sin_ref[pl.ds(base + 4, 1), :]
-        cos_az = cos_ref[pl.ds(base + 3, 1), :]
-        cos_pol = cos_ref[pl.ds(base + 4, 1), :]
-        normal = [cos_az * cos_pol, sin_az * cos_pol, sin_pol]
-        shape = (LANES, LANES)
-        dist = [
-            jnp.broadcast_to(columns[:, k : k + 1], shape) - jnp.broadcast_to(master[k : k + 1], shape)
-            for k in range(3)
-        ]
-        gap = dist[0] * normal[0] + dist[1] * normal[1] + dist[2] * normal[2]
-        tang = dist[0] * dist[0] + dist[1] * dist[1] + dist[2] * dist[2] - gap * gap
-        bend = gap * (-1.0 / PEN_DEPTH)
-        soft = jnp.maximum(bend, 0.0) + jnp.log(1.0 + jnp.exp(-jnp.abs(bend)))
-        press = soft * jnp.exp(-0.5 * tang)
-        press = press * jnp.broadcast_to(columns[:, 5:6], shape)
-        scale = PEN_STIFF * PEN_DEPTH * master[5:6]
-        total = jnp.sum(press, axis=0, keepdims=True) * scale
-        rows = jnp.concatenate([n * scale for n in normal] + [jnp.zeros((5, LANES), F32)], axis=0)
-        push_high, push_rest = split2(rows)
-        both = jnp.concatenate([push_high, push_rest], axis=0)
-        high, rest = split2(press)
-        got = dot_nt(both, high) + dot_nt(both, rest)
-        on_slave = got[0:8] + got[8:16]
-        slave_out[pl.ds(base, 8), :] = on_slave
-        for k in range(3):
-            master_out[pl.ds(base + k, 1), :] = -normal[k] * total
-        source = task_ref[0, task]
-
-        @pl.when(source != own)
-        def _():
-            for k in range(3):
-                back_ref[source, pl.ds(task_ref[2, task] + k, 1), :] = on_slave[k : k + 1]
-
-        source = task_ref[3, task]
-
-        @pl.when(source != own)
-        def _():
-            back_ref[source, pl.ds(task_ref[5, task], 1), :] = total
+    size = field_ref.shape[1]
+    slave = [field_ref[k] for k in range(3)]
+    master = [field_ref[4 + k] for k in range(3)]
+    sin_az, cos_az = sine_cosine(field_ref[8])
+    sin_pol, cos_pol = sine_cosine(field_ref[9])
+    normal = [cos_az * cos_pol, sin_az * cos_pol, sin_pol]
+
+    def inner(a, b):
+        return a[0] * b[0] + a[1] * b[1] + a[2] * b[2]
+
+    zero = jnp.zeros_like(sin_pol)
+    one = zero + 1.0
+    slope = -1.0 / PEN_DEPTH
+    hidden = 30000.0
+    slave_bias = -0.5 * inner(slave, slave) - hidden * (1.0 - field_ref[3])
+    master_bias = -0.5 * inner(master, master) - hidden * (1.0 - field_ref[7])
+    stacks = (
+        (left_ref, slave + [one, slave_bias]),
+        (gap_ref, [slope * n for n in normal] + [-slope * inner(normal, master), zero]),
+        (far_ref, master + [master_bias, one]),
+        (push_ref, [PEN_STIFF * PEN_DEPTH * n for n in normal] + [zero, zero]),
+    )
+    for ref, rows in stacks:
+        for row, value in enumerate(rows + [zero] * 3):
+            parts = split3(value)
+            for part in range(ref.shape[0]):
+                ref[part, pl.ds(row, size, stride=8), :] = parts[part].astype(F32)
+
+    def tile(step, carry):
+        tasks = [TASK_STEP * step + k for k in range(TASK_STEP)]
+        bases = [pl.multiple_of(task * 8, 8) for task in tasks]
+        fields = []
+        for base in bases:
+            high, mid, low = [left_ref[p, pl.ds(base, 8), :] for p in range(3)]
+            left = jnp.concatenate([high, high, mid, mid, high, low], axis=0).astype(BF16)
+            sides = []
+            for ref in (gap_ref, far_ref):
+                high, mid, low = [ref[p, pl.ds(base, 8), :] for p in range(3)]
+                sides.append(jnp.concatenate([high, mid, high, mid, low, high], axis=0))
+            fields.append(dot_tn(left, jnp.concatenate(sides, axis=1).astype(BF16)))
+        presses = []
+        for field in fields:
+            bend = field[:, :LANES]
+            power = field[:, LANES:] + bend * bend * (0.5 * PEN_DEPTH * PEN_DEPTH)
+            soft = jnp.maximum(bend, 0.0) + jnp.log(1.0 + jnp.exp(-jnp.abs(bend)))
+            presses.append(soft * jnp.exp(power))
+        results = []
+        for base, press in zip(bases, presses):
+            push = jnp.concatenate([push_ref[p, pl.ds(base, 8), :] for p in range(2)], axis=0)
+            push = push.astype(BF16)
+            got = dot_nt(
+                jnp.concatenate([push, push], axis=1), jnp.concatenate(split2(press), axis=1)
+            )
+            total = jnp.sum(press, axis=0, keepdims=True)
+            results.append((got[0:8] + got[8:16], total * (PEN_STIFF * PEN_DEPTH)))
+        for task, base, (on_slave, total) in zip(tasks, bases, results):
+            normals = gap_ref[0, pl.ds(base, 8), :] + gap_ref[1, pl.ds(base, 8), :]
+            normals = normals + gap_ref[2, pl.ds(base, 8), :]
+            slave_out[pl.ds(base, 8), :] = on_slave
+            master_out[pl.ds(base, 8), :] = normals * (total * (-1.0 / slope))
+            live = task < count
+            slave_from = task_ref[0, task]
+            master_from = task_ref[3, task]
+
+            @pl.when(live & (slave_from != own))
+            def _():
+                for k in range(3):
+                    back_ref[slave_from, pl.ds(task_ref[2, task] + k, 1), :] = on_slave[k : k + 1]
+
+            @pl.when(live & (master_from != own))
+            def _():
+                back_ref[master_from, pl.ds(task_ref[5, task], 1), :] = total
 
         return carry
 
-    lax.fori_loop(0, count, tile, 0)
+    lax.fori_loop(0, (count + TASK_STEP - 1) // TASK_STEP, tile, 0)
 
 
 def near_kernel(own_ref, task_ref, nodes_ref, slave_ref, master_ref, inner_ref, out_ref):
@@ -572,7 +608,18 @@
 
 
 def far_kernel(
-    chunks, entry_ref, back_ref, nodes_ref, normal_ref, near_ref, faces_ref, out_ref, low_ref, high_ref
+    chunks,
+    grid,
+    own_ref,
+    entry_ref,
+    back_ref,
+    nodes_ref,
+    normal_ref,
+    near_ref,
+    faces_ref,
+    out_ref,
+    send_ref,
+    value_ref,
 ):
     count = entry_ref[4, 0]
 
@@ -598,7 +645,7 @@
 
     acc = lax.fori_loop(0, (count + 1) // 2, step, jnp.zeros((6 * GROUP, LANES), F32))
     out_ref[...] = near_ref[...] + fold_terms(acc)
-    send_faces(out_ref, chunks, faces_ref, 0, low_ref, high_ref)
+    send_faces(own_ref[0], grid, out_ref, chunks, faces_ref, send_ref, value_ref)
 
 
 def element_kernel(conn_ref, coords_ref, disp_ref, modulus_ref, out_ref, order_ref):
@@ -696,9 +743,25 @@
     out_ref[...] = fold_terms(acc)
 
 
-def send_faces(total_ref, chunks, faces_ref, low_row, low_ref, high_ref):
-    low_ref[...] = jnp.zeros_like(low_ref)
-    high_ref[...] = jnp.zeros_like(high_ref)
+def around(grid):
+    return [(dx, dy) for dx in (-1, 0, 1) for dy in (-1, 0, 1) if (dx, dy) != (0, 0)]
+
+
+def face_toward(dx, dy):
+    if dx:
+        return 1 if dx > 0 else 0
+    return 3 if dy > 0 else 2
+
+
+def neighbour(own, grid, dx, dy):
+    ix = own // grid[1] + dx
+    iy = own % grid[1] + dy
+    there = (ix >= 0) & (ix < grid[0]) & (iy >= 0) & (iy < grid[1])
+    return there, jnp.where(there, ix * grid[1] + iy, 0)
+
+
+def send_faces(own, grid, total_ref, chunks, faces_ref, send_ref, value_ref):
+    value_ref[...] = jnp.zeros_like(value_ref)
     parts = faces_ref.shape[1] // LANES
     for part in range(parts):
         ids = faces_ref[:, part * LANES : (part + 1) * LANES]
@@ -710,24 +773,61 @@
         )
         for field in range(3):
             at = field * parts + part
-            low_ref[at : at + 1, :] = found[field][low_row : low_row + 1]
-            high_ref[at : at + 1, :] = found[field][low_row + 1 : low_row + 2]
-
-
-def add_faces(faces_ref, low_row, low_ref, high_ref):
+            for face in range(4):
+                value_ref[face, at : at + 1, :] = found[field][face : face + 1]
+    for dx, dy in around(grid):
+        there, target = neighbour(own, grid, dx, dy)
+
+        @pl.when(there)
+        def _():
+            send_ref[target] = value_ref[face_toward(dx, dy)]
+
+
+def face_map_kernel(chunks, faces_ref, low_ref, high_ref, table_ref):
     parts = faces_ref.shape[1] // LANES
     acc = None
-    for row, got_ref in ((low_row, low_ref), (low_row + 1, high_ref)):
+    for row in range(2):
         ids = [faces_ref[row : row + 1, p * LANES : (p + 1) * LANES] for p in range(parts)]
-        forces = [
-            [got_ref[f * parts + p : f * parts + p + 1, :] for f in range(3)] for p in range(parts)
-        ]
-        terms = scatter_terms(ids, forces)
+        zero = jnp.zeros((1, LANES), F32)
+        places = [(iota((1, LANES), 1) + (p * LANES + 1)).astype(F32) for p in range(parts)]
+        fields = [[place if f == row else zero for f in range(3)] for place in places]
+        terms = scatter_terms(ids, fields)
         acc = terms if acc is None else acc + terms
-    return fold_terms(acc)
-
-
-def assemble_kernel(slots, chunks, back_ref, ids_ref, inner_ref, faces_ref, out_ref, low_ref, high_ref):
+    table_ref[...] = fold_terms(acc)
+    low_ref[...] = jnp.zeros_like(low_ref)
+    high_ref[...] = jnp.zeros_like(high_ref)
+    for part in range(parts):
+        ids = faces_ref[:, part * LANES : (part + 1) * LANES]
+        found = gather_chunks(
+            lambda field, chunk: table_ref[field * GROUP + chunk : field * GROUP + chunk + 1, :],
+            2,
+            chunks,
+            ids,
+        )
+        for field in range(2):
+            at = field * parts + part
+            low_ref[at : at + 1, :] = found[field][2:3]
+            high_ref[at : at + 1, :] = found[field][3:4]
+
+
+def moved_faces(values, places, parts):
+    results = [None] * (3 * parts)
+    for part in range(parts):
+        place = places[part].astype(jnp.int32) - 1
+        low = jnp.broadcast_to(place & (LANES - 1), values.shape)
+        got = jnp.take_along_axis(values, low, axis=1, mode="promise_in_bounds")
+        for field in range(3):
+            total = jnp.zeros((1, LANES), F32)
+            for source in range(parts):
+                at = field * parts + source
+                total = jnp.where(place >> 7 == source, got[at : at + 1], total)
+            results[field * parts + part] = total
+    return results
+
+
+def assemble_kernel(
+    slots, chunks, grid, own_ref, back_ref, ids_ref, inner_ref, faces_ref, out_ref, send_ref, value_ref
+):
     devices = back_ref.shape[0]
 
     def step(turn, acc):
@@ -743,16 +843,37 @@
 
     acc = lax.fori_loop(0, devices, step, jnp.zeros((6 * GROUP, LANES), F32))
     out_ref[...] = inner_ref[...] + fold_terms(acc)
-    send_faces(out_ref, chunks, faces_ref, 0, low_ref, high_ref)
-
-
-def middle_kernel(chunks, total_ref, from_low, from_high, faces_ref, out_ref, low_ref, high_ref):
-    out_ref[...] = total_ref[...] + add_faces(faces_ref, 0, from_low, from_high)
-    send_faces(out_ref, chunks, faces_ref, 2, low_ref, high_ref)
-
-
-def final_kernel(total_ref, from_low, from_high, faces_ref, velocity_ref, mass_ref, out_ref, sum_ref):
-    sum_ref[...] = total_ref[...] + add_faces(faces_ref, 2, from_low, from_high)
+    send_faces(own_ref[0], grid, out_ref, chunks, faces_ref, send_ref, value_ref)
+
+
+def final_kernel(
+    grid, own_ref, total_ref, got_ref, low_ref, high_ref, faces_ref, velocity_ref, mass_ref, out_ref, sum_ref
+):
+    own = own_ref[0]
+    parts = faces_ref.shape[1] // LANES
+
+    def block(dx, dy):
+        there, source = neighbour(own, grid, dx, dy)
+        return jnp.where(there, got_ref[source], 0.0)
+
+    def rows_of(values):
+        return [values[at : at + 1] for at in range(3 * parts)]
+
+    def side(dy, map_ref):
+        rows = rows_of(block(0, dy))
+        for field, dx in enumerate((-1, 1)):
+            places = [map_ref[field * parts + p : field * parts + p + 1, :] for p in range(parts)]
+            rows = [a + b for a, b in zip(rows, moved_faces(block(dx, dy), places, parts))]
+        return rows
+
+    added = [rows_of(block(-1, 0)), rows_of(block(1, 0)), side(-1, low_ref), side(1, high_ref)]
+    acc = jnp.zeros((6 * GROUP, LANES), F32)
+    for face, rows in enumerate(added):
+        ids = [faces_ref[face : face + 1, p * LANES : (p + 1) * LANES] for p in range(parts)]
+        acc = acc + scatter_terms(
+            ids, [[rows[f * parts + p] for f in range(3)] for p in range(parts)]
+        )
+    sum_ref[...] = total_ref[...] + fold_terms(acc)
     for chunk in range(out_ref.shape[1] // LANES):
         span = slice(chunk * LANES, (chunk + 1) * LANES)
         scale = TIME_STEP / mass_ref[chunk : chunk + 1, :]
@@ -816,6 +937,8 @@
     face_rows = -(-3 * parts // 8) * 8
     total_shape = ((3 * GROUP, LANES), F32)
     face_shape = ((face_rows, LANES), F32)
+    send_shape = ((devices, face_rows, LANES), F32)
+    grid = (lax.axis_size("gx"), lax.axis_size("gy"))
 
     def to_all(values):
         return lax.all_to_all(values, axes, split_axis=0, concat_axis=0, tiled=True)
@@ -847,6 +970,14 @@
         (connectivity, coords, displacement, modulus.reshape(-1, LANES)),
         [pltpu.VMEM((connectivity.shape[1] // LANES * 8, LANES), jnp.int32)],
     )
+    map_low, map_high = call(
+        functools.partial(face_map_kernel, chunks),
+        [face_shape, face_shape],
+        (),
+        (faces,),
+        [pltpu.VMEM((3 * GROUP, LANES), F32)],
+    )
+    map_low, map_high = exchange(map_low, map_high, "gy")
     outbound, entries, tasks = call(
         functools.partial(plan_kernel, slots),
         [
@@ -860,6 +991,7 @@
         (1, 2),
     )
     inbound = to_all(outbound)
+    inbound, map_low, map_high = lax.optimization_barrier((inbound, map_low, map_high))
     over = jnp.max(inbound[:, SEND_ROWS - 1, 0]) > 0.0
 
     def by_tasks():
@@ -872,7 +1004,13 @@
             ],
             (0, 1),
             (own, tasks, inbound, asked, pos, surf_angles),
-            [pltpu.VMEM((TASKS * 8, LANES), F32)] * 4,
+            [
+                pltpu.VMEM((10, TASKS, LANES), F32),
+                pltpu.VMEM((3, TASKS * 8, LANES), F32),
+                pltpu.VMEM((3, TASKS * 8, LANES), F32),
+                pltpu.VMEM((3, TASKS * 8, LANES), F32),
+                pltpu.VMEM((2, TASKS * 8, LANES), F32),
+            ],
         )
         returned = to_all(back)
         [near] = call(
@@ -882,10 +1020,11 @@
             (own, tasks, surf_nodes, on_slave, on_master, internal),
         )
         return call(
-            functools.partial(far_kernel, chunks),
-            [total_shape, face_shape, face_shape],
-            (0,),
-            (entries, returned, surf_nodes, normals, near, faces),
+            functools.partial(far_kernel, chunks, grid),
+            [total_shape, send_shape],
+            (0, 1),
+            (own, entries, returned, surf_nodes, normals, near, faces),
+            [pltpu.VMEM((4,) + face_shape[0], F32)],
         )
 
     def by_owners():
@@ -909,26 +1048,28 @@
             [pltpu.VMEM((pairs * 8, LANES), F32)] * 4,
         )
         return call(
-            functools.partial(assemble_kernel, slots, chunks),
-            [total_shape, face_shape, face_shape],
-            (),
-            (to_all(forces), ids, internal, faces),
-        )
-
-    total, low, high = lax.cond(over, by_owners, by_tasks)
-    from_low, from_high = exchange(low, high, "gx")
-    total, low, high = call(
-        functools.partial(middle_kernel, chunks),
-        [total_shape, face_shape, face_shape],
-        (),
-        (total, from_low, from_high, faces),
-    )
-    from_low, from_high = exchange(low, high, "gy")
+            functools.partial(assemble_kernel, slots, chunks, grid),
+            [total_shape, send_shape],
+            (0,),
+            (own, to_all(forces), ids, internal, faces),
+            [pltpu.VMEM((4,) + face_shape[0], F32)],
+        )
+
+    total, send = lax.cond(over, by_owners, by_tasks)
     [result] = call(
-        final_kernel,
+        functools.partial(final_kernel, grid),
         [((3, node_count), F32)],
-        (),
-        (total, from_low, from_high, faces, velocity, node_mass.reshape(chunks, LANES)),
+        (0,),
+        (
+            own,
+            total,
+            to_all(send),
+            map_low,
+            map_high,
+            faces,
+            velocity,
+            node_mass.reshape(chunks, LANES),
+        ),
         [pltpu.VMEM((3 * GROUP, LANES), F32)],
     )
     return result

time: 90.7 us -> 78.9 us (0.87)
  the two profiles are of different devices: /device:TPU:3 before, /device:TPU:0 now
where the time goes in v2:
time: 78.9 us
  Pallas kernels  30.6 us (39%)
  waiting for transfers between devices  17.5 us (22%)
  starting transfers between devices  16.4 us (21%)
  blocking collectives  9.93 us (13%)
  local copies, waits for them, and re-layouts  2.11 us (3%)
  between operations  1.61 us (2%)
    pallas_call x9, Pallas kernels, call(): pl.pallas_call(kernel, out_shape=[jax.ShapeDtypeStruct(shape, dtype) for...  30.6 us
    all_to_all x3, waiting for transfers between devices, to_all(): return lax.all_to_all(values, axes, split_axis=0, concat_axis=0, tiled=True)  16.6 us
    all_to_all x3, starting transfers between devices, to_all(): return lax.all_to_all(values, axes, split_axis=0, concat_axis=0, tiled=True)  13.1 us
    all_to_all x1, blocking collectives, to_all(): return lax.all_to_all(values, axes, split_axis=0, concat_axis=0, tiled=True)  9.93 us
    ppermute x1, starting transfers between devices, exchange(): lax.ppermute(high, axis, forward)  2.02 us
  transfers between devices with their start and end apart: 5, of which 4 were waited for; matrix products, arithmetic and copies ran while one was open for 3% of the time, Pallas kernels for 14%

profile of v2, /device:TPU:0, one launch (start us, length us, event | category | flops | bytes accessed | tf_op | source)
XLA Modules:
  0.0 78.9 jit_solution(7764497624111761202)
XLA Ops:
  0.7 2.3 %shard_map.136 = s32[32,16,128]{2,1,0:T(8,128)} custom-call(s32[1]{0:T(128)} %bitcast.own_ref, s32[1]{0:T(128)S(6)} %copy.25.count_ref, s32[64,128]{1,0:T(8,128)} %bitcast.10, s32[2,64]{1,0:T(2,128)} %pairs_ref.1, s32[2,64,128]{2,1,0:T(8,128)} %masks_ref.1), custom_call_target="tpu_custom_call" | custom-call | tf_op jit(solution)/shard_map/pallas_call | solution.py:891
  3.0 7.3 %all-to-all-start.3 = ((s32[32,16,128]{2,1,0:T(8,128)}), s32[32,16,128]{2,1,0:T(8,128)S(1)}, u32[]{:S(2)}, u32[]{:S(2)}) async-start(s32[32,16,128]{2,1,0:T(8,128)} %shard_map.136), calls=%async_computation.3 | async-start | bytes 524288 | tf_op jit(solution)/shard_map/all_to_all | solution.py:944
  10.4 0.8 dynamic_slice.3.owners_ref
  11.1 1.3 %copy.19.ref_ref = f32[256,3,128]{2,1,0:T(4,128)S(1)} copy(f32[256,3,128]{2,0,1:T(8,128)} %param.24) | data formatting | bytes 786432 | tf_op args[8]
  12.4 0.0 copy-start.3
  12.5 4.6 %shard_map.137 = (f32[3,256,128]{2,1,0:T(8,128)S(1)}, f32[3,256,128]{2,1,0:T(8,128)S(1)}, s32[512]{0:T(512)S(1)}) custom-call(s32[256]{0:T(256)S(1)} %dynamic_slice.3.owners_ref, f32[3,1408]{1,0:T(4,128)S(1)} %copy-done, s32[256,128]{1,0:T(8,128)S(1)} %copy-done.7, f32[256,3,128]{2,1,0:T(4,128)S(1)} %copy.19.ref_ref, f32[256,2,128]{2,1,0:T(2,128)S(1)} %copy-done.6), custom_call_target="tpu_custom_call" | custom-call | tf_op jit(solution)/shard_map/pallas_call | solution.py:891
  17.1 3.8 %all-to-all-done.3 = s32[32,16,128]{2,1,0:T(8,128)S(1)} async-done(((s32[32,16,128]{2,1,0:T(8,128)}), s32[32,16,128]{2,1,0:T(8,128)S(1)}, u32[]{:S(2)}, u32[]{:S(2)}) %all-to-all-start.3) | async-done | bytes 262176 | tf_op jit(solution)/shard_map/all_to_all | solution.py:944
  21.0 5.5 %shard_map.138 = (f32[32,32,128]{2,1,0:T(8,128)}, s32[8,160]{1,0:T(8,128)S(1)}, s32[16,64]{1,0:T(8,128)S(1)}) custom-call(s32[1]{0:T(128)} %bitcast.own_ref, s32[32,128]{1,0:T(8,128)S(1)} %bitcast.7, s32[512]{0:T(512)S(1)} %get-tuple-element.86.block_ref, f32[3,256,128]{2,1,0:T(8,128)S(1)} %get-tuple-element.87.pos_ref, f32[256,2,128]{2,1,0:T(2,128)S(1)} %copy-done.6), custom_call_target="tpu_custom_call" | custom-call | tf_op jit(solution)/shard_map/pallas_call | solution.py:891
  26.4 2.6 %all-to-all-start.4 = ((f32[32,32,128]{2,1,0:T(8,128)}), f32[32,32,128]{2,1,0:T(8,128)S(1)}, u32[]{:S(2)}, u32[]{:S(2)}) async-start(f32[32,32,128]{2,1,0:T(8,128)} %get-tuple-element.88), calls=%async_computation.4 | async-start | bytes 1048576 | tf_op jit(solution)/shard_map/all_to_all | solution.py:944
  29.1 0.3 shard_map.139
  29.4 2.0 %collective-permute-start = (f32[8,128]{1,0:T(8,128)S(1)}, f32[8,128]{1,0:T(8,128)S(1)}, u32[]{:S(2)}, u32[]{:S(2)}) collective-permute-start(f32[8,128]{1,0:T(8,128)S(1)} %get-tuple-element.89), channel_id=1, source_target_pairs={{0,1},{1,2},{2,3},{3,4},{4,5},{5,6},{6,7},{8,9},{9,10},{10,11},{11... | collective-permute-start | bytes 12296 | tf_op jit(solution)/shard_map/ppermute | solution.py:905
  31.4 1.3 %collective-permute-start.1 = (f32[8,128]{1,0:T(8,128)S(1)}, f32[8,128]{1,0:T(8,128)S(1)}, u32[]{:S(2)}, u32[]{:S(2)}) collective-permute-start(f32[8,128]{1,0:T(8,128)S(1)} %get-tuple-element.90), channel_id=1, source_target_pairs={{1,0},{2,1},{3,2},{4,3},{5,4},{6,5},{7,6},{9,8},{10,9},{11,10},{12... | collective-permute-start | bytes 12296 | tf_op jit(solution)/shard_map/ppermute | solution.py:905
  32.7 1.9 %shard_map.140 = f32[48,128]{1,0:T(8,128)S(1)} custom-call(s32[8,1024]{1,0:T(8,128)S(1)} %copy-done.1, f32[3,1408]{1,0:T(4,128)S(1)} %copy-done.3, f32[3,1408]{1,0:T(4,128)S(1)} %copy-done, f32[8,128]{1,0:T(8,128)S(1)} %bitcast.9), custom_call_target="tpu_custom_call" | custom-call | tf_op jit(solution)/shard_map/pallas_call | solution.py:891
  34.7 1.0 %collective-permute-done.1.high_ref = f32[8,128]{1,0:T(8,128)S(1)} collective-permute-done((f32[8,128]{1,0:T(8,128)S(1)}, f32[8,128]{1,0:T(8,128)S(1)}, u32[]{:S(2)}, u32[]{:S(2)}) %collective-permute-start.1) | collective-permute-done | bytes 4128 | tf_op jit(solution)/shard_map/ppermute | solution.py:905
  35.6 9.0 %all-to-all-done.4 = f32[32,32,128]{2,1,0:T(8,128)S(1)} async-done(((f32[32,32,128]{2,1,0:T(8,128)}), f32[32,32,128]{2,1,0:T(8,128)S(1)}, u32[]{:S(2)}, u32[]{:S(2)}) %all-to-all-start.4) | async-done | bytes 524320 | tf_op jit(solution)/shard_map/all_to_all | solution.py:944
  44.6 0.6 slice_reduce_fusion
  45.9 22.1 %conditional.1 = ((f32[48,128]{1,0:T(8,128)S(1)}, f32[32,8,128]{2,1,0:T(8,128)S(1)})) conditional(s32[]{:T(128)} %convert_element_type.3, (s32[1]{0:T(128)}, s32[16,64]{1,0:T(8,128)S(1)}, f32[32,32,128]{2,1,0:T(8,128)S(1)}, s32[32,16,128]{2,1,0:T(8,128)S(1)}, f32[3,256,128]{2,1,0:T(8,128)S(1)}, /*index=5*/f32[256,2,128]{2,1,0:T(2,128)S(1)}, ...), branch_computations={%region_1.2_spmd, %region_2.3_spmd} | conditional | bytes 5505064 | solution.py:1058
  46.0 5.1 %branch_0_fun.3 = (f32[32,8,128]{2,1,0:T(8,128)}, f32[512,128]{1,0:T(8,128)S(1)}, f32[512,128]{1,0:T(8,128)S(1)}) custom-call(s32[1]{0:T(128)} %get-tuple-element.47.own_ref, s32[16,64]{1,0:T(8,128)S(1)} %get-tuple-element.49.task_ref, f32[32,32,128]{2,1,0:T(8,128)S(1)} %get-tuple-element.50.in_ref, s32[32,16,128]{2,1,0:T(8,128)S(1)} %get-tuple-element.51.request_ref, ...), custom_call_target="tpu_custom_call" | custom-call | tf_op jit(solution)/shard_map/cond/branch_0_fun/pallas_call | solution.py:891
  51.1 3.2 %all-to-all-start = ((f32[32,8,128]{2,1,0:T(8,128)}), f32[32,8,128]{2,1,0:T(8,128)S(1)}, u32[]{:S(2)}, u32[]{:S(2)}) async-start(f32[32,8,128]{2,1,0:T(8,128)} %get-tuple-element.54), calls=%async_computation | async-start | bytes 262144 | tf_op jit(solution)/shard_map/cond/branch_0_fun/all_to_all | solution.py:944
  54.3 4.5 %branch_0_fun.4.near_ref = f32[48,128]{1,0:T(8,128)S(1)} custom-call(s32[1]{0:T(128)} %get-tuple-element.47.own_ref, s32[16,64]{1,0:T(8,128)S(1)} %get-tuple-element.49.task_ref, s32[256,128]{1,0:T(8,128)S(1)} %get-tuple-element.55.nodes_ref, f32[512,128]{1,0:T(8,128)S(1)} %get-tuple-element.57.slave_ref, f32[512,128]{1,0:T(8,128)S(1)} %get-tuple-element.58.master_ref, ...), custom_call_target="tpu_custom_call" | custom-call | tf_op jit(solution)/shard_map/cond/branch_0_fun/pallas_call | solution.py:891
  58.8 3.7 %all-to-all-done.back_ref = f32[32,8,128]{2,1,0:T(8,128)S(1)} async-done(((f32[32,8,128]{2,1,0:T(8,128)}), f32[32,8,128]{2,1,0:T(8,128)S(1)}, u32[]{:S(2)}, u32[]{:S(2)}) %all-to-all-start) | async-done | bytes 131104 | tf_op jit(solution)/shard_map/cond/branch_0_fun/all_to_all | solution.py:944
  62.5 5.5 %branch_0_fun.5 = (f32[48,128]{1,0:T(8,128)S(1)}, f32[32,8,128]{2,1,0:T(8,128)S(1)}) custom-call(s32[1]{0:T(128)} %get-tuple-element.47.own_ref, s32[8,160]{1,0:T(8,128)S(1)} %get-tuple-element.48.entry_ref, f32[32,8,128]{2,1,0:T(8,128)S(1)} %all-to-all-done.back_ref, s32[256,128]{1,0:T(8,128)S(1)} %get-tuple-element.55.nodes_ref, ...), custom_call_target="tpu_custom_call" | custom-call | tf_op jit(solution)/shard_map/cond/branch_0_fun/pallas_call | solution.py:891
  68.1 9.9 %all_to_all.28.got_ref = f32[32,8,128]{2,1,0:T(8,128)S(1)} all-to-all(f32[32,8,128]{2,1,0:T(8,128)S(1)} %get-tuple-element.96), channel_id=1, replica_groups=mesh['gx'=4,'gy'=8] {'gx','gy'}, dimensions={0} | all-to-all | bytes 262144 | tf_op jit(solution)/shard_map/all_to_all | solution.py:944
  78.0 0.9 %shard_map.141 = f32[3,1408]{1,0:T(4,128)} custom-call(s32[1]{0:T(128)} %bitcast.own_ref, f32[48,128]{1,0:T(8,128)S(1)} %get-tuple-element.95.total_ref, f32[32,8,128]{2,1,0:T(8,128)S(1)} %all_to_all.28.got_ref, f32[8,128]{1,0:T(8,128)S(1)} %collective-permute-done.low_ref, f32[8,128]{1,0:T(8,128)S(1)} %collective-permute-done.1.high_ref, ...), custom_call_target="tpu_custom_call" | custom-call | tf_op jit(solution)/shard_map/pallas_call | solution.py:891
  (26 shorter events, 0.1 us)
Async XLA Ops:
  0.0 12.4 %copy-start = (f32[3,1408]{1,0:T(4,128)S(1)}, f32[3,1408]{1,0:T(4,128)}, u32[]{:S(2)}) copy-start(f32[3,1408]{1,0:T(4,128)} %disp_ref.3) | copy-start | bytes 50692
  0.0 12.4 %copy-start.7 = (s32[256,128]{1,0:T(8,128)S(1)}, s32[256,128]{1,0:T(8,128)}, u32[]{:S(2)}) copy-start(s32[256,128]{1,0:T(8,128)} %nodes_ref.1) | copy-start | bytes 393220
  0.0 12.4 %copy-start.6 = (f32[256,2,128]{2,1,0:T(2,128)S(1)}, f32[256,2,128]{2,1,0:T(2,128)}, u32[]{:S(2)}) copy-start(f32[256,2,128]{2,1,0:T(2,128)} %angles_ref.3) | copy-start | bytes 786436
  3.0 17.9 %all-to-all-start.3 = ((s32[32,16,128]{2,1,0:T(8,128)}), s32[32,16,128]{2,1,0:T(8,128)S(1)}, u32[]{:S(2)}, u32[]{:S(2)}) async-start(s32[32,16,128]{2,1,0:T(8,128)} %shard_map.136), calls=%async_computation.3 | async-start | bytes 524288 | tf_op jit(solution)/shard_map/all_to_all | solution.py:944
  12.4 16.6 %copy-start.11 = (s32[4,153]{1,0:T(4,128)S(1)}, s32[4,153]{1,0:T(4,128)}, u32[]{:S(2)}) copy-start(s32[4,153]{1,0:T(4,128)} %param.17) | copy-start | bytes 7348
  12.4 20.3 %copy-start.1 = (s32[8,1024]{1,0:T(8,128)S(1)}, s32[8,1024]{1,0:T(8,128)}, u32[]{:S(2)}) copy-start(s32[8,1024]{1,0:T(8,128)} %conn_ref.1) | copy-start | bytes 98308
  12.4 20.3 %copy-start.3 = (f32[3,1408]{1,0:T(4,128)S(1)}, f32[3,1408]{1,0:T(4,128)}, u32[]{:S(2)}) copy-start(f32[3,1408]{1,0:T(4,128)} %coords_ref.1) | copy-start | bytes 50692
  12.5 20.3 %copy-start.5 = (f32[1024]{0:T(1024)S(1)}, f32[1024]{0:T(1024)}, u32[]{:S(2)}) copy-start(f32[1024]{0:T(1024)} %param.22) | copy-start | bytes 12292
  12.5 33.4 %copy-start.8 = (s32[8192]{0:T(1024)S(1)}, s32[8192]{0:T(1024)}, u32[]{:S(2)}) copy-start(s32[8192]{0:T(1024)} %param.26) | copy-start | bytes 98308
  12.5 33.4 %copy-start.9 = (s32[2,64,128]{2,1,0:T(8,128)S(1)}, s32[2,64,128]{2,1,0:T(8,128)}, u32[]{:S(2)}) copy-start(s32[2,64,128]{2,1,0:T(8,128)} %masks_ref.1) | copy-start | bytes 196612
  12.5 33.4 %copy-start.10 = (s32[2,64]{1,0:T(2,128)S(1)}, s32[2,64]{1,0:T(2,128)}, u32[]{:S(2)}) copy-start(s32[2,64]{1,0:T(2,128)} %pairs_ref.1) | copy-start | bytes 1540
  26.4 18.2 %all-to-all-start.4 = ((f32[32,32,128]{2,1,0:T(8,128)}), f32[32,32,128]{2,1,0:T(8,128)S(1)}, u32[]{:S(2)}, u32[]{:S(2)}) async-start(f32[32,32,128]{2,1,0:T(8,128)} %get-tuple-element.88), calls=%async_computation.4 | async-start | bytes 1048576 | tf_op jit(solution)/shard_map/all_to_all | solution.py:944
  29.4 5.3 %collective-permute-start = (f32[8,128]{1,0:T(8,128)S(1)}, f32[8,128]{1,0:T(8,128)S(1)}, u32[]{:S(2)}, u32[]{:S(2)}) collective-permute-start(f32[8,128]{1,0:T(8,128)S(1)} %get-tuple-element.89), channel_id=1, source_target_pairs={{0,1},{1,2},{2,3},{3,4},{4,5},{5,6},{6,7},{8,9},{9,10},{10,11},{11... | collective-permute-start | bytes 12296 | tf_op jit(solution)/shard_map/ppermute | solution.py:905
  31.4 4.2 %collective-permute-start.1 = (f32[8,128]{1,0:T(8,128)S(1)}, f32[8,128]{1,0:T(8,128)S(1)}, u32[]{:S(2)}, u32[]{:S(2)}) collective-permute-start(f32[8,128]{1,0:T(8,128)S(1)} %get-tuple-element.90), channel_id=1, source_target_pairs={{1,0},{2,1},{3,2},{4,3},{5,4},{6,5},{7,6},{9,8},{10,9},{11,10},{12... | collective-permute-start | bytes 12296 | tf_op jit(solution)/shard_map/ppermute | solution.py:905
  45.9 32.1 %copy-start.2 = (f32[3,1408]{1,0:T(4,128)S(1)}, f32[3,1408]{1,0:T(4,128)}, u32[]{:S(2)}) copy-start(f32[3,1408]{1,0:T(4,128)} %velocity_ref.1) | copy-start | bytes 50692
  45.9 32.1 %copy-start.4 = (f32[1408]{0:T(1024)S(1)}, f32[1408]{0:T(1024)}, u32[]{:S(2)}) copy-start(f32[1408]{0:T(1024)} %param.21) | copy-start | bytes 16900
  51.1 11.4 %all-to-all-start = ((f32[32,8,128]{2,1,0:T(8,128)}), f32[32,8,128]{2,1,0:T(8,128)S(1)}, u32[]{:S(2)}, u32[]{:S(2)}) async-start(f32[32,8,128]{2,1,0:T(8,128)} %get-tuple-element.54), calls=%async_computation | async-start | bytes 262144 | tf_op jit(solution)/shard_map/cond/branch_0_fun/all_to_all | solution.py:944

commit v3 on v2

--- a/solution.py
+++ b/solution.py
@@ -42,6 +42,7 @@
 ENTRIES = 160
 TASKS = 64
 TASK_STEP = 8
+BLOCK_STEP = 8
 
 
 def iota(shape, dim):
@@ -263,15 +264,12 @@
     lax.fori_loop(0, nodes_ref.shape[0] // 8, step, 0, unroll=2)
 
 
-def plan_kernel(
-    cap, own_ref, list_ref, block_ref, pos_ref, angles_ref, out_ref, entry_ref, task_ref, used_ref
-):
-    own = own_ref[0]
+def plan_kernel(cap, list_ref, block_ref, pos_ref, angles_ref, out_ref, entry_ref, used_ref):
     devices = list_ref.shape[0]
 
     def clear(device, carry):
-        for row in range(4):
-            used_ref[row, device] = 0
+        used_ref[0, device] = 0
+        used_ref[1, device] = 0
         return carry
 
     lax.fori_loop(0, devices, clear, 0)
@@ -287,6 +285,8 @@
             back = used_ref[1, worker]
             after = first + 3 + 2 * role
             back_after = back + 3 - 2 * role
+            used_ref[0, worker] = after
+            used_ref[1, worker] = back_after
             fits = (after < SEND_ROWS) & (back_after <= BACK_ROWS) & (number < ENTRIES)
 
             @pl.when(fits)
@@ -302,31 +302,6 @@
             def _():
                 out_ref[worker, pl.ds(first + 3, 2), :] = angles_ref[block]
 
-            used_ref[0, worker] = after
-            used_ref[1, worker] = back_after
-            return (number + 1, jnp.where(fits, over, 1))
-
-        def task(turn, state):
-            number, over = state
-            at = TASK_LANE + 4 * turn
-            fits = number < TASKS
-
-            @pl.when(fits)
-            def _():
-                for side in range(2):
-                    source = list_ref[owner, at + 2 * side]
-                    here = source == own
-                    block = block_ref[owner * cap + list_ref[owner, at + 2 * side + 1]]
-                    used = used_ref[2, source]
-                    back = used_ref[3, source]
-                    task_ref[3 * side, number] = source
-                    task_ref[3 * side + 1, number] = jnp.where(here, block, used)
-                    task_ref[3 * side + 2, number] = back
-                    used_ref[2, source] = jnp.where(here, used, used + 3 + 2 * side)
-                    used_ref[3, source] = jnp.where(here, back, back + 3 - 2 * side)
-                task_ref[6, number] = owner
-                task_ref[7, number] = turn
-
             return (number + 1, jnp.where(fits, over, 1))
 
         entries, tasks, over = carry
@@ -334,17 +309,85 @@
         entries, over = lax.fori_loop(
             0, jnp.minimum(list_ref[owner, 0], ENTRY_CAP), entry, (entries, over)
         )
-        tasks, over = lax.fori_loop(
-            0, jnp.minimum(list_ref[owner, 1], TASK_CAP), task, (tasks, over)
-        )
-        return (entries, tasks, over)
+        return (entries, tasks + list_ref[owner, 1], over)
 
     zero = jnp.int32(0)
     entries, tasks, over = lax.fori_loop(0, devices, from_owner, (zero, zero, zero))
+    over = jnp.where(tasks > TASKS, 1, over)
     entry_ref[4, 0] = jnp.minimum(entries, ENTRIES)
-    task_ref[8, 0] = jnp.minimum(tasks, TASKS)
     mark = jnp.full((devices, LANES), over.astype(F32), F32)
     out_ref[:, SEND_ROWS - 1, :] = mark
+
+
+def table_kernel(
+    cap,
+    own_ref,
+    list_ref,
+    block_ref,
+    request_ref,
+    pos_ref,
+    angles_ref,
+    task_ref,
+    near_ref,
+    field_ref,
+    used_ref,
+):
+    own = own_ref[0]
+    devices = list_ref.shape[0]
+    size = field_ref.shape[1]
+
+    def clear(device, carry):
+        used_ref[0, device] = 0
+        used_ref[1, device] = 0
+        return carry
+
+    lax.fori_loop(0, devices, clear, 0)
+
+    def from_owner(owner, carry):
+        def task(turn, state):
+            at = TASK_LANE + 4 * turn
+            number, near = state
+            for side in range(2):
+                source = list_ref[owner, at + 2 * side]
+                here = source == own
+                block = block_ref[owner * cap + list_ref[owner, at + 2 * side + 1]]
+                used = used_ref[0, source]
+                back = used_ref[1, source]
+                used_ref[0, source] = jnp.where(here, used, used + 3 + 2 * side)
+                used_ref[1, source] = jnp.where(here, back, back + 3 - 2 * side)
+                task_ref[3 * side, number] = source
+                task_ref[3 * side + 1, number] = jnp.where(here, block, used)
+                task_ref[3 * side + 2, number] = back
+                base = 4 * side
+                field_ref[base + 3, pl.ds(number, 1), :] = request_ref[
+                    owner, pl.ds(1 + 2 * turn + side, 1), :
+                ].astype(F32)
+                spot = near
+
+                @pl.when(here)
+                def _():
+                    near_ref[0, spot] = block
+                    near_ref[1, spot] = (side * size + number) * 8
+                    for field in range(3):
+                        field_ref[base + field, pl.ds(number, 1), :] = pos_ref[
+                            field, pl.ds(block, 1), :
+                        ]
+                    if side == 1:
+                        both = angles_ref[block]
+                        field_ref[8, pl.ds(number, 1), :] = both[0:1]
+                        field_ref[9, pl.ds(number, 1), :] = both[1:2]
+
+                near = near + jnp.where(here, 1, 0)
+            return (number + 1, near)
+
+        number, near = carry
+        count = jnp.minimum(list_ref[owner, 1], TASK_CAP)
+        count = jnp.minimum(count, TASKS - number)
+        return lax.fori_loop(0, count, task, (number, near))
+
+    tasks, near = lax.fori_loop(0, devices, from_owner, (jnp.int32(0), jnp.int32(0)))
+    task_ref[6, 0] = tasks
+    near_ref[2, 0] = near
 
 
 def pack_kernel(slots, rows_per, own_ref, map_ref, pos_ref, angles_ref, nodes_ref, out_ref, ids_ref):
@@ -460,12 +503,9 @@
     own_ref,
     task_ref,
     in_ref,
-    request_ref,
-    pos_ref,
-    angles_ref,
+    start_ref,
     back_ref,
-    slave_out,
-    master_out,
+    force_ref,
     field_ref,
     left_ref,
     gap_ref,
@@ -473,29 +513,18 @@
     push_ref,
 ):
     own = own_ref[0]
-    count = task_ref[8, 0]
+    count = task_ref[6, 0]
+    field_ref[...] = start_ref[...]
 
     def stage(task, carry):
-        owner = task_ref[6, task]
-        turn = task_ref[7, task]
         for side in range(2):
             source = task_ref[3 * side, task]
             first = task_ref[3 * side + 1, task]
-            base = 4 * side
-
-            @pl.when(source == own)
-            def _():
-                for field in range(3):
-                    field_ref[base + field, pl.ds(task, 1), :] = pos_ref[field, pl.ds(first, 1), :]
-                if side == 1:
-                    both = angles_ref[first]
-                    field_ref[8, pl.ds(task, 1), :] = both[0:1]
-                    field_ref[9, pl.ds(task, 1), :] = both[1:2]
 
             @pl.when(source != own)
             def _():
                 for field in range(3):
-                    field_ref[base + field, pl.ds(task, 1), :] = in_ref[
+                    field_ref[4 * side + field, pl.ds(task, 1), :] = in_ref[
                         source, pl.ds(first + field, 1), :
                     ]
                 if side == 1:
@@ -504,9 +533,6 @@
                             source, pl.ds(first + 3 + field, 1), :
                         ]
 
-            field_ref[base + 3, pl.ds(task, 1), :] = request_ref[
-                owner, pl.ds(1 + 2 * turn + side, 1), :
-            ].astype(F32)
         return carry
 
     lax.fori_loop(0, count, stage, 0)
@@ -568,8 +594,8 @@
         for task, base, (on_slave, total) in zip(tasks, bases, results):
             normals = gap_ref[0, pl.ds(base, 8), :] + gap_ref[1, pl.ds(base, 8), :]
             normals = normals + gap_ref[2, pl.ds(base, 8), :]
-            slave_out[pl.ds(base, 8), :] = on_slave
-            master_out[pl.ds(base, 8), :] = normals * (total * (-1.0 / slope))
+            force_ref[pl.ds(base, 8), :] = on_slave
+            force_ref[pl.ds(base + size * 8, 8), :] = normals * (total * (-1.0 / slope))
             live = task < count
             slave_from = task_ref[0, task]
             master_from = task_ref[3, task]
@@ -588,22 +614,23 @@
     lax.fori_loop(0, (count + TASK_STEP - 1) // TASK_STEP, tile, 0)
 
 
-def near_kernel(own_ref, task_ref, nodes_ref, slave_ref, master_ref, inner_ref, out_ref):
-    own = own_ref[0]
-
-    def step(task, acc):
+def near_kernel(near_ref, nodes_ref, force_ref, inner_ref, out_ref):
+    count = near_ref[2, 0]
+
+    def step(turn, acc):
         ids = []
         forces = []
-        for side, force_ref in ((0, slave_ref), (1, master_ref)):
-            here = task_ref[3 * side, task] == own
-            block = jnp.where(here, task_ref[3 * side + 1, task], 0)
-            ids.append(nodes_ref[pl.ds(block, 1), :])
-            rows = force_ref[pl.ds(pl.multiple_of(task * 8, 8), 8), :]
-            rows = jnp.where(here, rows, 0.0)
-            forces.append([rows[k : k + 1] for k in range(3)])
+        for k in range(BLOCK_STEP):
+            valid = BLOCK_STEP * turn + k < count
+            number = jnp.where(valid, BLOCK_STEP * turn + k, 0)
+            ids.append(nodes_ref[pl.ds(near_ref[0, number], 1), :])
+            rows = force_ref[pl.ds(pl.multiple_of(near_ref[1, number], 8), 8), :]
+            rows = jnp.where(valid, rows, 0.0)
+            forces.append([rows[f : f + 1] for f in range(3)])
         return acc + scatter_terms(ids, forces)
 
-    acc = lax.fori_loop(0, task_ref[8, 0], step, jnp.zeros((6 * GROUP, LANES), F32))
+    steps = (count + BLOCK_STEP - 1) // BLOCK_STEP
+    acc = lax.fori_loop(0, steps, step, jnp.zeros((6 * GROUP, LANES), F32))
     out_ref[...] = inner_ref[...] + fold_terms(acc)
 
 
@@ -626,9 +653,9 @@
     def step(turn, acc):
         ids = []
         forces = []
-        for k in range(2):
-            valid = 2 * turn + k < count
-            number = jnp.where(valid, 2 * turn + k, 0)
+        for k in range(BLOCK_STEP):
+            valid = BLOCK_STEP * turn + k < count
+            number = jnp.where(valid, BLOCK_STEP * turn + k, 0)
             block = entry_ref[0, number]
             role = entry_ref[1, number]
             worker = entry_ref[2, number]
@@ -643,7 +670,8 @@
             forces.append(rows)
         return acc + scatter_terms(ids, forces)
 
-    acc = lax.fori_loop(0, (count + 1) // 2, step, jnp.zeros((6 * GROUP, LANES), F32))
+    steps = (count + BLOCK_STEP - 1) // BLOCK_STEP
+    acc = lax.fori_loop(0, steps, step, jnp.zeros((6 * GROUP, LANES), F32))
     out_ref[...] = near_ref[...] + fold_terms(acc)
     send_faces(own_ref[0], grid, out_ref, chunks, faces_ref, send_ref, value_ref)
 
@@ -978,32 +1006,33 @@
         [pltpu.VMEM((3 * GROUP, LANES), F32)],
     )
     map_low, map_high = exchange(map_low, map_high, "gy")
-    outbound, entries, tasks = call(
+    lists = asked[:, 0, :]
+    outbound, entries = call(
         functools.partial(plan_kernel, slots),
-        [
-            ((devices, SEND_ROWS, LANES), F32),
-            ((8, ENTRIES), jnp.int32),
-            ((16, TASKS), jnp.int32),
-        ],
+        [((devices, SEND_ROWS, LANES), F32), ((8, ENTRIES), jnp.int32)],
+        (0, 1),
+        (lists, block_of, pos, surf_angles),
+        [pltpu.SMEM((2, devices), jnp.int32)],
+        (1,),
+    )
+    tasks, near_list, fields = call(
+        functools.partial(table_kernel, slots),
+        [((8, TASKS), jnp.int32), ((8, 2 * TASKS), jnp.int32), ((10, TASKS, LANES), F32)],
         (0, 1, 2),
-        (own, asked[:, 0, :], block_of, pos, surf_angles),
-        [pltpu.SMEM((4, devices), jnp.int32)],
-        (1, 2),
+        (own, lists, block_of, asked, pos, surf_angles),
+        [pltpu.SMEM((2, devices), jnp.int32)],
+        (0, 1),
     )
     inbound = to_all(outbound)
     inbound, map_low, map_high = lax.optimization_barrier((inbound, map_low, map_high))
     over = jnp.max(inbound[:, SEND_ROWS - 1, 0]) > 0.0
 
     def by_tasks():
-        back, on_slave, on_master = call(
+        back, forces = call(
             work_kernel,
-            [
-                ((devices, BACK_ROWS, LANES), F32),
-                ((TASKS * 8, LANES), F32),
-                ((TASKS * 8, LANES), F32),
-            ],
+            [((devices, BACK_ROWS, LANES), F32), ((2 * TASKS * 8, LANES), F32)],
             (0, 1),
-            (own, tasks, inbound, asked, pos, surf_angles),
+            (own, tasks, inbound, fields),
             [
                 pltpu.VMEM((10, TASKS, LANES), F32),
                 pltpu.VMEM((3, TASKS * 8, LANES), F32),
@@ -1014,10 +1043,7 @@
         )
         returned = to_all(back)
         [near] = call(
-            near_kernel,
-            [total_shape],
-            (0, 1),
-            (own, tasks, surf_nodes, on_slave, on_master, internal),
+            near_kernel, [total_shape], (0,), (near_list, surf_nodes, forces, internal)
         )
         return call(
             functools.partial(far_kernel, chunks, grid),

time: 78.9 us -> 74 us (0.938)
  Pallas kernels: 30.6 us -> 24.7 us
    pallas_call x9 -> x10, Pallas kernels: 30.6 us -> 24.7 us  [call(): pl.pallas_call(kernel, out_shape=[jax.ShapeDtypeStruct(shape, dtype) for...]
    all_to_all x3, waiting for transfers between devices: 16.6 us -> 17.9 us  [to_all(): return lax.all_to_all(values, axes, split_axis=0, concat_axis=0, tiled=True)]
    ppermute x1, waiting for transfers between devices: 0.96 us -> 0.01 us  [exchange(): lax.ppermute(low, axis, backward)]
  transfers between devices with their start and end apart: 5 -> 5, of which waited for: 4 -> 3; matrix products, arithmetic and copies ran while one was open for 3% -> 3% of each run, Pallas kernels for 14% -> 15%
where the time goes in v3:
time: 74 us; the launch traced here: 73.6 us
  Pallas kernels  24.7 us (33%)
  waiting for transfers between devices  17.9 us (24%)
  starting transfers between devices  16.7 us (23%)
  blocking collectives  9.93 us (13%)
  local copies, waits for them, and re-layouts  2.11 us (3%)
  between operations  1.62 us (2%)
    pallas_call x10, Pallas kernels, call(): pl.pallas_call(kernel, out_shape=[jax.ShapeDtypeStruct(shape, dtype) for...  24.7 us
    all_to_all x3, waiting for transfers between devices, to_all(): return lax.all_to_all(values, axes, split_axis=0, concat_axis=0, tiled=True)  17.9 us
    all_to_all x3, starting transfers between devices, to_all(): return lax.all_to_all(values, axes, split_axis=0, concat_axis=0, tiled=True)  13.3 us
    all_to_all x1, blocking collectives, to_all(): return lax.all_to_all(values, axes, split_axis=0, concat_axis=0, tiled=True)  9.93 us
    ppermute x1, starting transfers between devices, exchange(): lax.ppermute(high, axis, forward)  2.02 us
  transfers between devices with their start and end apart: 5, of which 3 were waited for; matrix products, arithmetic and copies ran while one was open for 3% of the time, Pallas kernels for 15%

profile of v3, /device:TPU:0, one launch (start us, length us, event | category | flops | bytes accessed | tf_op | source)
XLA Modules:
  0.0 73.6 jit_solution(8908618753252671774)
XLA Ops:
  0.7 2.3 %shard_map.136 = s32[32,16,128]{2,1,0:T(8,128)} custom-call(s32[1]{0:T(128)} %bitcast.own_ref, s32[1]{0:T(128)S(6)} %copy.20.count_ref, s32[64,128]{1,0:T(8,128)} %bitcast.9, s32[2,64]{1,0:T(2,128)} %pairs_ref.1, s32[2,64,128]{2,1,0:T(8,128)} %masks_ref.1), custom_call_target="tpu_custom_call" | custom-call | tf_op jit(solution)/shard_map/pallas_call | solution.py:919
  3.0 7.3 %all-to-all-start.3 = ((s32[32,16,128]{2,1,0:T(8,128)}), s32[32,16,128]{2,1,0:T(8,128)S(1)}, u32[]{:S(2)}, u32[]{:S(2)}) async-start(s32[32,16,128]{2,1,0:T(8,128)} %shard_map.136), calls=%async_computation.3 | async-start | bytes 524288 | tf_op jit(solution)/shard_map/all_to_all | solution.py:972
  10.3 0.8 %dynamic_slice.3.owners_ref = s32[256]{0:T(256)S(1)} dynamic-slice(s32[8192]{0:T(1024)} %param.26, s32[]{:T(128)S(6)} %select_n.3), dynamic_slice_sizes={256} | dynamic-slice | bytes 2052 | tf_op jit(solution)/shard_map/dynamic_slice | solution.py:981
  11.1 1.3 %copy.15.ref_ref = f32[256,3,128]{2,1,0:T(4,128)S(1)} copy(f32[256,3,128]{2,0,1:T(8,128)} %param.24) | data formatting | bytes 786432 | tf_op args[8]
  12.4 0.0 copy-start.11
  12.5 4.6 %shard_map.137 = (f32[3,256,128]{2,1,0:T(8,128)S(1)}, f32[3,256,128]{2,1,0:T(8,128)S(1)}, s32[512]{0:T(512)S(1)}) custom-call(s32[256]{0:T(256)S(1)} %dynamic_slice.3.owners_ref, f32[3,1408]{1,0:T(4,128)S(1)} %copy-done, s32[256,128]{1,0:T(8,128)S(1)} %copy-done.7, f32[256,3,128]{2,1,0:T(4,128)S(1)} %copy.15.ref_ref, f32[256,2,128]{2,1,0:T(2,128)S(1)} %copy-done.6), custom_call_target="tpu_custom_call" | custom-call | tf_op jit(solution)/shard_map/pallas_call | solution.py:919
  17.0 3.9 %all-to-all-done.3.request_ref = s32[32,16,128]{2,1,0:T(8,128)S(1)} async-done(((s32[32,16,128]{2,1,0:T(8,128)}), s32[32,16,128]{2,1,0:T(8,128)S(1)}, u32[]{:S(2)}, u32[]{:S(2)}) %all-to-all-start.3) | async-done | bytes 262176 | tf_op jit(solution)/shard_map/all_to_all | solution.py:972
  21.0 4.1 %shard_map.138 = (f32[32,32,128]{2,1,0:T(8,128)}, s32[8,160]{1,0:T(8,128)S(1)}) custom-call(s32[32,128]{1,0:T(8,128)S(1)} %bitcast.5, s32[512]{0:T(512)S(1)} %get-tuple-element.84.block_ref, f32[3,256,128]{2,1,0:T(8,128)S(1)} %get-tuple-element.85.pos_ref, f32[256,2,128]{2,1,0:T(2,128)S(1)} %copy-done.6), custom_call_target="tpu_custom_call" | custom-call | tf_op jit(solution)/shard_map/pallas_call | solution.py:919
  25.1 2.6 %all-to-all-start.4 = ((f32[32,32,128]{2,1,0:T(8,128)}), f32[32,32,128]{2,1,0:T(8,128)S(1)}, u32[]{:S(2)}, u32[]{:S(2)}) async-start(f32[32,32,128]{2,1,0:T(8,128)} %get-tuple-element.86), calls=%async_computation.4 | async-start | bytes 1048576 | tf_op jit(solution)/shard_map/all_to_all | solution.py:972
  27.8 0.3 shard_map.139
  28.1 2.0 %collective-permute-start = (f32[8,128]{1,0:T(8,128)S(1)}, f32[8,128]{1,0:T(8,128)S(1)}, u32[]{:S(2)}, u32[]{:S(2)}) collective-permute-start(f32[8,128]{1,0:T(8,128)S(1)} %get-tuple-element.87), channel_id=1, source_target_pairs={{0,1},{1,2},{2,3},{3,4},{4,5},{5,6},{6,7},{8,9},{9,10},{10,11},{11... | collective-permute-start | bytes 12296 | tf_op jit(solution)/shard_map/ppermute | solution.py:933
  30.1 1.3 %collective-permute-start.1 = (f32[8,128]{1,0:T(8,128)S(1)}, f32[8,128]{1,0:T(8,128)S(1)}, u32[]{:S(2)}, u32[]{:S(2)}) collective-permute-start(f32[8,128]{1,0:T(8,128)S(1)} %get-tuple-element.88), channel_id=1, source_target_pairs={{1,0},{2,1},{3,2},{4,3},{5,4},{6,5},{7,6},{9,8},{10,9},{11,10},{12... | collective-permute-start | bytes 12296 | tf_op jit(solution)/shard_map/ppermute | solution.py:933
  31.4 1.9 %shard_map.141 = f32[48,128]{1,0:T(8,128)S(1)} custom-call(s32[8,1024]{1,0:T(8,128)S(1)} %copy-done.1, f32[3,1408]{1,0:T(4,128)S(1)} %copy-done.3, f32[3,1408]{1,0:T(4,128)S(1)} %copy-done, f32[8,128]{1,0:T(8,128)S(1)} %bitcast.8), custom_call_target="tpu_custom_call" | custom-call | tf_op jit(solution)/shard_map/pallas_call | solution.py:919
  33.3 3.0 %shard_map.140 = (s32[8,64]{1,0:T(8,128)S(1)}, s32[8,128]{1,0:T(8,128)S(1)}, f32[10,64,128]{2,1,0:T(8,128)S(1)}) custom-call(s32[1]{0:T(128)} %bitcast.own_ref, s32[32,128]{1,0:T(8,128)S(1)} %bitcast.6, s32[512]{0:T(512)S(1)} %get-tuple-element.84.block_ref, s32[32,16,128]{2,1,0:T(8,128)S(1)} %all-to-all-done.3.request_ref, ...), custom_call_target="tpu_custom_call" | custom-call | tf_op jit(solution)/shard_map/pallas_call | solution.py:919
  36.3 7.0 %all-to-all-done.4 = f32[32,32,128]{2,1,0:T(8,128)S(1)} async-done(((f32[32,32,128]{2,1,0:T(8,128)}), f32[32,32,128]{2,1,0:T(8,128)S(1)}, u32[]{:S(2)}, u32[]{:S(2)}) %all-to-all-start.4) | async-done | bytes 524320 | tf_op jit(solution)/shard_map/all_to_all | solution.py:972
  43.3 0.6 slice_reduce_fusion
  44.6 18.1 %conditional.1 = ((f32[48,128]{1,0:T(8,128)S(1)}, f32[32,8,128]{2,1,0:T(8,128)S(1)})) conditional(s32[]{:T(128)} %convert_element_type.3, (s32[1]{0:T(128)}, s32[8,64]{1,0:T(8,128)S(1)}, f32[32,32,128]{2,1,0:T(8,128)S(1)}, f32[10,64,128]{2,1,0:T(8,128)S(1)}, s32[8,128]{1,0:T(8,128)S(1)}, /*index=5*/s32[256,128]{1,0:T(8,128)S(1)}, ...), branch_computations={%region_1.2_spmd, %region_2.3_spmd} | conditional | bytes 5505064 | solution.py:1084
  44.6 3.8 %branch_0_fun.3 = (f32[32,8,128]{2,1,0:T(8,128)}, f32[1024,128]{1,0:T(8,128)S(1)}) custom-call(s32[1]{0:T(128)} %get-tuple-element.45.own_ref, s32[8,64]{1,0:T(8,128)S(1)} %get-tuple-element.47.task_ref, f32[32,32,128]{2,1,0:T(8,128)S(1)} %get-tuple-element.48.in_ref, f32[10,64,128]{2,1,0:T(8,128)S(1)} %get-tuple-element.49.start_ref), custom_call_target="tpu_custom_call" | custom-call | tf_op jit(solution)/shard_map/cond/branch_0_fun/pallas_call | solution.py:919
  48.5 3.4 %all-to-all-start = ((f32[32,8,128]{2,1,0:T(8,128)}), f32[32,8,128]{2,1,0:T(8,128)S(1)}, u32[]{:S(2)}, u32[]{:S(2)}) async-start(f32[32,8,128]{2,1,0:T(8,128)} %get-tuple-element.50), calls=%async_computation | async-start | bytes 262144 | tf_op jit(solution)/shard_map/cond/branch_0_fun/all_to_all | solution.py:972
  51.9 1.2 %branch_0_fun.4.near_ref = f32[48,128]{1,0:T(8,128)S(1)} custom-call(s32[8,128]{1,0:T(8,128)S(1)} %get-tuple-element.53.near_ref, s32[256,128]{1,0:T(8,128)S(1)} %get-tuple-element.51.nodes_ref, f32[1024,128]{1,0:T(8,128)S(1)} %get-tuple-element.54.force_ref, f32[48,128]{1,0:T(8,128)S(1)} %get-tuple-element.55.inner_ref), custom_call_target="tpu_custom_call" | custom-call | tf_op jit(solution)/shard_map/cond/branch_0_fun/pallas_call | solution.py:919
  53.1 7.1 %all-to-all-done.back_ref = f32[32,8,128]{2,1,0:T(8,128)S(1)} async-done(((f32[32,8,128]{2,1,0:T(8,128)}), f32[32,8,128]{2,1,0:T(8,128)S(1)}, u32[]{:S(2)}, u32[]{:S(2)}) %all-to-all-start) | async-done | bytes 131104 | tf_op jit(solution)/shard_map/cond/branch_0_fun/all_to_all | solution.py:972
  60.1 2.6 %branch_0_fun.5 = (f32[48,128]{1,0:T(8,128)S(1)}, f32[32,8,128]{2,1,0:T(8,128)S(1)}) custom-call(s32[1]{0:T(128)} %get-tuple-element.45.own_ref, s32[8,160]{1,0:T(8,128)S(1)} %get-tuple-element.46.entry_ref, f32[32,8,128]{2,1,0:T(8,128)S(1)} %all-to-all-done.back_ref, s32[256,128]{1,0:T(8,128)S(1)} %get-tuple-element.51.nodes_ref, ...), custom_call_target="tpu_custom_call" | custom-call | tf_op jit(solution)/shard_map/cond/branch_0_fun/pallas_call | solution.py:919
  62.7 9.9 %all_to_all.28.got_ref = f32[32,8,128]{2,1,0:T(8,128)S(1)} all-to-all(f32[32,8,128]{2,1,0:T(8,128)S(1)} %get-tuple-element.96), channel_id=1, replica_groups=mesh['gx'=4,'gy'=8] {'gx','gy'}, dimensions={0} | all-to-all | bytes 262144 | tf_op jit(solution)/shard_map/all_to_all | solution.py:972
  72.7 0.9 %shard_map.142 = f32[3,1408]{1,0:T(4,128)} custom-call(s32[1]{0:T(128)} %bitcast.own_ref, f32[48,128]{1,0:T(8,128)S(1)} %get-tuple-element.95.total_ref, f32[32,8,128]{2,1,0:T(8,128)S(1)} %all_to_all.28.got_ref, f32[8,128]{1,0:T(8,128)S(1)} %collective-permute-done.low_ref, f32[8,128]{1,0:T(8,128)S(1)} %collective-permute-done.1.high_ref, ...), custom_call_target="tpu_custom_call" | custom-call | tf_op jit(solution)/shard_map/pallas_call | solution.py:919
  (27 shorter events, 0.1 us)
Async XLA Ops:
  0.0 12.4 %copy-start = (f32[3,1408]{1,0:T(4,128)S(1)}, f32[3,1408]{1,0:T(4,128)}, u32[]{:S(2)}) copy-start(f32[3,1408]{1,0:T(4,128)} %disp_ref.3) | copy-start | bytes 50692
  0.0 12.4 %copy-start.7 = (s32[256,128]{1,0:T(8,128)S(1)}, s32[256,128]{1,0:T(8,128)}, u32[]{:S(2)}) copy-start(s32[256,128]{1,0:T(8,128)} %nodes_ref.1) | copy-start | bytes 393220
  0.0 12.4 %copy-start.6 = (f32[256,2,128]{2,1,0:T(2,128)S(1)}, f32[256,2,128]{2,1,0:T(2,128)}, u32[]{:S(2)}) copy-start(f32[256,2,128]{2,1,0:T(2,128)} %angles_ref.5) | copy-start | bytes 786436
  3.0 17.9 %all-to-all-start.3 = ((s32[32,16,128]{2,1,0:T(8,128)}), s32[32,16,128]{2,1,0:T(8,128)S(1)}, u32[]{:S(2)}, u32[]{:S(2)}) async-start(s32[32,16,128]{2,1,0:T(8,128)} %shard_map.136), calls=%async_computation.3 | async-start | bytes 524288 | tf_op jit(solution)/shard_map/all_to_all | solution.py:972
  12.4 15.3 %copy-start.11 = (s32[4,153]{1,0:T(4,128)S(1)}, s32[4,153]{1,0:T(4,128)}, u32[]{:S(2)}) copy-start(s32[4,153]{1,0:T(4,128)} %param.17) | copy-start | bytes 7348
  12.4 19.0 %copy-start.1 = (s32[8,1024]{1,0:T(8,128)S(1)}, s32[8,1024]{1,0:T(8,128)}, u32[]{:S(2)}) copy-start(s32[8,1024]{1,0:T(8,128)} %conn_ref.1) | copy-start | bytes 98308
  12.4 19.0 %copy-start.3 = (f32[3,1408]{1,0:T(4,128)S(1)}, f32[3,1408]{1,0:T(4,128)}, u32[]{:S(2)}) copy-start(f32[3,1408]{1,0:T(4,128)} %coords_ref.1) | copy-start | bytes 50692
  12.4 19.0 %copy-start.5 = (f32[1024]{0:T(1024)S(1)}, f32[1024]{0:T(1024)}, u32[]{:S(2)}) copy-start(f32[1024]{0:T(1024)} %param.22) | copy-start | bytes 12292
  20.9 23.6 %copy-start.8 = (s32[8192]{0:T(1024)S(1)}, s32[8192]{0:T(1024)}, u32[]{:S(2)}) copy-start(s32[8192]{0:T(1024)} %param.26) | copy-start | bytes 98308
  21.0 23.6 %copy-start.9 = (s32[2,64,128]{2,1,0:T(8,128)S(1)}, s32[2,64,128]{2,1,0:T(8,128)}, u32[]{:S(2)}) copy-start(s32[2,64,128]{2,1,0:T(8,128)} %masks_ref.1) | copy-start | bytes 196612
  21.0 23.6 %copy-start.10 = (s32[2,64]{1,0:T(2,128)S(1)}, s32[2,64]{1,0:T(2,128)}, u32[]{:S(2)}) copy-start(s32[2,64]{1,0:T(2,128)} %pairs_ref.1) | copy-start | bytes 1540
  25.1 18.2 %all-to-all-start.4 = ((f32[32,32,128]{2,1,0:T(8,128)}), f32[32,32,128]{2,1,0:T(8,128)S(1)}, u32[]{:S(2)}, u32[]{:S(2)}) async-start(f32[32,32,128]{2,1,0:T(8,128)} %get-tuple-element.86), calls=%async_computation.4 | async-start | bytes 1048576 | tf_op jit(solution)/shard_map/all_to_all | solution.py:972
  28.1 8.2 %collective-permute-start = (f32[8,128]{1,0:T(8,128)S(1)}, f32[8,128]{1,0:T(8,128)S(1)}, u32[]{:S(2)}, u32[]{:S(2)}) collective-permute-start(f32[8,128]{1,0:T(8,128)S(1)} %get-tuple-element.87), channel_id=1, source_target_pairs={{0,1},{1,2},{2,3},{3,4},{4,5},{5,6},{6,7},{8,9},{9,10},{10,11},{11... | collective-permute-start | bytes 12296 | tf_op jit(solution)/shard_map/ppermute | solution.py:933
  30.1 6.2 %collective-permute-start.1 = (f32[8,128]{1,0:T(8,128)S(1)}, f32[8,128]{1,0:T(8,128)S(1)}, u32[]{:S(2)}, u32[]{:S(2)}) collective-permute-start(f32[8,128]{1,0:T(8,128)S(1)} %get-tuple-element.88), channel_id=1, source_target_pairs={{1,0},{2,1},{3,2},{4,3},{5,4},{6,5},{7,6},{9,8},{10,9},{11,10},{12... | collective-permute-start | bytes 12296 | tf_op jit(solution)/shard_map/ppermute | solution.py:933
  44.6 28.1 %copy-start.2 = (f32[3,1408]{1,0:T(4,128)S(1)}, f32[3,1408]{1,0:T(4,128)}, u32[]{:S(2)}) copy-start(f32[3,1408]{1,0:T(4,128)} %velocity_ref.1) | copy-start | bytes 50692
  44.6 28.0 %copy-start.4 = (f32[1408]{0:T(1024)S(1)}, f32[1408]{0:T(1024)}, u32[]{:S(2)}) copy-start(f32[1408]{0:T(1024)} %param.21) | copy-start | bytes 16900
  48.5 11.7 %all-to-all-start = ((f32[32,8,128]{2,1,0:T(8,128)}), f32[32,8,128]{2,1,0:T(8,128)S(1)}, u32[]{:S(2)}, u32[]{:S(2)}) async-start(f32[32,8,128]{2,1,0:T(8,128)} %get-tuple-element.50), calls=%async_computation | async-start | bytes 262144 | tf_op jit(solution)/shard_map/cond/branch_0_fun/all_to_all | solution.py:972

commit v4 on v3

--- a/solution.py
+++ b/solution.py
@@ -40,7 +40,7 @@
 SEND_ROWS = 32
 BACK_ROWS = 8
 ENTRIES = 160
-TASKS = 64
+TASKS = 48
 TASK_STEP = 8
 BLOCK_STEP = 8
 
@@ -356,7 +356,7 @@
                 used_ref[0, source] = jnp.where(here, used, used + 3 + 2 * side)
                 used_ref[1, source] = jnp.where(here, back, back + 3 - 2 * side)
                 task_ref[3 * side, number] = source
-                task_ref[3 * side + 1, number] = jnp.where(here, block, used)
+                task_ref[3 * side + 1, number] = jnp.where(here, block, jnp.minimum(used, SEND_ROWS - 5))
                 task_ref[3 * side + 2, number] = back
                 base = 4 * side
                 field_ref[base + 3, pl.ds(number, 1), :] = request_ref[
@@ -506,6 +506,7 @@
     start_ref,
     back_ref,
     force_ref,
+    over_ref,
     field_ref,
     left_ref,
     gap_ref,
@@ -515,6 +516,10 @@
     own = own_ref[0]
     count = task_ref[6, 0]
     field_ref[...] = start_ref[...]
+    over = jnp.max(in_ref[:, SEND_ROWS - 1, :])
+    over_ref[0] = over.astype(jnp.int32)
+    marks = force_ref.shape[0] - 8
+    force_ref[marks:, :] = jnp.full((8, LANES), over, F32)
 
     def stage(task, carry):
         for side in range(2):
@@ -614,7 +619,7 @@
     lax.fori_loop(0, (count + TASK_STEP - 1) // TASK_STEP, tile, 0)
 
 
-def near_kernel(near_ref, nodes_ref, force_ref, inner_ref, out_ref):
+def near_kernel(near_ref, nodes_ref, force_ref, inner_ref, whole_ref, out_ref):
     count = near_ref[2, 0]
 
     def step(turn, acc):
@@ -631,7 +636,11 @@
 
     steps = (count + BLOCK_STEP - 1) // BLOCK_STEP
     acc = lax.fori_loop(0, steps, step, jnp.zeros((6 * GROUP, LANES), F32))
-    out_ref[...] = inner_ref[...] + fold_terms(acc)
+    marks = force_ref[force_ref.shape[0] - 8 :, :]
+    total = inner_ref[...] + fold_terms(acc)
+    rows = total.shape[0]
+    out_ref[:rows, :] = jnp.where(marks[0:1] > 0.0, whole_ref[...], total)
+    out_ref[rows:, :] = marks
 
 
 def far_kernel(
@@ -648,7 +657,8 @@
     send_ref,
     value_ref,
 ):
-    count = entry_ref[4, 0]
+    rows = out_ref.shape[0]
+    count = jnp.where(jnp.max(near_ref[rows:, :]) > 0.0, 0, entry_ref[4, 0])
 
     def step(turn, acc):
         ids = []
@@ -672,7 +682,7 @@
 
     steps = (count + BLOCK_STEP - 1) // BLOCK_STEP
     acc = lax.fori_loop(0, steps, step, jnp.zeros((6 * GROUP, LANES), F32))
-    out_ref[...] = near_ref[...] + fold_terms(acc)
+    out_ref[...] = near_ref[:rows, :] + fold_terms(acc)
     send_faces(own_ref[0], grid, out_ref, chunks, faces_ref, send_ref, value_ref)
 
 
@@ -853,9 +863,7 @@
     return results
 
 
-def assemble_kernel(
-    slots, chunks, grid, own_ref, back_ref, ids_ref, inner_ref, faces_ref, out_ref, send_ref, value_ref
-):
+def assemble_kernel(slots, back_ref, ids_ref, inner_ref, out_ref):
     devices = back_ref.shape[0]
 
     def step(turn, acc):
@@ -871,7 +879,6 @@
 
     acc = lax.fori_loop(0, devices, step, jnp.zeros((6 * GROUP, LANES), F32))
     out_ref[...] = inner_ref[...] + fold_terms(acc)
-    send_faces(own_ref[0], grid, out_ref, chunks, faces_ref, send_ref, value_ref)
 
 
 def final_kernel(
@@ -1025,33 +1032,25 @@
     )
     inbound = to_all(outbound)
     inbound, map_low, map_high = lax.optimization_barrier((inbound, map_low, map_high))
-    over = jnp.max(inbound[:, SEND_ROWS - 1, 0]) > 0.0
-
-    def by_tasks():
-        back, forces = call(
-            work_kernel,
-            [((devices, BACK_ROWS, LANES), F32), ((2 * TASKS * 8, LANES), F32)],
-            (0, 1),
-            (own, tasks, inbound, fields),
-            [
-                pltpu.VMEM((10, TASKS, LANES), F32),
-                pltpu.VMEM((3, TASKS * 8, LANES), F32),
-                pltpu.VMEM((3, TASKS * 8, LANES), F32),
-                pltpu.VMEM((3, TASKS * 8, LANES), F32),
-                pltpu.VMEM((2, TASKS * 8, LANES), F32),
-            ],
-        )
-        returned = to_all(back)
-        [near] = call(
-            near_kernel, [total_shape], (0,), (near_list, surf_nodes, forces, internal)
-        )
-        return call(
-            functools.partial(far_kernel, chunks, grid),
-            [total_shape, send_shape],
-            (0, 1),
-            (own, entries, returned, surf_nodes, normals, near, faces),
-            [pltpu.VMEM((4,) + face_shape[0], F32)],
-        )
+    back, forces, over = call(
+        work_kernel,
+        [
+            ((devices, BACK_ROWS, LANES), F32),
+            ((2 * TASKS * 8 + 8, LANES), F32),
+            ((1,), jnp.int32),
+        ],
+        (0, 1),
+        (own, tasks, inbound, fields),
+        [
+            pltpu.VMEM((10, TASKS, LANES), F32),
+            pltpu.VMEM((3, TASKS * 8, LANES), F32),
+            pltpu.VMEM((3, TASKS * 8, LANES), F32),
+            pltpu.VMEM((3, TASKS * 8, LANES), F32),
+            pltpu.VMEM((2, TASKS * 8, LANES), F32),
+        ],
+        (2,),
+    )
+    returned = to_all(back)
 
     def by_owners():
         [index] = call(
@@ -1074,14 +1073,26 @@
             [pltpu.VMEM((pairs * 8, LANES), F32)] * 4,
         )
         return call(
-            functools.partial(assemble_kernel, slots, chunks, grid),
-            [total_shape, send_shape],
-            (0,),
-            (own, to_all(forces), ids, internal, faces),
-            [pltpu.VMEM((4,) + face_shape[0], F32)],
-        )
-
-    total, send = lax.cond(over, by_owners, by_tasks)
+            functools.partial(assemble_kernel, slots),
+            [total_shape],
+            (),
+            (to_all(forces), ids, internal),
+        )[0]
+
+    whole = lax.cond(over[0] > 0, by_owners, lambda: internal)
+    [near] = call(
+        near_kernel,
+        [((3 * GROUP + 8, LANES), F32)],
+        (0,),
+        (near_list, surf_nodes, forces, internal, whole),
+    )
+    total, send = call(
+        functools.partial(far_kernel, chunks, grid),
+        [total_shape, send_shape],
+        (0, 1),
+        (own, entries, returned, surf_nodes, normals, near, faces),
+        [pltpu.VMEM((4,) + face_shape[0], F32)],
+    )
     [result] = call(
         functools.partial(final_kernel, grid),
         [((3, node_count), F32)],

time: 74 us -> 74.2 us (level)
  Pallas kernels: 24.7 us -> 27.1 us
  waiting for transfers between devices: 17.9 us -> 16.8 us
  starting transfers between devices: 16.7 us -> 15.9 us
    pallas_call x10, Pallas kernels: 24.7 us -> 27.1 us  [call(): pl.pallas_call(kernel, out_shape=[jax.ShapeDtypeStruct(shape, dtype) for...]
    all_to_all x3, waiting for transfers between devices: 17.9 us -> 16.8 us  [to_all(): return lax.all_to_all(values, axes, split_axis=0, concat_axis=0, tiled=True)]
  transfers between devices with their start and end apart: 5 -> 5, of which waited for: 3 -> 3; matrix products, arithmetic and copies ran while one was open for 3% -> 3% of each run, Pallas kernels for 15% -> 16%
where the time goes in v4:
time: 74.2 us; the launch traced here: 73.6 us
  Pallas kernels  27.1 us (37%)
  waiting for transfers between devices  16.8 us (23%)
  starting transfers between devices  15.9 us (21%)
  blocking collectives  9.93 us (13%)
  local copies, waits for them, and re-layouts  2.12 us (3%)
  between operations  1.65 us (2%)
    pallas_call x10, Pallas kernels, call(): pl.pallas_call(kernel, out_shape=[jax.ShapeDtypeStruct(shape, dtype) for...  27.1 us
    all_to_all x3, waiting for transfers between devices, to_all(): return lax.all_to_all(values, axes, split_axis=0, concat_axis=0, tiled=True)  16.8 us
    all_to_all x3, starting transfers between devices, to_all(): return lax.all_to_all(values, axes, split_axis=0, concat_axis=0, tiled=True)  12.6 us
    all_to_all x1, blocking collectives, to_all(): return lax.all_to_all(values, axes, split_axis=0, concat_axis=0, tiled=True)  9.93 us
    ppermute x1, starting transfers between devices, exchange(): lax.ppermute(high, axis, forward)  2.02 us
  transfers between devices with their start and end apart: 5, of which 3 were waited for; matrix products, arithmetic and copies ran while one was open for 3% of the time, Pallas kernels for 16%

profile of v4, /device:TPU:0, one launch (start us, length us, event | category | flops | bytes accessed | tf_op | source)
XLA Modules:
  0.0 73.6 jit_solution(17045012053853295947)
XLA Ops:
  0.7 2.3 %shard_map.136 = s32[32,16,128]{2,1,0:T(8,128)} custom-call(s32[1]{0:T(128)} %bitcast.own_ref, s32[1]{0:T(128)S(6)} %copy.18.count_ref, s32[64,128]{1,0:T(8,128)} %bitcast.10, s32[2,64]{1,0:T(2,128)} %pairs_ref.1, s32[2,64,128]{2,1,0:T(8,128)} %masks_ref.1), custom_call_target="tpu_custom_call" | custom-call | tf_op jit(solution)/shard_map/pallas_call | solution.py:926
  3.0 7.3 %all-to-all-start.2 = ((s32[32,16,128]{2,1,0:T(8,128)}), s32[32,16,128]{2,1,0:T(8,128)S(1)}, u32[]{:S(2)}, u32[]{:S(2)}) async-start(s32[32,16,128]{2,1,0:T(8,128)} %shard_map.136), calls=%async_computation.2 | async-start | bytes 524288 | tf_op jit(solution)/shard_map/all_to_all | solution.py:979
  10.3 0.8 %dynamic_slice.3.owners_ref = s32[256]{0:T(256)S(1)} dynamic-slice(s32[8192]{0:T(1024)} %param.26, s32[]{:T(128)S(6)} %select_n.3), dynamic_slice_sizes={256} | dynamic-slice | bytes 2052 | tf_op jit(solution)/shard_map/dynamic_slice | solution.py:988
  11.1 1.3 %copy.15.ref_ref = f32[256,3,128]{2,1,0:T(4,128)S(1)} copy(f32[256,3,128]{2,0,1:T(8,128)} %param.24) | data formatting | bytes 786432 | tf_op args[8]
  12.4 0.0 copy-start.3
  12.4 0.0 copy-start.5
  12.5 4.6 %shard_map.137 = (f32[3,256,128]{2,1,0:T(8,128)S(1)}, f32[3,256,128]{2,1,0:T(8,128)S(1)}, s32[512]{0:T(512)S(1)}) custom-call(s32[256]{0:T(256)S(1)} %dynamic_slice.3.owners_ref, f32[3,1408]{1,0:T(4,128)S(1)} %copy-done, s32[256,128]{1,0:T(8,128)S(1)} %copy-done.7, f32[256,3,128]{2,1,0:T(4,128)S(1)} %copy.15.ref_ref, f32[256,2,128]{2,1,0:T(2,128)S(1)} %copy-done.6), custom_call_target="tpu_custom_call" | custom-call | tf_op jit(solution)/shard_map/pallas_call | solution.py:926
  17.1 3.9 %all-to-all-done.2.request_ref = s32[32,16,128]{2,1,0:T(8,128)S(1)} async-done(((s32[32,16,128]{2,1,0:T(8,128)}), s32[32,16,128]{2,1,0:T(8,128)S(1)}, u32[]{:S(2)}, u32[]{:S(2)}) %all-to-all-start.2) | async-done | bytes 262176 | tf_op jit(solution)/shard_map/all_to_all | solution.py:979
  21.0 4.0 %shard_map.138 = (f32[32,32,128]{2,1,0:T(8,128)}, s32[8,160]{1,0:T(8,128)S(1)}) custom-call(s32[32,128]{1,0:T(8,128)S(1)} %bitcast.6, s32[512]{0:T(512)S(1)} %get-tuple-element.56.block_ref, f32[3,256,128]{2,1,0:T(8,128)S(1)} %get-tuple-element.57.pos_ref, f32[256,2,128]{2,1,0:T(2,128)S(1)} %copy-done.6), custom_call_target="tpu_custom_call" | custom-call | tf_op jit(solution)/shard_map/pallas_call | solution.py:926
  24.9 0.0 copy-start.9
  25.0 2.8 %all-to-all-start.3 = ((f32[32,32,128]{2,1,0:T(8,128)}), f32[32,32,128]{2,1,0:T(8,128)S(1)}, u32[]{:S(2)}, u32[]{:S(2)}) async-start(f32[32,32,128]{2,1,0:T(8,128)} %get-tuple-element.60), calls=%async_computation.3 | async-start | bytes 1048576 | tf_op jit(solution)/shard_map/all_to_all | solution.py:979
  27.7 0.3 shard_map.140
  28.1 2.0 %collective-permute-start = (f32[8,128]{1,0:T(8,128)S(1)}, f32[8,128]{1,0:T(8,128)S(1)}, u32[]{:S(2)}, u32[]{:S(2)}) collective-permute-start(f32[8,128]{1,0:T(8,128)S(1)} %get-tuple-element.61), channel_id=1, source_target_pairs={{0,1},{1,2},{2,3},{3,4},{4,5},{5,6},{6,7},{8,9},{9,10},{10,11},{11... | collective-permute-start | bytes 12296 | tf_op jit(solution)/shard_map/ppermute | solution.py:940
  30.1 1.3 %collective-permute-start.1 = (f32[8,128]{1,0:T(8,128)S(1)}, f32[8,128]{1,0:T(8,128)S(1)}, u32[]{:S(2)}, u32[]{:S(2)}) collective-permute-start(f32[8,128]{1,0:T(8,128)S(1)} %get-tuple-element.62), channel_id=1, source_target_pairs={{1,0},{2,1},{3,2},{4,3},{5,4},{6,5},{7,6},{9,8},{10,9},{11,10},{12... | collective-permute-start | bytes 12296 | tf_op jit(solution)/shard_map/ppermute | solution.py:940
  31.4 1.9 %shard_map.142.inner_ref = f32[48,128]{1,0:T(8,128)S(1)} custom-call(s32[8,1024]{1,0:T(8,128)S(1)} %copy-done.1, f32[3,1408]{1,0:T(4,128)S(1)} %copy-done.3, f32[3,1408]{1,0:T(4,128)S(1)} %copy-done, f32[8,128]{1,0:T(8,128)S(1)} %bitcast.9), custom_call_target="tpu_custom_call" | custom-call | tf_op jit(solution)/shard_map/pallas_call | solution.py:926
  33.3 3.5 %shard_map.139 = (s32[8,48]{1,0:T(8,128)S(1)}, s32[8,96]{1,0:T(8,128)S(1)}, f32[10,48,128]{2,1,0:T(8,128)S(1)}) custom-call(s32[1]{0:T(128)} %bitcast.own_ref, s32[32,128]{1,0:T(8,128)S(1)} %bitcast.7, s32[512]{0:T(512)S(1)} %get-tuple-element.56.block_ref, s32[32,16,128]{2,1,0:T(8,128)S(1)} %all-to-all-done.2.request_ref, ...), custom_call_target="tpu_custom_call" | custom-call | tf_op jit(solution)/shard_map/pallas_call | solution.py:926
  36.8 6.4 %all-to-all-done.3.in_ref = f32[32,32,128]{2,1,0:T(8,128)S(1)} async-done(((f32[32,32,128]{2,1,0:T(8,128)}), f32[32,32,128]{2,1,0:T(8,128)S(1)}, u32[]{:S(2)}, u32[]{:S(2)}) %all-to-all-start.3) | async-done | bytes 524320 | tf_op jit(solution)/shard_map/all_to_all | solution.py:979
  43.3 5.5 %shard_map.141 = (f32[32,8,128]{2,1,0:T(8,128)}, f32[776,128]{1,0:T(8,128)S(1)}, s32[1]{0:T(128)}) custom-call(s32[1]{0:T(128)} %bitcast.own_ref, s32[8,48]{1,0:T(8,128)S(1)} %get-tuple-element.59.task_ref, f32[32,32,128]{2,1,0:T(8,128)S(1)} %all-to-all-done.3.in_ref, f32[10,48,128]{2,1,0:T(8,128)S(1)} %get-tuple-element.64.start_ref), custom_call_target="tpu_custom_call" | custom-call | tf_op jit(solution)/shard_map/pallas_call | solution.py:926
  49.5 2.6 %all-to-all-start.4 = ((f32[32,8,128]{2,1,0:T(8,128)}), f32[32,8,128]{2,1,0:T(8,128)S(1)}, u32[]{:S(2)}, u32[]{:S(2)}) async-start(f32[32,8,128]{2,1,0:T(8,128)} %get-tuple-element.65), calls=%async_computation.4 | async-start | bytes 262144 | tf_op jit(solution)/shard_map/all_to_all | solution.py:979
  52.1 1.7 %shard_map.143.near_ref = f32[56,128]{1,0:T(8,128)S(1)} custom-call(s32[8,96]{1,0:T(8,128)S(1)} %get-tuple-element.67.near_ref, s32[256,128]{1,0:T(8,128)S(1)} %copy-done.7, f32[776,128]{1,0:T(8,128)S(1)} %get-tuple-element.68.force_ref, f32[48,128]{1,0:T(8,128)S(1)} %shard_map.142.inner_ref, f32[48,128]{1,0:T(8,128)S(1)} %get-tuple-element.74.whole_ref), custom_call_target="tpu_custom_call" | custom-call | tf_op jit(solution)/shard_map/pallas_call | solution.py:926
  53.8 6.5 %all-to-all-done.4.back_ref = f32[32,8,128]{2,1,0:T(8,128)S(1)} async-done(((f32[32,8,128]{2,1,0:T(8,128)}), f32[32,8,128]{2,1,0:T(8,128)S(1)}, u32[]{:S(2)}, u32[]{:S(2)}) %all-to-all-start.4) | async-done | bytes 131104 | tf_op jit(solution)/shard_map/all_to_all | solution.py:979
  60.3 2.4 %shard_map.144 = (f32[48,128]{1,0:T(8,128)S(1)}, f32[32,8,128]{2,1,0:T(8,128)S(1)}) custom-call(s32[1]{0:T(128)} %bitcast.own_ref, s32[8,160]{1,0:T(8,128)S(1)} %get-tuple-element.58.entry_ref, f32[32,8,128]{2,1,0:T(8,128)S(1)} %all-to-all-done.4.back_ref, s32[256,128]{1,0:T(8,128)S(1)} %copy-done.7, f32[3,256,128]{2,1,0:T(8,128)S(1)} %get-tuple-element.66.normal_ref, ...), custom_call_target="tpu_custom_call" | custom-call | tf_op jit(solution)/shard_map/pallas_call | solution.py:926
  62.8 9.9 %all_to_all.29.got_ref = f32[32,8,128]{2,1,0:T(8,128)S(1)} all-to-all(f32[32,8,128]{2,1,0:T(8,128)S(1)} %get-tuple-element.71), channel_id=1, replica_groups=mesh['gx'=4,'gy'=8] {'gx','gy'}, dimensions={0} | all-to-all | bytes 262144 | tf_op jit(solution)/shard_map/all_to_all | solution.py:979
  72.7 0.9 %shard_map.145 = f32[3,1408]{1,0:T(4,128)} custom-call(s32[1]{0:T(128)} %bitcast.own_ref, f32[48,128]{1,0:T(8,128)S(1)} %get-tuple-element.70.total_ref, f32[32,8,128]{2,1,0:T(8,128)S(1)} %all_to_all.29.got_ref, f32[8,128]{1,0:T(8,128)S(1)} %collective-permute-done.low_ref, f32[8,128]{1,0:T(8,128)S(1)} %collective-permute-done.1.high_ref, ...), custom_call_target="tpu_custom_call" | custom-call | tf_op jit(solution)/shard_map/pallas_call | solution.py:926
  (27 shorter events, 0.1 us)
Async XLA Ops:
  0.0 12.4 %copy-start = (f32[3,1408]{1,0:T(4,128)S(1)}, f32[3,1408]{1,0:T(4,128)}, u32[]{:S(2)}) copy-start(f32[3,1408]{1,0:T(4,128)} %disp_ref.3) | copy-start | bytes 50692
  0.0 12.4 %copy-start.7 = (s32[256,128]{1,0:T(8,128)S(1)}, s32[256,128]{1,0:T(8,128)}, u32[]{:S(2)}) copy-start(s32[256,128]{1,0:T(8,128)} %nodes_ref.5) | copy-start | bytes 393220
  0.0 12.4 %copy-start.6 = (f32[256,2,128]{2,1,0:T(2,128)S(1)}, f32[256,2,128]{2,1,0:T(2,128)}, u32[]{:S(2)}) copy-start(f32[256,2,128]{2,1,0:T(2,128)} %angles_ref.5) | copy-start | bytes 786436
  3.0 17.9 %all-to-all-start.2 = ((s32[32,16,128]{2,1,0:T(8,128)}), s32[32,16,128]{2,1,0:T(8,128)S(1)}, u32[]{:S(2)}, u32[]{:S(2)}) async-start(s32[32,16,128]{2,1,0:T(8,128)} %shard_map.136), calls=%async_computation.2 | async-start | bytes 524288 | tf_op jit(solution)/shard_map/all_to_all | solution.py:979
  12.4 15.3 %copy-start.11 = (s32[4,153]{1,0:T(4,128)S(1)}, s32[4,153]{1,0:T(4,128)}, u32[]{:S(2)}) copy-start(s32[4,153]{1,0:T(4,128)} %param.17) | copy-start | bytes 7348
  12.4 19.0 %copy-start.1 = (s32[8,1024]{1,0:T(8,128)S(1)}, s32[8,1024]{1,0:T(8,128)}, u32[]{:S(2)}) copy-start(s32[8,1024]{1,0:T(8,128)} %conn_ref.1) | copy-start | bytes 98308
  12.4 19.0 %copy-start.3 = (f32[3,1408]{1,0:T(4,128)S(1)}, f32[3,1408]{1,0:T(4,128)}, u32[]{:S(2)}) copy-start(f32[3,1408]{1,0:T(4,128)} %coords_ref.1) | copy-start | bytes 50692
  12.4 19.0 %copy-start.5 = (f32[1024]{0:T(1024)S(1)}, f32[1024]{0:T(1024)}, u32[]{:S(2)}) copy-start(f32[1024]{0:T(1024)} %param.22) | copy-start | bytes 12292
  24.9 24.5 %copy-start.8 = (s32[8192]{0:T(1024)S(1)}, s32[8192]{0:T(1024)}, u32[]{:S(2)}) copy-start(s32[8192]{0:T(1024)} %param.26) | copy-start | bytes 98308
  24.9 24.5 %copy-start.9 = (s32[2,64,128]{2,1,0:T(8,128)S(1)}, s32[2,64,128]{2,1,0:T(8,128)}, u32[]{:S(2)}) copy-start(s32[2,64,128]{2,1,0:T(8,128)} %masks_ref.1) | copy-start | bytes 196612
  24.9 24.5 %copy-start.10 = (s32[2,64]{1,0:T(2,128)S(1)}, s32[2,64]{1,0:T(2,128)}, u32[]{:S(2)}) copy-start(s32[2,64]{1,0:T(2,128)} %pairs_ref.1) | copy-start | bytes 1540
  25.0 18.3 %all-to-all-start.3 = ((f32[32,32,128]{2,1,0:T(8,128)}), f32[32,32,128]{2,1,0:T(8,128)S(1)}, u32[]{:S(2)}, u32[]{:S(2)}) async-start(f32[32,32,128]{2,1,0:T(8,128)} %get-tuple-element.60), calls=%async_computation.3 | async-start | bytes 1048576 | tf_op jit(solution)/shard_map/all_to_all | solution.py:979
  28.1 8.8 %collective-permute-start = (f32[8,128]{1,0:T(8,128)S(1)}, f32[8,128]{1,0:T(8,128)S(1)}, u32[]{:S(2)}, u32[]{:S(2)}) collective-permute-start(f32[8,128]{1,0:T(8,128)S(1)} %get-tuple-element.61), channel_id=1, source_target_pairs={{0,1},{1,2},{2,3},{3,4},{4,5},{5,6},{6,7},{8,9},{9,10},{10,11},{11... | collective-permute-start | bytes 12296 | tf_op jit(solution)/shard_map/ppermute | solution.py:940
  30.1 6.7 %collective-permute-start.1 = (f32[8,128]{1,0:T(8,128)S(1)}, f32[8,128]{1,0:T(8,128)S(1)}, u32[]{:S(2)}, u32[]{:S(2)}) collective-permute-start(f32[8,128]{1,0:T(8,128)S(1)} %get-tuple-element.62), channel_id=1, source_target_pairs={{1,0},{2,1},{3,2},{4,3},{5,4},{6,5},{7,6},{9,8},{10,9},{11,10},{12... | collective-permute-start | bytes 12296 | tf_op jit(solution)/shard_map/ppermute | solution.py:940
  49.5 23.2 %copy-start.2 = (f32[3,1408]{1,0:T(4,128)S(1)}, f32[3,1408]{1,0:T(4,128)}, u32[]{:S(2)}) copy-start(f32[3,1408]{1,0:T(4,128)} %velocity_ref.1) | copy-start | bytes 50692
  49.5 23.2 %copy-start.4 = (f32[1408]{0:T(1024)S(1)}, f32[1408]{0:T(1024)}, u32[]{:S(2)}) copy-start(f32[1408]{0:T(1024)} %param.21) | copy-start | bytes 16900
  49.5 10.8 %all-to-all-start.4 = ((f32[32,8,128]{2,1,0:T(8,128)}), f32[32,8,128]{2,1,0:T(8,128)S(1)}, u32[]{:S(2)}, u32[]{:S(2)}) async-start(f32[32,8,128]{2,1,0:T(8,128)} %get-tuple-element.65), calls=%async_computation.4 | async-start | bytes 262144 | tf_op jit(solution)/shard_map/all_to_all | solution.py:979

commit v5 on v4

--- a/solution.py
+++ b/solution.py
@@ -32,13 +32,15 @@
 F32 = jnp.float32
 BF16 = jnp.bfloat16
 VMEM_LIMIT = 48 * 1024 * 1024
-REQUEST_ROWS = 16
-TASK_CAP = 7
+REQUEST_ROWS = 8
+TASK_CAP = 3
+OWN_CAP = 12
 TASK_LANE = 64
+TASK_FIELDS = 5
 ENTRY_LANE = 4
 ENTRY_CAP = 20
 SEND_ROWS = 32
-BACK_ROWS = 8
+BACK_ROWS = 10
 ENTRIES = 160
 TASKS = 48
 TASK_STEP = 8
@@ -75,6 +77,10 @@
     rest = x - high.astype(F32)
     mid = rest.astype(BF16)
     return high, mid, (rest - mid.astype(F32)).astype(BF16)
+
+
+def span_of(row):
+    return pl.ds(pl.multiple_of(row * LANES, LANES), LANES)
 
 
 def strict_upper(size):
@@ -171,12 +177,17 @@
     def pick(target, keep):
         return jnp.where((device == target) & keep, 1.0, 0.0)
 
+    def turns(worker):
+        tasks = pick(worker, live)
+        ahead = dot_nn(tasks.astype(BF16), earlier)
+        return tasks, jnp.sum(tasks * ahead, axis=0, keepdims=True)
+
     worker = jnp.where(lane == 0, me, slave)
-    tasks = pick(worker, live)
-    turn = jnp.sum(tasks * dot_nn(tasks.astype(BF16), earlier), axis=0, keepdims=True)
-    worker = jnp.where(turn >= TASK_CAP, me, worker)
-    tasks = pick(worker, live)
-    turn = jnp.sum(tasks * dot_nn(tasks.astype(BF16), earlier), axis=0, keepdims=True)
+    for other in (master, me):
+        tasks, turn = turns(worker)
+        worker = jnp.where((turn >= TASK_CAP) & (worker != me), other, worker)
+    tasks, turn = turns(worker)
+    room = turn < jnp.where(worker == me, float(OWN_CAP), float(TASK_CAP))
     send_slave = live & (slave != worker)
     send_master = live & (master != worker)
     from_slave = pick(slave, send_slave)
@@ -203,12 +214,15 @@
     )
     line = line + dot_nt(from_master.astype(BF16), entry)
     entry = placed(
-        TASK_LANE + 4 * turn, (slave, slave_rank, master, master_rank), turn < TASK_CAP
+        TASK_LANE + TASK_FIELDS * turn,
+        (slave, slave_rank, master, master_rank, lane.astype(F32)),
+        room,
     )
     line = line + dot_nt(tasks.astype(BF16), entry)
     entry_count = jnp.sum(both, axis=1, keepdims=True)
     task_count = jnp.sum(tasks, axis=1, keepdims=True)
-    over = jnp.where((entry_count > ENTRY_CAP) | (task_count > TASK_CAP), 1.0, 0.0)
+    limit = jnp.where(iota((devices, 1), 0) == own, float(OWN_CAP), float(TASK_CAP))
+    over = jnp.where((entry_count > ENTRY_CAP) | (task_count > limit), 1.0, 0.0)
     over = jnp.max(over, axis=0, keepdims=True)
     spot = iota((devices, LANES), 1)
     line = jnp.where(spot == 0, entry_count, line)
@@ -228,23 +242,26 @@
 
 
 def segment_kernel(
-    cap, owners_ref, disp_ref, nodes_ref, ref_ref, angles_ref, pos_ref, normal_ref, block_ref, seen_ref
+    cap,
+    rows_per,
+    own_ref,
+    map_ref,
+    disp_ref,
+    nodes_ref,
+    ref_ref,
+    pos_ref,
+    block_ref,
+    group_ref,
+    sem,
 ):
     chunks = disp_ref.shape[1] // LANES
-
-    def clear(device, carry):
-        seen_ref[device] = 0
-        return carry
-
-    lax.fori_loop(0, seen_ref.shape[0], clear, 0)
+    first = own_ref[0] * rows_per
+    start = pl.multiple_of(first // 8 * 8, 8)
+    move = pltpu.make_async_copy(map_ref.at[pl.ds(start, 8), :], group_ref, sem)
+    move.start()
 
     def step(turn, carry):
         base = pl.multiple_of(turn * 8, 8)
-        for k in range(8):
-            owner = owners_ref[base + k]
-            rank = seen_ref[owner]
-            block_ref[owner * cap + rank] = base + k
-            seen_ref[owner] = rank + 1
         ids = nodes_ref[pl.ds(base, 8), :]
         found = gather_chunks(
             lambda field, chunk: disp_ref[field : field + 1, chunk * LANES : (chunk + 1) * LANES],
@@ -253,15 +270,28 @@
             ids,
         )
         for field in range(3):
-            pos_ref[field, pl.ds(base, 8), :] = found[field] + ref_ref[pl.ds(base, 8), field, :]
-        sin_az, cos_az = sine_cosine(angles_ref[pl.ds(base, 8), 0, :])
-        sin_pol, cos_pol = sine_cosine(angles_ref[pl.ds(base, 8), 1, :])
-        normal_ref[0, pl.ds(base, 8), :] = cos_az * cos_pol
-        normal_ref[1, pl.ds(base, 8), :] = sin_az * cos_pol
-        normal_ref[2, pl.ds(base, 8), :] = sin_pol
+            pos_ref[field, pl.ds(base, 8), :] = found[field] + ref_ref[field, pl.ds(base, 8), :]
         return carry
 
     lax.fori_loop(0, nodes_ref.shape[0] // 8, step, 0, unroll=2)
+    move.wait()
+    owner = jnp.concatenate(
+        [group_ref[pl.ds(first - start + i, 1), :] for i in range(rows_per)], axis=1
+    )
+    blocks = owner.shape[1]
+    total = block_ref.shape[0] * LANES
+    mine = iota((total // cap, blocks), 0) == owner
+    before = dot_nn(as_bf16(mine), strict_upper(blocks))
+    rank = jnp.sum(jnp.where(mine, before, 0.0), axis=0, keepdims=True).astype(jnp.int32)
+    hit = as_bf16(iota((total, blocks), 0) == owner * cap + rank)
+    high, rest = split2(iota((8, blocks), 1).astype(F32))
+    table = (dot_nt(high, hit) + dot_nt(rest, hit)).astype(jnp.int32)
+    for row in range(total // LANES):
+        block_ref[row : row + 1, :] = table[0:1, row * LANES : (row + 1) * LANES]
+
+
+def block_at(block_ref, slot):
+    return block_ref[slot >> 7, slot & (LANES - 1)]
 
 
 def plan_kernel(cap, list_ref, block_ref, pos_ref, angles_ref, out_ref, entry_ref, used_ref):
@@ -279,7 +309,7 @@
             number, over = state
             at = ENTRY_LANE + 3 * turn
             role = list_ref[owner, at]
-            block = block_ref[owner * cap + list_ref[owner, at + 1]]
+            block = block_at(block_ref, owner * cap + list_ref[owner, at + 1])
             worker = list_ref[owner, at + 2]
             first = used_ref[0, worker]
             back = used_ref[1, worker]
@@ -325,6 +355,7 @@
     list_ref,
     block_ref,
     request_ref,
+    masks_ref,
     pos_ref,
     angles_ref,
     task_ref,
@@ -345,12 +376,13 @@
 
     def from_owner(owner, carry):
         def task(turn, state):
-            at = TASK_LANE + 4 * turn
+            at = TASK_LANE + TASK_FIELDS * turn
+            pair = list_ref[owner, at + 4]
             number, near = state
             for side in range(2):
                 source = list_ref[owner, at + 2 * side]
                 here = source == own
-                block = block_ref[owner * cap + list_ref[owner, at + 2 * side + 1]]
+                block = block_at(block_ref, owner * cap + list_ref[owner, at + 2 * side + 1])
                 used = used_ref[0, source]
                 back = used_ref[1, source]
                 used_ref[0, source] = jnp.where(here, used, used + 3 + 2 * side)
@@ -359,9 +391,17 @@
                 task_ref[3 * side + 1, number] = jnp.where(here, block, jnp.minimum(used, SEND_ROWS - 5))
                 task_ref[3 * side + 2, number] = back
                 base = 4 * side
-                field_ref[base + 3, pl.ds(number, 1), :] = request_ref[
-                    owner, pl.ds(1 + 2 * turn + side, 1), :
-                ].astype(F32)
+
+                @pl.when(owner == own)
+                def _():
+                    mask = masks_ref[side, pl.ds(pair, 1), :]
+                    field_ref[base + 3, pl.ds(number, 1), :] = mask.astype(F32)
+
+                @pl.when(owner != own)
+                def _():
+                    mask = request_ref[owner, pl.ds(1 + 2 * turn + side, 1), :]
+                    field_ref[base + 3, pl.ds(number, 1), :] = mask.astype(F32)
+
                 spot = near
 
                 @pl.when(here)
@@ -381,7 +421,7 @@
             return (number + 1, near)
 
         number, near = carry
-        count = jnp.minimum(list_ref[owner, 1], TASK_CAP)
+        count = jnp.minimum(list_ref[owner, 1], jnp.where(owner == own, OWN_CAP, TASK_CAP))
         count = jnp.minimum(count, TASKS - number)
         return lax.fori_loop(0, count, task, (number, near))
 
@@ -608,18 +648,20 @@
             @pl.when(live & (slave_from != own))
             def _():
                 for k in range(3):
-                    back_ref[slave_from, pl.ds(task_ref[2, task] + k, 1), :] = on_slave[k : k + 1]
+                    back_ref[slave_from, :, span_of(task_ref[2, task] + k)] = on_slave[k : k + 1]
 
             @pl.when(live & (master_from != own))
             def _():
-                back_ref[master_from, pl.ds(task_ref[5, task], 1), :] = total
+                back_ref[master_from, :, span_of(task_ref[5, task])] = total
 
         return carry
 
     lax.fori_loop(0, (count + TASK_STEP - 1) // TASK_STEP, tile, 0)
 
 
-def near_kernel(near_ref, nodes_ref, force_ref, inner_ref, whole_ref, out_ref):
+def near_kernel(
+    near_ref, nodes_ref, force_ref, inner_ref, whole_ref, angles_ref, out_ref, normal_ref
+):
     count = near_ref[2, 0]
 
     def step(turn, acc):
@@ -641,6 +683,17 @@
     rows = total.shape[0]
     out_ref[:rows, :] = jnp.where(marks[0:1] > 0.0, whole_ref[...], total)
     out_ref[rows:, :] = marks
+
+    def turn_angles(turn, carry):
+        at = pl.ds(pl.multiple_of(turn * 8, 8), 8)
+        sin_az, cos_az = sine_cosine(angles_ref[at, 0, :])
+        sin_pol, cos_pol = sine_cosine(angles_ref[at, 1, :])
+        normal_ref[0, at, :] = cos_az * cos_pol
+        normal_ref[1, at, :] = sin_az * cos_pol
+        normal_ref[2, at, :] = sin_pol
+        return carry
+
+    lax.fori_loop(0, nodes_ref.shape[0] // 8, turn_angles, 0, unroll=4)
 
 
 def far_kernel(
@@ -671,10 +724,10 @@
             worker = entry_ref[2, number]
             first = entry_ref[3, number]
             ids.append(nodes_ref[pl.ds(block, 1), :])
-            total = back_ref[worker, pl.ds(first, 1), :]
+            total = back_ref[worker, :, span_of(first)]
             rows = []
             for field in range(3):
-                row = back_ref[worker, pl.ds(jnp.minimum(first + field, BACK_ROWS - 1), 1), :]
+                row = back_ref[worker, :, span_of(jnp.minimum(first + field, BACK_ROWS - 1))]
                 row = jnp.where(role == 1, -normal_ref[field, pl.ds(block, 1), :] * total, row)
                 rows.append(jnp.where(valid, row, 0.0))
             forces.append(rows)
@@ -818,7 +871,9 @@
 
         @pl.when(there)
         def _():
-            send_ref[target] = value_ref[face_toward(dx, dy)]
+            for row in range(3 * parts):
+                span = slice(row * LANES, (row + 1) * LANES)
+                send_ref[target, :, span] = value_ref[face_toward(dx, dy), row : row + 1, :]
 
 
 def face_map_kernel(chunks, faces_ref, low_ref, high_ref, table_ref):
@@ -889,19 +944,20 @@
 
     def block(dx, dy):
         there, source = neighbour(own, grid, dx, dy)
-        return jnp.where(there, got_ref[source], 0.0)
-
-    def rows_of(values):
-        return [values[at : at + 1] for at in range(3 * parts)]
+        spans = [slice(row * LANES, (row + 1) * LANES) for row in range(3 * parts)]
+        return [jnp.where(there, got_ref[source, :, span], 0.0) for span in spans]
 
     def side(dy, map_ref):
-        rows = rows_of(block(0, dy))
+        rows = block(0, dy)
         for field, dx in enumerate((-1, 1)):
             places = [map_ref[field * parts + p : field * parts + p + 1, :] for p in range(parts)]
-            rows = [a + b for a, b in zip(rows, moved_faces(block(dx, dy), places, parts))]
+            corner = block(dx, dy)
+            corner = corner + [jnp.zeros((1, LANES), F32)] * (-len(corner) % 8)
+            moved = moved_faces(jnp.concatenate(corner, axis=0), places, parts)
+            rows = [a + b for a, b in zip(rows, moved)]
         return rows
 
-    added = [rows_of(block(-1, 0)), rows_of(block(1, 0)), side(-1, low_ref), side(1, high_ref)]
+    added = [block(-1, 0), block(1, 0), side(-1, low_ref), side(1, high_ref)]
     acc = jnp.zeros((6 * GROUP, LANES), F32)
     for face, rows in enumerate(added):
         ids = [faces_ref[face : face + 1, p * LANES : (p + 1) * LANES] for p in range(parts)]
@@ -919,14 +975,16 @@
             )
 
 
-def call(kernel, outs, in_smem, args, scratch=(), out_smem=()):
-    def spec(smem):
+def call(kernel, outs, in_smem, args, scratch=(), out_smem=(), in_any=()):
+    def spec(smem, anywhere=False):
+        if anywhere:
+            return pl.BlockSpec(memory_space=pl.ANY)
         return pl.BlockSpec(memory_space=pltpu.SMEM if smem else pltpu.VMEM)
 
     return pl.pallas_call(
         kernel,
         out_shape=[jax.ShapeDtypeStruct(shape, dtype) for shape, dtype in outs],
-        in_specs=[spec(i in in_smem) for i in range(len(args))],
+        in_specs=[spec(i in in_smem, i in in_any) for i in range(len(args))],
         out_specs=[spec(i in out_smem) for i in range(len(outs))],
         scratch_shapes=list(scratch),
         compiler_params=pltpu.CompilerParams(vmem_limit_bytes=VMEM_LIMIT),
@@ -972,7 +1030,7 @@
     face_rows = -(-3 * parts // 8) * 8
     total_shape = ((3 * GROUP, LANES), F32)
     face_shape = ((face_rows, LANES), F32)
-    send_shape = ((devices, face_rows, LANES), F32)
+    send_shape = ((devices, 1, 3 * parts * LANES), F32)
     grid = (lax.axis_size("gx"), lax.axis_size("gy"))
 
     def to_all(values):
@@ -985,18 +1043,14 @@
         (own, pair_count, owners, pair_blocks, pair_masks),
     )
     asked = to_all(request)
-    own_owners = lax.dynamic_slice_in_dim(owner_map, own[0] * per_dev, per_dev)
-    pos, normals, block_of = call(
-        functools.partial(segment_kernel, slots),
-        [
-            ((3, per_dev, LANES), F32),
-            ((3, per_dev, LANES), F32),
-            ((devices * slots,), jnp.int32),
-        ],
+    pos, block_of = call(
+        functools.partial(segment_kernel, slots, rows_per),
+        [((3, per_dev, LANES), F32), ((devices * slots // LANES, LANES), jnp.int32)],
         (0,),
-        (own_owners, displacement, surf_nodes, surf_ref, surf_angles),
-        [pltpu.SMEM((devices,), jnp.int32)],
-        (2,),
+        (own, owners, displacement, surf_nodes, jnp.transpose(surf_ref, (1, 0, 2))),
+        [pltpu.VMEM((8, LANES), jnp.int32), pltpu.SemaphoreType.DMA],
+        (),
+        (1,),
     )
     [internal] = call(
         element_kernel,
@@ -1026,7 +1080,7 @@
         functools.partial(table_kernel, slots),
         [((8, TASKS), jnp.int32), ((8, 2 * TASKS), jnp.int32), ((10, TASKS, LANES), F32)],
         (0, 1, 2),
-        (own, lists, block_of, asked, pos, surf_angles),
+        (own, lists, block_of, asked, pair_masks, pos, surf_angles),
         [pltpu.SMEM((2, devices), jnp.int32)],
         (0, 1),
     )
@@ -1035,7 +1089,7 @@
     back, forces, over = call(
         work_kernel,
         [
-            ((devices, BACK_ROWS, LANES), F32),
+            ((devices, 1, BACK_ROWS * LANES), F32),
             ((2 * TASKS * 8 + 8, LANES), F32),
             ((1,), jnp.int32),
         ],
@@ -1080,11 +1134,11 @@
         )[0]
 
     whole = lax.cond(over[0] > 0, by_owners, lambda: internal)
-    [near] = call(
+    near, normals = call(
         near_kernel,
-        [((3 * GROUP + 8, LANES), F32)],
+        [((3 * GROUP + 8, LANES), F32), ((3, per_dev, LANES), F32)],
         (0,),
-        (near_list, surf_nodes, forces, internal, whole),
+        (near_list, surf_nodes, forces, internal, whole, surf_angles),
     )
     total, send = call(
         functools.partial(far_kernel, chunks, grid),

time: 74.2 us -> 72.8 us (0.981)
  waiting for transfers between devices: 16.8 us -> 14 us
  starting transfers between devices: 15.9 us -> 18.2 us
    all_to_all x3, waiting for transfers between devices: 16.8 us -> 14 us  [to_all(): return lax.all_to_all(values, axes, split_axis=0, concat_axis=0, tiled=True)]
    all_to_all x3, starting transfers between devices: 12.6 us -> 14.7 us  [to_all(): return lax.all_to_all(values, axes, split_axis=0, concat_axis=0, tiled=True)]
    dynamic_slice x1 -> x0, local copies, waits for them, and re-layouts: 0.76 us -> none  [local(): own_owners = lax.dynamic_slice_in_dim(owner_map, own[0] * per_dev, per_dev)]
    unnamed x25 -> x28, local copies, waits for them, and re-layouts: 1.33 us -> 1.79 us
  transfers between devices with their start and end apart: 5 -> 5, of which waited for: 3 -> 3; matrix products, arithmetic and copies ran while one was open for 3% -> 0% of each run, Pallas kernels for 16% -> 18%
where the time goes in v5:
time: 72.8 us; the launch traced here: 72.3 us
  Pallas kernels  26.9 us (37%)
  starting transfers between devices  18.2 us (25%)
  waiting for transfers between devices  14 us (19%)
  blocking collectives  9.75 us (13%)
  local copies, waits for them, and re-layouts  1.81 us (2%)
  between operations  1.64 us (2%)
    pallas_call x10, Pallas kernels, call(): pl.pallas_call(kernel, out_shape=[jax.ShapeDtypeStruct(shape, dtype) for...  26.9 us
    all_to_all x3, starting transfers between devices, to_all(): return lax.all_to_all(values, axes, split_axis=0, concat_axis=0, tiled=True)  14.7 us
    all_to_all x3, waiting for transfers between devices, to_all(): return lax.all_to_all(values, axes, split_axis=0, concat_axis=0, tiled=True)  14 us
    all_to_all x1, blocking collectives, to_all(): return lax.all_to_all(values, axes, split_axis=0, concat_axis=0, tiled=True)  9.75 us
    ppermute x1, starting transfers between devices, exchange(): lax.ppermute(high, axis, forward)  2.15 us
    unnamed x28, local copies, waits for them, and re-layouts  1.79 us
  transfers between devices with their start and end apart: 5, of which 3 were waited for; matrix products, arithmetic and copies ran while one was open for 0% of the time, Pallas kernels for 18%

profile of v5, /device:TPU:0, one launch (start us, length us, event | category | flops | bytes accessed | tf_op | source)
XLA Modules:
  0.0 72.3 jit_solution(4765941985523363387)
XLA Ops:
  0.7 2.4 %shard_map.136 = s32[32,8,128]{2,1,0:T(8,128)} custom-call(s32[1]{0:T(128)} %bitcast.own_ref, s32[1]{0:T(128)S(6)} %copy.17.count_ref, s32[64,128]{1,0:T(8,128)} %bitcast.12, s32[2,64]{1,0:T(2,128)} %pairs_ref.1, s32[2,64,128]{2,1,0:T(8,128)} %masks_ref.3), custom_call_target="tpu_custom_call" | custom-call | tf_op jit(solution)/shard_map/pallas_call | solution.py:984
  3.1 0.0 copy-start.7
  3.1 7.3 %all-to-all-start.2 = ((s32[32,8,128]{2,1,0:T(8,128)}), s32[32,8,128]{2,1,0:T(8,128)S(1)}, u32[]{:S(2)}, u32[]{:S(2)}) async-start(s32[32,8,128]{2,1,0:T(8,128)} %shard_map.136), calls=%async_computation.2 | async-start | bytes 262144 | tf_op jit(solution)/shard_map/all_to_all | solution.py:1037
  10.4 0.0 copy-start
  10.4 1.0 %copy-done = f32[256,3,128]{2,0,1:T(8,128)S(1)} copy-done((f32[256,3,128]{2,0,1:T(8,128)S(1)}, f32[256,3,128]{2,0,1:T(8,128)}, u32[]{:S(2)}) %copy-start) | copy-done | bytes 393240
  11.4 0.7 %copy-done.1 = f32[3,1408]{1,0:T(4,128)S(1)} copy-done((f32[3,1408]{1,0:T(4,128)S(1)}, f32[3,1408]{1,0:T(4,128)}, u32[]{:S(2)}) %copy-start.1) | copy-done | bytes 16920
  12.2 3.7 %shard_map.137 = (f32[3,256,128]{2,1,0:T(8,128)S(1)}, s32[4,128]{1,0:T(4,128)S(1)}) custom-call(s32[1]{0:T(128)} %bitcast.own_ref, s32[64,128]{1,0:T(8,128)} %bitcast.13, f32[3,1408]{1,0:T(4,128)S(1)} %copy-done.1, s32[256,128]{1,0:T(8,128)} %nodes_ref.5, f32[3,256,128]{2,1,0:T(8,128)S(1)} %bitcast.7), custom_call_target="tpu_custom_call" | custom-call | tf_op jit(solution)/shard_map/pallas_call | solution.py:984
  15.8 2.8 %all-to-all-done.2.request_ref = s32[32,8,128]{2,1,0:T(8,128)S(1)} async-done(((s32[32,8,128]{2,1,0:T(8,128)}), s32[32,8,128]{2,1,0:T(8,128)S(1)}, u32[]{:S(2)}, u32[]{:S(2)}) %all-to-all-start.2) | async-done | bytes 131104 | tf_op jit(solution)/shard_map/all_to_all | solution.py:1037
  18.7 4.1 %shard_map.138 = (f32[32,32,128]{2,1,0:T(8,128)}, s32[8,160]{1,0:T(8,128)S(1)}) custom-call(s32[32,128]{1,0:T(8,128)S(1)} %bitcast.8, s32[4,128]{1,0:T(4,128)S(1)} %get-tuple-element.57.block_ref, f32[3,256,128]{2,1,0:T(8,128)S(1)} %get-tuple-element.58.pos_ref, f32[256,2,128]{2,1,0:T(2,128)S(1)} %copy-done.8), custom_call_target="tpu_custom_call" | custom-call | tf_op jit(solution)/shard_map/pallas_call | solution.py:984
  22.8 0.0 copy-start.9
  22.8 3.1 %all-to-all-start.3 = ((f32[32,32,128]{2,1,0:T(8,128)}), f32[32,32,128]{2,1,0:T(8,128)S(1)}, u32[]{:S(2)}, u32[]{:S(2)}) async-start(f32[32,32,128]{2,1,0:T(8,128)} %get-tuple-element.61), calls=%async_computation.3 | async-start | bytes 1048576 | tf_op jit(solution)/shard_map/all_to_all | solution.py:1037
  26.0 0.3 shard_map.140
  26.3 2.2 %collective-permute-start = (f32[8,128]{1,0:T(8,128)S(1)}, f32[8,128]{1,0:T(8,128)S(1)}, u32[]{:S(2)}, u32[]{:S(2)}) collective-permute-start(f32[8,128]{1,0:T(8,128)S(1)} %get-tuple-element.62), channel_id=1, source_target_pairs={{0,1},{1,2},{2,3},{3,4},{4,5},{5,6},{6,7},{8,9},{9,10},{10,11},{11... | collective-permute-start | bytes 12296 | tf_op jit(solution)/shard_map/ppermute | solution.py:998
  28.4 1.3 %collective-permute-start.1 = (f32[8,128]{1,0:T(8,128)S(1)}, f32[8,128]{1,0:T(8,128)S(1)}, u32[]{:S(2)}, u32[]{:S(2)}) collective-permute-start(f32[8,128]{1,0:T(8,128)S(1)} %get-tuple-element.63), channel_id=1, source_target_pairs={{1,0},{2,1},{3,2},{4,3},{5,4},{6,5},{7,6},{9,8},{10,9},{11,10},{12... | collective-permute-start | bytes 12296 | tf_op jit(solution)/shard_map/ppermute | solution.py:998
  29.8 1.9 %shard_map.142.inner_ref = f32[48,128]{1,0:T(8,128)S(1)} custom-call(s32[8,1024]{1,0:T(8,128)S(1)} %copy-done.3, f32[3,1408]{1,0:T(4,128)S(1)} %copy-done.5, f32[3,1408]{1,0:T(4,128)S(1)} %copy-done.2, f32[8,128]{1,0:T(8,128)S(1)} %bitcast.11), custom_call_target="tpu_custom_call" | custom-call | tf_op jit(solution)/shard_map/pallas_call | solution.py:984
  31.7 3.5 %shard_map.139 = (s32[8,48]{1,0:T(8,128)S(1)}, s32[8,96]{1,0:T(8,128)S(1)}, f32[10,48,128]{2,1,0:T(8,128)S(1)}) custom-call(s32[1]{0:T(128)} %bitcast.own_ref, s32[32,128]{1,0:T(8,128)S(1)} %bitcast.9, s32[4,128]{1,0:T(4,128)S(1)} %get-tuple-element.57.block_ref, s32[32,8,128]{2,1,0:T(8,128)S(1)} %all-to-all-done.2.request_ref, ...), custom_call_target="tpu_custom_call" | custom-call | tf_op jit(solution)/shard_map/pallas_call | solution.py:984
  35.2 6.2 %all-to-all-done.3.in_ref = f32[32,32,128]{2,1,0:T(8,128)S(1)} async-done(((f32[32,32,128]{2,1,0:T(8,128)}), f32[32,32,128]{2,1,0:T(8,128)S(1)}, u32[]{:S(2)}, u32[]{:S(2)}) %all-to-all-start.3) | async-done | bytes 524320 | tf_op jit(solution)/shard_map/all_to_all | solution.py:1037
  41.5 3.8 %shard_map.141 = (f32[32,1,1280]{2,1,0:T(1,128)}, f32[776,128]{1,0:T(8,128)S(1)}, s32[1]{0:T(128)}) custom-call(s32[1]{0:T(128)} %bitcast.own_ref, s32[8,48]{1,0:T(8,128)S(1)} %get-tuple-element.60.task_ref, f32[32,32,128]{2,1,0:T(8,128)S(1)} %all-to-all-done.3.in_ref, f32[10,48,128]{2,1,0:T(8,128)S(1)} %get-tuple-element.65.start_ref), custom_call_target="tpu_custom_call" | custom-call | tf_op jit(solution)/shard_map/pallas_call | solution.py:984
  46.1 4.3 %all-to-all-start.4 = ((f32[32,1,1280]{2,1,0:T(1,128)}), f32[32,1,1280]{2,1,0:T(1,128)S(1)}, u32[]{:S(2)}, u32[]{:S(2)}) async-start(f32[32,1,1280]{2,1,0:T(1,128)} %get-tuple-element.66), calls=%async_computation.4 | async-start | bytes 327680 | tf_op jit(solution)/shard_map/all_to_all | solution.py:1037
  50.4 3.6 %shard_map.143 = (f32[56,128]{1,0:T(8,128)S(1)}, f32[3,256,128]{2,1,0:T(8,128)S(1)}) custom-call(s32[8,96]{1,0:T(8,128)S(1)} %get-tuple-element.67.near_ref, s32[256,128]{1,0:T(8,128)S(1)} %copy-done.9, f32[776,128]{1,0:T(8,128)S(1)} %get-tuple-element.68.force_ref, f32[48,128]{1,0:T(8,128)S(1)} %shard_map.142.inner_ref, ...), custom_call_target="tpu_custom_call" | custom-call | tf_op jit(solution)/shard_map/pallas_call | solution.py:984
  54.0 4.9 %all-to-all-done.4.back_ref = f32[32,1,1280]{2,1,0:T(1,128)S(1)} async-done(((f32[32,1,1280]{2,1,0:T(1,128)}), f32[32,1,1280]{2,1,0:T(1,128)S(1)}, u32[]{:S(2)}, u32[]{:S(2)}) %all-to-all-start.4) | async-done | bytes 163872 | tf_op jit(solution)/shard_map/all_to_all | solution.py:1037
  59.0 2.7 %shard_map.144 = (f32[48,128]{1,0:T(8,128)S(1)}, f32[32,1,768]{2,1,0:T(1,128)S(1)}) custom-call(s32[1]{0:T(128)} %bitcast.own_ref, s32[8,160]{1,0:T(8,128)S(1)} %get-tuple-element.59.entry_ref, f32[32,1,1280]{2,1,0:T(1,128)S(1)} %all-to-all-done.4.back_ref, s32[256,128]{1,0:T(8,128)S(1)} %copy-done.9, f32[3,256,128]{2,1,0:T(8,128)S(1)} %get-tuple-element.70.normal_ref, ...), custom_call_target="tpu_custom_call" | custom-call | tf_op jit(solution)/shard_map/pallas_call | solution.py:984
  61.7 9.7 %all_to_all.29.got_ref = f32[32,1,768]{2,1,0:T(1,128)S(1)} all-to-all(f32[32,1,768]{2,1,0:T(1,128)S(1)} %get-tuple-element.73), channel_id=1, replica_groups=mesh['gx'=4,'gy'=8] {'gx','gy'}, dimensions={0} | all-to-all | bytes 196608 | tf_op jit(solution)/shard_map/all_to_all | solution.py:1037
  71.4 0.9 %shard_map.145 = f32[3,1408]{1,0:T(4,128)} custom-call(s32[1]{0:T(128)} %bitcast.own_ref, f32[48,128]{1,0:T(8,128)S(1)} %get-tuple-element.72.total_ref, f32[32,1,768]{2,1,0:T(1,128)S(1)} %all_to_all.29.got_ref, f32[8,128]{1,0:T(8,128)S(1)} %collective-permute-done.low_ref, f32[8,128]{1,0:T(8,128)S(1)} %collective-permute-done.1.high_ref, ...), custom_call_target="tpu_custom_call" | custom-call | tf_op jit(solution)/shard_map/pallas_call | solution.py:984
  (29 shorter events, 0.1 us)
Async XLA Ops:
  0.0 18.7 %copy-start.8 = (f32[256,2,128]{2,1,0:T(2,128)S(1)}, f32[256,2,128]{2,1,0:T(2,128)}, u32[]{:S(2)}) copy-start(f32[256,2,128]{2,1,0:T(2,128)} %angles_ref.5) | copy-start | bytes 786436
  3.1 22.9 %copy-start.13 = (s32[4,153]{1,0:T(4,128)S(1)}, s32[4,153]{1,0:T(4,128)}, u32[]{:S(2)}) copy-start(s32[4,153]{1,0:T(4,128)} %param.17) | copy-start | bytes 7348
  3.1 26.7 %copy-start.2 = (f32[3,1408]{1,0:T(4,128)S(1)}, f32[3,1408]{1,0:T(4,128)}, u32[]{:S(2)}) copy-start(f32[3,1408]{1,0:T(4,128)} %disp_ref.3) | copy-start | bytes 50692
  3.1 26.7 %copy-start.3 = (s32[8,1024]{1,0:T(8,128)S(1)}, s32[8,1024]{1,0:T(8,128)}, u32[]{:S(2)}) copy-start(s32[8,1024]{1,0:T(8,128)} %conn_ref.1) | copy-start | bytes 98308
  3.1 26.7 %copy-start.5 = (f32[3,1408]{1,0:T(4,128)S(1)}, f32[3,1408]{1,0:T(4,128)}, u32[]{:S(2)}) copy-start(f32[3,1408]{1,0:T(4,128)} %coords_ref.1) | copy-start | bytes 50692
  3.1 26.7 %copy-start.7 = (f32[1024]{0:T(1024)S(1)}, f32[1024]{0:T(1024)}, u32[]{:S(2)}) copy-start(f32[1024]{0:T(1024)} %param.22) | copy-start | bytes 12292
  3.1 28.6 %copy-start.10 = (s32[2,64,128]{2,1,0:T(8,128)S(1)}, s32[2,64,128]{2,1,0:T(8,128)}, u32[]{:S(2)}) copy-start(s32[2,64,128]{2,1,0:T(8,128)} %masks_ref.3) | copy-start | bytes 196612
  3.1 15.5 %all-to-all-start.2 = ((s32[32,8,128]{2,1,0:T(8,128)}), s32[32,8,128]{2,1,0:T(8,128)S(1)}, u32[]{:S(2)}, u32[]{:S(2)}) async-start(s32[32,8,128]{2,1,0:T(8,128)} %shard_map.136), calls=%async_computation.2 | async-start | bytes 262144 | tf_op jit(solution)/shard_map/all_to_all | solution.py:1037
  10.4 1.0 %copy-start = (f32[256,3,128]{2,0,1:T(8,128)S(1)}, f32[256,3,128]{2,0,1:T(8,128)}, u32[]{:S(2)}) copy-start(f32[256,3,128]{2,0,1:T(8,128)} %param.24) | copy-start | bytes 1179652
  11.4 0.7 %copy-start.1 = (f32[3,1408]{1,0:T(4,128)S(1)}, f32[3,1408]{1,0:T(4,128)}, u32[]{:S(2)}) copy-start(f32[3,1408]{1,0:T(4,128)} %disp_ref.3) | copy-start | bytes 50692
  22.8 23.2 %copy-start.9 = (s32[256,128]{1,0:T(8,128)S(1)}, s32[256,128]{1,0:T(8,128)}, u32[]{:S(2)}) copy-start(s32[256,128]{1,0:T(8,128)} %nodes_ref.5) | copy-start | bytes 393220
  22.8 23.2 %copy-start.11 = (s32[8192]{0:T(1024)S(1)}, s32[8192]{0:T(1024)}, u32[]{:S(2)}) copy-start(s32[8192]{0:T(1024)} %param.26) | copy-start | bytes 98308
  22.8 23.2 %copy-start.12 = (s32[2,64]{1,0:T(2,128)S(1)}, s32[2,64]{1,0:T(2,128)}, u32[]{:S(2)}) copy-start(s32[2,64]{1,0:T(2,128)} %pairs_ref.1) | copy-start | bytes 1540
  22.8 18.7 %all-to-all-start.3 = ((f32[32,32,128]{2,1,0:T(8,128)}), f32[32,32,128]{2,1,0:T(8,128)S(1)}, u32[]{:S(2)}, u32[]{:S(2)}) async-start(f32[32,32,128]{2,1,0:T(8,128)} %get-tuple-element.61), calls=%async_computation.3 | async-start | bytes 1048576 | tf_op jit(solution)/shard_map/all_to_all | solution.py:1037
  26.3 9.0 %collective-permute-start = (f32[8,128]{1,0:T(8,128)S(1)}, f32[8,128]{1,0:T(8,128)S(1)}, u32[]{:S(2)}, u32[]{:S(2)}) collective-permute-start(f32[8,128]{1,0:T(8,128)S(1)} %get-tuple-element.62), channel_id=1, source_target_pairs={{0,1},{1,2},{2,3},{3,4},{4,5},{5,6},{6,7},{8,9},{9,10},{10,11},{11... | collective-permute-start | bytes 12296 | tf_op jit(solution)/shard_map/ppermute | solution.py:998
  28.4 6.8 %collective-permute-start.1 = (f32[8,128]{1,0:T(8,128)S(1)}, f32[8,128]{1,0:T(8,128)S(1)}, u32[]{:S(2)}, u32[]{:S(2)}) collective-permute-start(f32[8,128]{1,0:T(8,128)S(1)} %get-tuple-element.63), channel_id=1, source_target_pairs={{1,0},{2,1},{3,2},{4,3},{5,4},{6,5},{7,6},{9,8},{10,9},{11,10},{12... | collective-permute-start | bytes 12296 | tf_op jit(solution)/shard_map/ppermute | solution.py:998
  46.0 25.4 %copy-start.4 = (f32[3,1408]{1,0:T(4,128)S(1)}, f32[3,1408]{1,0:T(4,128)}, u32[]{:S(2)}) copy-start(f32[3,1408]{1,0:T(4,128)} %velocity_ref.1) | copy-start | bytes 50692
  46.1 25.4 %copy-start.6 = (f32[1408]{0:T(1024)S(1)}, f32[1408]{0:T(1024)}, u32[]{:S(2)}) copy-start(f32[1408]{0:T(1024)} %param.21) | copy-start | bytes 16900
  46.1 12.9 %all-to-all-start.4 = ((f32[32,1,1280]{2,1,0:T(1,128)}), f32[32,1,1280]{2,1,0:T(1,128)S(1)}, u32[]{:S(2)}, u32[]{:S(2)}) async-start(f32[32,1,1280]{2,1,0:T(1,128)} %get-tuple-element.66), calls=%async_computation.4 | async-start | bytes 327680 | tf_op jit(solution)/shard_map/all_to_all | solution.py:1037
